TPU v7x, 32 devices: a whole 2x2x4 slice. The times are simulated.
32 devices in a mesh: lat: 4 (over x, core), lon: 8 (over z, y).
Axes of the slice: x: 2, y: 2, z: 4, core: 2. Of those that a mesh axis runs over, the one named last changes fastest.
Arguments:
- field: bfloat16 [512, 256, 128], P('lat', 'lon'), may hold values from -6 to 6
- land: int32 [512, 256], P('lat', 'lon'), may hold values 0 or 1
- mirror: int32 [256], replicated, may hold values from 0 to 255, as said below
- depth_weight: bfloat16 [49, 128], replicated, may hold values from -2 to 2
- norm_gain: bfloat16 [128], replicated, may hold values from 0.5 to 2
- up_weight: bfloat16 [128, 512], replicated, may hold values from -0.5 to 0.5
- up_bias: bfloat16 [512], replicated, may hold values from -3 to 3
- down_proj: bfloat16 [512, 128], replicated, may hold values from -0.25 to 0.25
- layer_scale: bfloat16 [128], replicated, may hold values from 0.25 to 1
- section_gain: bfloat16 [3, 128], replicated, may hold values from 0.5 to 2
- section_weight: bfloat16 [3, 512, 128], replicated, may hold values from -0.25 to 0.25
- section_bias: bfloat16 [3, 128], replicated, may hold values from -3 to 3
- cotangent: bfloat16 [64, 32, 128], P('lat', 'lon'), may hold values from -6 to 6
Outputs:
- bottleneck: bfloat16 [64, 32, 128], P('lat', 'lon')
- grad_field: bfloat16 [512, 256, 128], P('lat', 'lon')
- grad_depth: float32 [49, 128], replicated
- grad_up: float32 [128, 512], replicated
- grad_down: float32 [512, 128], replicated
- grad_section: float32 [3, 512, 128], replicated
Inputs may be any that keep to these rules, and one draw needn't show every extreme that they name: mirror[i] = (s - i) mod 256 for one s, the same for all i; mirror is its own inverse.
All inputs are finite; a program needn't handle non-finite values. No bound on the sum of `land` on one device may be relied on, other than what follows from the above.
Results may differ from a plain program's by a relative error of at most 0.017.
Values may be sent and summed in bfloat16 or wider, within the bound.
No kernel may reach another device: no remote copies, remote signals or barrier semaphores. Data moves between devices by JAX's collectives and lax.ppermute only.
A program may use at most 128 MiB of HBM per device.

v0:
```python
import functools
import math

import jax
import jax.numpy as jnp
from jax import lax
from jax.experimental import pallas as pl
from jax.experimental.pallas import tpu as pltpu
from jax.sharding import PartitionSpec as P

SECTIONS = 3
EPS = 1e-6
f32, bf16 = jnp.float32, jnp.bfloat16
S = 16
LOG2E = 1.4426950408889634
VMEM = pl.BlockSpec(memory_space=pltpu.VMEM)
SMEM = pl.BlockSpec(memory_space=pltpu.SMEM)
PARAMS = pltpu.CompilerParams(vmem_limit_bytes=60 * 2**20)


def dot(a, b):
    return jnp.dot(a, b, preferred_element_type=f32)


def dot_t(a, b):
    return lax.dot_general(a, b, (((0,), (0,)), ((), ())), preferred_element_type=f32)


def dot_r(a, b):
    return lax.dot_general(a, b, (((1,), (1,)), ((), ())), preferred_element_type=f32)


def ones_mean(n):
    return jnp.full((n, 128), 1.0 / 128, bf16)


def pair_mean():
    r = lax.broadcasted_iota(jnp.int32, (256, 256), 0) // 128
    c = lax.broadcasted_iota(jnp.int32, (256, 256), 1) // 128
    return jnp.where(r == c, 1.0 / 128, 0.0).astype(bf16)


def split2(x):
    hi = x.astype(bf16)
    lo = (x - hi.astype(f32)).astype(bf16)
    return jnp.concatenate([hi, lo], axis=1)


def norm_bwd(u, hat, rstd, pm):
    m = dot(jnp.concatenate([u.astype(bf16), (u * hat).astype(bf16)], axis=1), pm)
    return rstd * (u - m[:, :128] - hat * m[:, 128:])


def gelu(h):
    cdf = 0.5 + 0.5 * lax.erf(h * 0.7071067811865476)
    e = jnp.exp2(h * h * (-0.5 * LOG2E))
    return h * cdf, cdf + h * (e * 0.3989422804014327)


def weights_table(dw, w49, flip):
    for t in range(49):
        w49[48 - t if flip else t] = jnp.broadcast_to(dw[t : t + 1, :].astype(f32), (S, 128))


def conv49(el, w49, emit, I, CW):
    CE = CW + 6
    CG = 8

    def step(n, _):
        i = n // (CW // CG)
        c0 = (n % (CW // CG)) * CG
        acc = [None] * CG
        for a in range(7):
            row = [el[(i + a) * CE + c0 + m].astype(f32) for m in range(CG + 6)]
            for b in range(7):
                w = w49[a * 7 + b]
                for k in range(CG):
                    pr = row[k + b] * w
                    acc[k] = pr if acc[k] is None else acc[k] + pr
        for k in range(CG):
            emit(i, c0 + k, acc[k])
        return 0

    lax.fori_loop(0, I * (CW // CG), step, 0)


def block_body(
    R, CW,
    field, south, north, left, right, landb, dw, gain, up, down, scale, sgain, sw, sbias, cot,
    bott, gout, dirout, first, last, lcol, rcol, sums,
    x2d, el, w49, dep, hat, rst, nrm, act, slp, shat, srst, p1, back, tacc, downs, ups,
):
    I = R // S
    CE = CW + 6
    XW = 40
    n0 = R * CW

    def asm(r, _):
        x2d[pl.ds((r + 3) * XW + 3, CW), :] = field[r].astype(f32)
        return 0

    lax.fori_loop(0, R, asm, 0, unroll=4)
    for k in range(3):
        x2d[pl.ds(k * XW + 3, CW), :] = south[k].astype(f32)
        x2d[pl.ds((R + 3 + k) * XW + 3, CW), :] = north[k].astype(f32)
        x2d[pl.ds(k, R + 6, stride=XW), :] = left[k].astype(f32)
        x2d[pl.ds(CW + 3 + k, R + 6, stride=XW), :] = right[k].astype(f32)

    def tr(i, _):
        for c in range(CE):
            el[i * CE + c] = x2d[pl.ds(i * XW + c, S, stride=I * XW), :].astype(bf16)
        return 0

    lax.fori_loop(0, I + 6, tr, 0)
    weights_table(dw, w49, False)

    def emit(i, c, v):
        dep[pl.ds((i * CW + c) * S, S), :] = v

    conv49(el, w49, emit, I, CW)

    jj, j1, pm = ones_mean(256), ones_mean(128), pair_mean()
    g_n = gain[...].astype(f32)
    sc = scale[...].astype(f32)
    sg0 = sgain[0:1, :].astype(f32)
    T1 = 1024

    def nfwd(n, _):
        base = pl.multiple_of(n * T1, T1)
        x = dep[pl.ds(base, T1), :]
        cen = x - dot(split2(x), jj)
        rs = lax.rsqrt(dot((cen * cen).astype(bf16), j1) + EPS)
        ht = cen * rs
        hat[pl.ds(base, T1), :] = ht
        rst[pl.ds(base, T1), :] = rs
        nrm[pl.ds(base, T1), :] = (ht * g_n).astype(bf16)
        return 0

    lax.fori_loop(0, n0 // T1, nfwd, 0)

    T2 = 512
    onec = (lax.broadcasted_iota(jnp.int32, (T2, 128), 1) == 0).astype(f32).astype(bf16)

    def upf(n, _):
        base = pl.multiple_of(n * T2, T2)
        lhs = jnp.concatenate([nrm[pl.ds(base, T2), :], onec], axis=1)
        for q in range(2):
            hid = dot(lhs, up[:, q * 256 : (q + 1) * 256])
            ac, sl = gelu(hid)
            act[pl.ds(base, T2), q * 256 : (q + 1) * 256] = ac.astype(bf16)
            slp[pl.ds(base, T2), q * 256 : (q + 1) * 256] = sl.astype(bf16)
        return 0

    lax.fori_loop(0, n0 // T2, upf, 0)

    TP = 2 * CW * S

    def sect_norm(lv, s):
        cen = lv.astype(f32) - dot(lv, j1)
        rs1 = lax.rsqrt(dot((cen * cen).astype(bf16), j1) + EPS)
        h1 = cen * rs1
        return h1, rs1, (h1 * sgain[s : s + 1, :].astype(f32)).astype(bf16)

    def dnf(i2, _):
        base = pl.multiple_of(i2 * TP, TP)
        mixed = dot(act[pl.ds(base, TP), :], down[...])
        xs = jnp.concatenate(
            [el[pl.ds((i2 * 2 + a + 3) * CE + 3, CW)].reshape(CW * S, 128) for a in range(2)], axis=0
        ).astype(f32)
        lv = (landb[pl.ds(base, TP), :].astype(f32) * (xs + sc * mixed)).astype(bf16)
        h1, rs1, sn = sect_norm(lv, 0)
        shat[pl.ds(base, TP), :] = h1
        srst[pl.ds(base, TP), :] = rs1
        sn = sn.reshape(2, CW // 2, 2, S, 128)
        pb = pl.multiple_of(i2 * (TP // 4), TP // 4)
        for a in range(2):
            for b in range(2):
                k = 2 * a + b
                p1[pl.ds(pb, TP // 4), k * 128 : (k + 1) * 128] = sn[a, :, b].reshape(TP // 4, 128)
        return 0

    lax.fori_loop(0, I // 2, dnf, 0)

    def to_patches(sn, ii, cc):
        v = sn.reshape(ii // 2, 2, cc // 2, 2, S, 128)
        return jnp.concatenate(
            [v[:, a, :, b].reshape(ii * cc * S // 4, 128) for a in range(2) for b in range(2)], axis=1
        )

    def from_patches(sp, ii, cc):
        ps = [sp[:, k * 128 : (k + 1) * 128].reshape(ii // 2, cc // 2, S, 128) for k in range(4)]
        rows = [jnp.stack([ps[2 * a], ps[2 * a + 1]], axis=2).reshape(ii // 2, cc, S, 128) for a in range(2)]
        return jnp.stack(rows, axis=1).reshape(ii * cc * S, 128)

    def put(at, value, blocks):
        for q in range(blocks):
            sums[at + q * 128 : at + (q + 1) * 128, :] = value[:, q * 128 : (q + 1) * 128].astype(bf16)

    l1 = (dot(p1[...], sw[0]) + sbias[0:1, :].astype(f32)).astype(bf16)
    h1, r1, sn1 = sect_norm(l1, 1)
    P2 = to_patches(sn1, I // 2, CW // 2)
    l2 = (dot(P2, sw[1]) + sbias[1:2, :].astype(f32)).astype(bf16)
    h2, r2, sn2 = sect_norm(l2, 2)
    P3 = to_patches(sn2, I // 4, CW // 4)
    l3 = (dot(P3, sw[2]) + sbias[2:3, :].astype(f32)).astype(bf16)
    bott[...] = l3
    b3 = cot[...]
    put(1024, dot_t(b3, P3), 4)
    u2 = from_patches(dot_r(b3, sw[2]), I // 4, CW // 4) * sgain[2:3, :].astype(f32)
    b2 = norm_bwd(u2, h2, r2, pm).astype(bf16)
    put(512, dot_t(b2, P2), 4)
    u1 = from_patches(dot_r(b2, sw[1]), I // 2, CW // 2) * sgain[1:2, :].astype(f32)
    b1 = norm_bwd(u1, h1, r1, pm).astype(bf16)
    put(0, dot_t(b1, p1[...]), 4)
    back[...] = b1

    downs[...] = jnp.zeros_like(downs)
    ups[...] = jnp.zeros_like(ups)
    T = 256
    TC = T // S

    def bwd(n, _):
        i2 = n // (CW // TC)
        h = n % (CW // TC)
        pb = pl.multiple_of((i2 * (CW // 2) + h * (TC // 2)) * S, T // 2)
        bk = back[pl.ds(pb, T // 2), :]
        for a in range(2):
            base = pl.multiple_of(((i2 * 2 + a) * CW + h * TC) * S, T)
            sp = dot_r(bk, sw[0, a * 256 : (a + 1) * 256, :])
            sp = jnp.stack(
                [sp[:, :128].reshape(TC // 2, S, 128), sp[:, 128:].reshape(TC // 2, S, 128)], axis=1
            ).reshape(T, 128)
            b0 = norm_bwd(sp * sg0, shat[pl.ds(base, T), :], srst[pl.ds(base, T), :], pm).astype(bf16).astype(f32)
            dr = landb[pl.ds(base, T), :].astype(f32) * b0
            dirout[pl.ds(base, T), :] = dr.astype(bf16)
            mg = (dr * sc).astype(bf16)
            downs[...] += dot_t(mg, act[pl.ds(base, T), :])
            hgs = []
            for q in range(2):
                ag = dot_r(mg, down[q * 256 : (q + 1) * 256, :])
                hgs.append((ag * slp[pl.ds(base, T), q * 256 : (q + 1) * 256].astype(f32)).astype(bf16))
            hg = jnp.concatenate(hgs, axis=1)
            ups[...] += dot_t(nrm[pl.ds(base, T), :], hg)
            ng = dot_r(hg, up[0:128, :])
            dg = norm_bwd(ng * g_n, hat[pl.ds(base, T), :], rst[pl.ds(base, T), :], pm)
            gout[pl.ds(base, T), :] = dg.astype(bf16)
        return 0

    lax.fori_loop(0, (I // 2) * (CW // TC), bwd, 0)
    put(1536, downs[...], 4)
    put(2048, ups[...], 4)

    tacc[...] = jnp.zeros_like(tacc)

    def tap(n, _):
        i = n // (CW // 8)
        c0 = (n % (CW // 8)) * 8
        g = [gout[pl.ds((i * CW + c0 + k) * S, S), :].astype(f32) for k in range(8)]
        for a in range(7):
            row = [el[(i + a) * CE + c0 + m].astype(f32) for m in range(14)]
            for b in range(7):
                s = None
                for k in range(8):
                    pr = row[k + b] * g[k]
                    s = pr if s is None else s + pr
                tacc[a * 7 + b] += s[:8] + s[8:]
        return 0

    lax.fori_loop(0, I * (CW // 8), tap, 0)
    ts = [jnp.sum(tacc[t], axis=0, keepdims=True) for t in range(49)]
    ts = jnp.concatenate(ts + [jnp.zeros((15, 128), f32)], axis=0)
    sums[2560:2624, :] = ts.astype(bf16)
    sums[2624:2688, :] = jnp.zeros((64, 128), bf16)

    x2d[0:n0, :] = gout[...].astype(f32)
    for k in range(3):
        first[k] = x2d[pl.ds(k * CW * S, CW, stride=S), :].astype(bf16)
        last[k] = x2d[pl.ds((I - 3 + k) * CW * S + S - 1, CW, stride=S), :].astype(bf16)
    for i in range(I):
        lcol[i * 3 * S : (i + 1) * 3 * S, :] = gout[i * CW * S : (i * CW + 3) * S, :]
        rcol[i * 3 * S : (i + 1) * 3 * S, :] = gout[((i + 1) * CW - 3) * S : (i + 1) * CW * S, :]


def block_pass(field, south, north, left, right, landb, dw, gain, upx, down, scale, sgain, sw, sbias, cot):
    R, CW, C = field.shape
    n = R * CW
    I = R // S
    sd = jax.ShapeDtypeStruct
    out_shape = (
        sd((n // 64, C), bf16),
        sd((n, C), bf16),
        sd((n, C), bf16),
        sd((3, CW, C), bf16),
        sd((3, CW, C), bf16),
        sd((I * 3 * S, C), bf16),
        sd((I * 3 * S, C), bf16),
        sd((2688, C), bf16),
    )
    V = pltpu.VMEM
    scratch = [
        V(((R + 6) * 40, C), f32),
        V(((I + 6) * (CW + 6), S, C), bf16),
        V((49, S, C), f32),
        V((n, C), f32),
        V((n, C), f32),
        V((n, C), f32),
        V((n, C), bf16),
        V((n, 512), bf16),
        V((n, 512), bf16),
        V((n, C), f32),
        V((n, C), f32),
        V((n // 4, 512), bf16),
        V((n // 4, C), bf16),
        V((49, 8, C), f32),
        V((C, 512), f32),
        V((C, 512), f32),
    ]
    return pl.pallas_call(
        functools.partial(block_body, R, CW),
        out_shape=out_shape,
        in_specs=[VMEM] * 15,
        out_specs=[VMEM] * 8,
        scratch_shapes=scratch,
        compiler_params=PARAMS,
        name="block_pass",
    )(field, south, north, left, right, landb, dw, gain, upx, down, scale, sgain, sw, sbias, cot)


def conv_back_body(R, CW, g, dirin, south, north, gl, gr, dw, flag, out, gx, gext, w49, acc):
    I = R // S
    CE = CW + 6
    n0 = R * CW
    isn = flag[...].astype(f32)
    nots = 1.0 - isn
    core = I * 3 * S

    for i in range(I):
        at = (i + 3) * CE * S
        gx[pl.ds(at, 3 * S), :] = gl[i * 3 * S : (i + 1) * 3 * S, :].astype(f32)
        gx[pl.ds(at + 3 * S, CW * S), :] = g[i * CW * S : (i + 1) * CW * S, :].astype(f32)
        gx[pl.ds(at + (3 + CW) * S, 3 * S), :] = gr[i * 3 * S : (i + 1) * 3 * S, :].astype(f32)
    row = lax.broadcasted_iota(jnp.int32, (S, 128), 0)

    for k in range(3):
        sk = jnp.concatenate([gl[core + k * 3 : core + k * 3 + 3, :].astype(f32), south[k].astype(f32), gr[core + k * 3 : core + k * 3 + 3, :].astype(f32)], axis=0)
        nk = jnp.concatenate([gl[core + 9 + k * 3 : core + 12 + k * 3, :].astype(f32), north[k].astype(f32), gr[core + 9 + k * 3 : core + 12 + k * 3, :].astype(f32)], axis=0)
        acc[k * 40 : k * 40 + CE, :] = sk
        acc[(3 + k) * 40 : (3 + k) * 40 + CE, :] = nk
    for k in range(3):
        def lo(c, _, k=k):
            v = gx[pl.ds(((I + k) * CE + c) * S, S), :]
            v = pltpu.roll(v, 1, 0)
            h = acc[pl.ds(k * 40 + c, 1), :]
            gext[k * CE + c] = jnp.where(row == 0, h, v).astype(bf16)
            v = gx[pl.ds(((3 + k) * CE + c) * S, S), :]
            v = pltpu.roll(v, S - 1, 0)
            h = acc[pl.ds((3 + k) * 40 + c, 1), :] * nots
            gext[(I + 3 + k) * CE + c] = jnp.where(row == S - 1, h, v).astype(bf16)
            return 0
        lax.fori_loop(0, CE, lo, 0, unroll=2)

    def cpy(i, _):
        gext[pl.ds((i + 3) * CE, CE)] = gx[pl.ds((i + 3) * CE * S, CE * S), :].astype(bf16).reshape(CE, S, 128)
        return 0

    lax.fori_loop(0, I, cpy, 0)
    weights_table(dw, w49, True)
    fold = []
    for k in range(1, 4):
        s = None
        for rho in range(k - 1, 3):
            a = 5 + k - rho
            for b in range(7):
                pr = acc[pl.ds((3 + rho) * 40 + b, CW), :] * w49[48 - (7 * a + b), 0:1, :]
                s = pr if s is None else s + pr
        fold.append(s * isn)

    def emit(i, c, v):
        at = pl.multiple_of((i * CW + c) * S, S)
        gx[pl.ds(at, S), :] = v + dirin[pl.ds(at, S), :].astype(f32)

    conv49(gext, w49, emit, I, CW)

    def unt(r, _):
        s = r // I
        i = r % I
        out[r] = gx[pl.ds(i * CW * S + s, CW, stride=S), :].astype(bf16)
        return 0

    lax.fori_loop(0, R - 3, unt, 0, unroll=4)
    for k in range(1, 4):
        r = R - k
        v = gx[pl.ds((r % I) * CW * S + r // I, CW, stride=S), :]
        out[r] = (v + fold[k - 1]).astype(bf16)


def conv_back(g, dirin, south, north, gl, gr, dw, flag, R, CW):
    C = g.shape[1]
    I = R // S
    return pl.pallas_call(
        functools.partial(conv_back_body, R, CW),
        out_shape=jax.ShapeDtypeStruct((R, CW, C), bf16),
        in_specs=[VMEM] * 8,
        out_specs=VMEM,
        scratch_shapes=[
            pltpu.VMEM(((I + 6) * (CW + 6) * S, C), f32),
            pltpu.VMEM(((I + 6) * (CW + 6), S, C), bf16),
            pltpu.VMEM((49, S, C), f32),
            pltpu.VMEM((240, C), f32),
        ],
        compiler_params=PARAMS,
        name="conv_back",
    )(g, dirin, south, north, gl, gr, dw, flag)


def finish_body(factor, chunk, idx, mine, other, o_depth, o_up, o_down, o_sec, full):
    core = idx[0]
    place = idx[1]
    half = 4 * chunk
    for j in range(4):
        src = lax.bitwise_xor(place, j)
        at = pl.multiple_of(core * half + j * chunk, 16)
        full[pl.ds(at, chunk), :] = mine[src]
        at = pl.multiple_of((1 - core) * half + j * chunk, 16)
        full[pl.ds(at, chunk), :] = other[src]

    def block(n):
        return full[n * 128 : (n + 1) * 128, :].astype(f32) * factor

    for s in range(3):
        for q in range(4):
            o_sec[s, q * 128 : (q + 1) * 128, :] = block(s * 4 + q).T
    for q in range(4):
        o_down[q * 128 : (q + 1) * 128, :] = block(12 + q).T
        o_up[:, q * 128 : (q + 1) * 128] = block(16 + q)
    o_depth[...] = block(20)[:49, :]


def finish(idx, mine, other, factor):
    chunk = mine.shape[1]
    sd = jax.ShapeDtypeStruct
    return pl.pallas_call(
        functools.partial(finish_body, factor, chunk),
        out_shape=(sd((49, 128), f32), sd((128, 512), f32), sd((512, 128), f32), sd((3, 512, 128), f32)),
        in_specs=[SMEM, VMEM, VMEM],
        out_specs=[VMEM] * 4,
        scratch_shapes=[pltpu.VMEM((8 * chunk, 128), bf16)],
        compiler_params=PARAMS,
        name="finish_sums",
    )(idx, mine, other)


def add_bf(*vals):
    vals = [v.astype(f32) for v in vals]
    while len(vals) > 1:
        vals = [vals[i] + vals[i + 1] for i in range(0, len(vals), 2)]
    return vals[0].astype(bf16)


def flip_pairs(axis, bits):
    return [(i, i ^ bits) for i in range(lax.axis_size(axis))]


def both_pairs(lat_bits, lon_bits):
    nl = lax.axis_size("lon")
    return [
        (a * nl + b, (a ^ lat_bits) * nl + (b ^ lon_bits))
        for a in range(lax.axis_size("lat"))
        for b in range(nl)
    ]


def all_sums(sums):
    lat = lax.axis_index("lat")
    lon = lax.axis_index("lon")
    core = lat % 2
    place = (lat // 2) * 2 + lon % 2
    half = sums.shape[0] // 2
    chunk = half // 4
    keep = lax.dynamic_slice_in_dim(sums, core * half, half, 0)
    away = lax.dynamic_slice_in_dim(sums, (1 - core) * half, half, 0)
    got = lax.ppermute(away, "lat", flip_pairs("lat", 1))
    held = add_bf(keep, got).reshape(4, chunk, 128)
    own = lax.dynamic_index_in_dim(held, place, 0, keepdims=False)
    came = []
    for k in (1, 2, 3):
        part = lax.dynamic_index_in_dim(held, lax.bitwise_xor(place, k), 0, keepdims=False)
        came.append(lax.ppermute(part, ("lat", "lon"), both_pairs((k // 2) * 2, k % 2)))
    total = add_bf(own, *came)
    left = lax.axis_size("lon") // 2
    bit = 2
    while left > 1:
        if left % 4 == 0:
            total = add_bf(total, *[lax.ppermute(total, "lon", flip_pairs("lon", bit * k)) for k in (1, 2, 3)])
            left //= 4
            bit *= 4
        else:
            total = add_bf(total, lax.ppermute(total, "lon", flip_pairs("lon", bit)))
            left //= 2
            bit *= 2
    back = [lax.ppermute(total, ("lat", "lon"), both_pairs((k // 2) * 2, k % 2)) for k in (1, 2, 3)]
    mine = jnp.stack([total, *back])
    other = lax.ppermute(mine, "lat", flip_pairs("lat", 1))
    return jnp.stack([core, place]).astype(jnp.int32), mine, other


def halo_rows(first, last, quot, rem, north):
    nl = lax.axis_size("lon")
    nt = lax.axis_size("lat")
    cols = first.shape[1]
    top = (nt - 1) * nl

    def branch(q):
        def run(first, last):
            up = [(a * nl + b, (a + 1) * nl + b) for a in range(nt - 1) for b in range(nl)]
            down = [(j, i) for i, j in up]
            fa = [(top + e, top + (q - e) % nl) for e in range(nl)]
            fb = [(top + e, top + (q - 1 - e) % nl) for e in range(nl)]
            axes = ("lat", "lon")
            return (
                lax.ppermute(last, axes, up),
                lax.ppermute(first, axes, down),
                lax.ppermute(last, axes, fa),
                lax.ppermute(last, axes, fb),
            )

        return run

    south, above, blk_a, blk_b = lax.switch(quot, [branch(q) for q in range(nl)], first, last)
    both = jnp.concatenate([blk_b, blk_a], axis=1)
    window = lax.dynamic_slice_in_dim(both, rem + 1, cols, 1)
    return south, above, window[:, ::-1]


def shift_pairs(axis, by):
    n = lax.axis_size(axis)
    return [(i, (i + by) % n) for i in range(n)]


def on_device(
    field, land, mirror, depth_weight, norm_gain, up_weight, up_bias, down_proj, layer_scale,
    section_gain, section_weight, section_bias, cotangent,
):
    R, CW, C = field.shape
    I = R // S
    n = R * CW
    total = R * CW * lax.axis_size("lat") * lax.axis_size("lon")
    factor = 1.0 / math.sqrt(total / 64.0)
    north = lax.axis_index("lat") == lax.axis_size("lat") - 1
    quot = mirror[0] // CW
    rem = mirror[0] % CW

    south_f, above_f, fold_f = halo_rows(field[:3], field[R - 3 :], quot, rem, north)
    north_f = jnp.where(north, fold_f[::-1], above_f)

    def edge(lo):
        return jnp.stack(
            [jnp.concatenate([south_f[:, c], field[:, c], north_f[:, c]], axis=0) for c in range(lo, lo + 3)]
        )

    right_f = lax.ppermute(edge(0), "lon", shift_pairs("lon", -1))
    left_f = lax.ppermute(edge(CW - 3), "lon", shift_pairs("lon", 1))

    landb = jnp.broadcast_to(
        land.astype(bf16).reshape(S, I, CW).transpose(1, 2, 0).reshape(n, 1), (n, C)
    )
    upx = jnp.concatenate([up_weight, up_bias[None, :], jnp.zeros((127, up_bias.shape[0]), bf16)], axis=0)
    cot = cotangent.transpose(1, 0, 2).reshape(n // 64, C)
    bott, g, direct, first, last, lcol, rcol, sums = block_pass(
        field, south_f, north_f, left_f, right_f, landb, depth_weight, norm_gain[None, :], upx, down_proj,
        layer_scale[None, :], section_gain, section_weight, section_bias, cot,
    )
    level = bott.reshape(CW // 8, S, C).transpose(1, 0, 2)

    south_g, above_g, fold_g = halo_rows(first, last, quot, rem, north)
    north_g = jnp.where(north, fold_g, above_g)

    def pack(cols, lo):
        return jnp.concatenate(
            [cols, south_g[:, lo : lo + 3].reshape(9, C), north_g[:, lo : lo + 3].reshape(9, C)], axis=0
        )

    gr = lax.ppermute(pack(lcol, 0), "lon", shift_pairs("lon", -1))
    gl = lax.ppermute(pack(rcol, CW - 3), "lon", shift_pairs("lon", 1))
    flag = jnp.broadcast_to(north.astype(bf16), (1, C))
    idx, mine, other = all_sums(sums)
    grad_field = conv_back(g, direct, south_g, north_g, gl, gr, depth_weight, flag, R, CW)
    g_depth, g_up, g_down, g_sec = finish(idx, mine, other, factor)
    return level, grad_field, g_depth, g_up, g_down, g_sec


def solution(mesh):
    cells = P("lat", "lon", None)
    in_specs = (cells, P("lat", "lon")) + (P(),) * 10 + (cells,)
    out_specs = (cells, cells, P(), P(), P(), P())
    return jax.shard_map(on_device, mesh=mesh, in_specs=in_specs, out_specs=out_specs, check_vma=False)
```

profile of v0, /device:TPU:0, one launch (start us, length us, event | category | flops | bytes accessed | tf_op | source)
XLA Modules:
  0.0 145.4 jit_solution(3463625231848074936)
XLA Ops:
  0.6 1.2 slice.120
  4.4 0.8 fusion.13
  5.2 2.0 %fusion.12 = (bf16[128,1,128]{2,1,0:T(2,128)(2,1)S(1)}, bf16[128,1,128]{2,1,0:T(2,128)(2,1)S(1)}, bf16[128,1,128]{2,1,0:T(2,128)(2,1)S(1)}, bf16[128,1,128]{2,1,...) fusion(bf16[128,32,128]{2,1,0:T(8,128)(2,1)} %field.1), kind=kLoop, calls=%fused_computation.58 | loop fusion | bytes 393216 | tf_op jit(solution)/shard_map/slice | solution.py:558
  7.3 7.7 %conditional.2 = (bf16[3,32,128]{2,1,0:T(8,128)(2,1)}, bf16[3,32,128]{2,1,0:T(8,128)(2,1)}, bf16[3,32,128]{2,1,0:T(8,128)(2,1)}, bf16[3,32,128]{2,1,0:T(8,128)(2,1)}) conditional(s32[]{:T(128)} %clamp.4, (bf16[3,32,128]{2,1,0:T(8,128)(2,1)S(1)}, bf16[3,32,128]{2,1,0:T(8,128)(2,1)S(1)}) %tuple.80, ...), branch_computations={%region_0.1_spmd, %region_1.2_spmd, %region_2.3_spmd, %region_3.4_... | conditional | bytes 393408 | solution.py:529
  7.3 3.0 %collective-permute-start.20 = (bf16[3,32,128]{2,1,0:T(8,128)(2,1)S(1)}, bf16[3,32,128]{2,1,0:T(8,128)(2,1)}, u32[]{:S(2)}, u32[]{:S(2)}) collective-permute-start(bf16[3,32,128]{2,1,0:T(8,128)(2,1)S(1)} %get-tuple-element.78), channel_id=1, source_target_pairs={{0,8},{1,9},{2,10},{3,11},{4,12},{5,13},{6,14},{7,15},{8,16},{9,17... | collective-permute-start | bytes 73736 | tf_op jit(solution)/shard_map/cond/branch_5_fun/ppermute | solution.py:521
  10.3 1.3 collective-permute-start.21
  11.5 1.3 collective-permute-start.22
  12.8 1.3 collective-permute-start.23
  14.1 0.9 collective-permute-done.21
  15.0 0.8 fusion.3
  15.8 0.8 broadcast_select_fusion.1.north
  16.6 0.8 copy.33
  17.5 1.6 %collective-permute-start.64 = (bf16[3,134,128]{2,1,0:T(8,128)(2,1)S(1)}, bf16[3,134,128]{2,1,0:T(8,128)(2,1)S(1)}, u32[]{:S(2)}, u32[]{:S(2)}) collective-permute-start(bf16[3,134,128]{2,1,0:T(8,128)(2,1)S(1)} %pad_maximum_fusion.1), channel_id=1, source_target_pairs={{0,1},{1,2},{2,3},{3,4},{4,5},{5,6},{6,7},{7,0},{8,9},{9,10},{10,1... | collective-permute-start | bytes 308744 | tf_op jit(solution)/shard_map/ppermute | solution.py:562
  19.3 3.3 %collective-permute-start.65 = (bf16[3,134,128]{2,1,0:T(8,128)(2,1)S(1)}, bf16[3,134,128]{2,1,0:T(8,128)(2,1)S(1)}, u32[]{:S(2)}, u32[]{:S(2)}) collective-permute-start(bf16[3,134,128]{2,1,0:T(8,128)(2,1)S(1)} %pad_maximum_fusion.2), channel_id=1, source_target_pairs={{0,7},{1,0},{2,1},{3,2},{4,3},{5,4},{6,5},{7,6},{8,15},{9,8},{10,9... | collective-permute-start | bytes 308744 | tf_op jit(solution)/shard_map/ppermute | solution.py:561
  22.7 0.8 maximum_maximum_fusion.up
  25.1 1.6 %broadcast_in_dim.23.landb = bf16[4096,128]{1,0:T(8,128)(2,1)} broadcast(bf16[4096]{0:T(1024)(128)(2,1)S(1)} %broadcast_in_dim.22), dimensions={0} | broadcast | bytes 1056768 | tf_op jit(solution)/shard_map/broadcast_in_dim | solution.py:564
  26.7 46.3 %block_pass.1 = (bf16[64,128]{1,0:T(8,128)(2,1)}, bf16[4096,128]{1,0:T(8,128)(2,1)}, bf16[4096,128]{1,0:T(8,128)(2,1)}, bf16[3,32,128]{2,1,0:T(8,128)(2,1)S(1)},...) custom-call(bf16[128,32,128]{2,1,0:T(8,128)(2,1)} %field.1, ...), custom_call_target="tpu_custom_call" | custom-call | tf_op jit(solution)/shard_map/block_pass/pallas_call | solution.py:318
  73.0 1.1 constant_dynamic-slice_fusion
  74.1 2.1 %collective-permute-start.68 = (bf16[1344,128]{1,0:T(8,128)(2,1)S(1)}, bf16[1344,128]{1,0:T(8,128)(2,1)S(1)}, u32[]{:S(2)}, u32[]{:S(2)}) collective-permute-start(bf16[1344,128]{1,0:T(8,128)(2,1)S(1)} %constant_dynamic-slice_fusion), channel_id=1, source_target_pairs={{0,8},{8,0},{16,24},{24,16},{1,9},{9,1},{17,25},{25,17},{2,10},{10... | collective-permute-start | bytes 1032200 | tf_op jit(solution)/shard_map/ppermute | solution.py:482
  76.2 14.8 %conditional.3 = (bf16[3,32,128]{2,1,0:T(8,128)(2,1)}, bf16[3,32,128]{2,1,0:T(8,128)(2,1)}, bf16[3,32,128]{2,1,0:T(8,128)(2,1)}, bf16[3,32,128]{2,1,0:T(8,128)(2...) conditional(s32[]{:T(128)} %clamp.4, ...), branch_computations={%region_8.9_spmd, %region_9.10_spmd, %region_10.11_spmd, %region_1... | conditional | bytes 421116 | solution.py:529
  76.2 2.6 %collective-permute-start.52 = (bf16[3,32,128]{2,1,0:T(8,128)(2,1)S(1)}, bf16[3,32,128]{2,1,0:T(8,128)(2,1)}, u32[]{:S(2)}, u32[]{:S(2)}) collective-permute-start(bf16[3,32,128]{2,1,0:T(8,128)(2,1)S(1)} %get-tuple-element.94), channel_id=1, source_target_pairs={{0,8},{1,9},{2,10},{3,11},{4,12},{5,13},{6,14},{7,15},{8,16},{9,17... | collective-permute-start | bytes 73736 | tf_op jit(solution)/shard_map/cond/branch_5_fun/ppermute | solution.py:521
  78.8 1.2 collective-permute-start.54
  80.1 1.3 collective-permute-start.55
  81.3 1.3 collective-permute-start.53
  82.6 1.3 fusion.9
  84.5 0.7 reshape.73
  85.2 5.8 %collective-permute-done.53 = bf16[3,32,128]{2,1,0:T(8,128)(2,1)} collective-permute-done((bf16[3,32,128]{2,1,0:T(8,128)(2,1)S(1)}, bf16[3,32,128]{2,1,0:T(8,128)(2,1)}, u32[]{:S(2)}, u32[]{:S(2)}) %collective-permute-start.53) | collective-permute-done | bytes 24608 | tf_op jit(solution)/shard_map/cond/branch_5_fun/ppermute | solution.py:522
  91.1 1.2 collective-permute-start.71
  92.3 2.5 %collective-permute-start.70 = (bf16[336,128]{1,0:T(8,128)(2,1)S(1)}, bf16[336,128]{1,0:T(8,128)(2,1)S(1)}, u32[]{:S(2)}, u32[]{:S(2)}) collective-permute-start(bf16[336,128]{1,0:T(8,128)(2,1)S(1)} %get-tuple-element.176), channel_id=1, source_target_pairs={{0,16},{1,17},{2,18},{3,19},{4,20},{5,21},{6,22},{7,23},{8,24},{9,... | collective-permute-start | bytes 258056 | tf_op jit(solution)/shard_map/ppermute | solution.py:488
  94.9 1.4 collective-permute-start.69
  96.6 2.5 %collective-permute-done.70 = bf16[336,128]{1,0:T(8,128)(2,1)S(1)} collective-permute-done((bf16[336,128]{1,0:T(8,128)(2,1)S(1)}, bf16[336,128]{1,0:T(8,128)(2,1)S(1)}, u32[]{:S(2)}, u32[]{:S(2)}) %collective-permute-start.70) | collective-permute-done | bytes 86048 | tf_op jit(solution)/shard_map/ppermute | solution.py:488
  99.1 0.9 collective-permute-done.69
  100.0 3.8 %collective-permute-start.74 = (bf16[336,128]{1,0:T(8,128)(2,1)S(1)}, bf16[336,128]{1,0:T(8,128)(2,1)S(1)}, u32[]{:S(2)}, u32[]{:S(2)}) collective-permute-start(bf16[336,128]{1,0:T(8,128)(2,1)S(1)} %fusion.1), channel_id=1, source_target_pairs={{0,6},{1,7},{2,4},{3,5},{4,2},{5,3},{6,0},{7,1},{8,14},{9,15},{10,... | collective-permute-start | bytes 258056 | tf_op jit(solution)/shard_map/ppermute | solution.py:494
  104.5 0.8 fusion.2
  105.3 2.0 %collective-permute-done.74 = bf16[336,128]{1,0:T(8,128)(2,1)S(1)} collective-permute-done((bf16[336,128]{1,0:T(8,128)(2,1)S(1)}, bf16[336,128]{1,0:T(8,128)(2,1)S(1)}, u32[]{:S(2)}, u32[]{:S(2)}) %collective-permute-start.74) | collective-permute-done | bytes 86048 | tf_op jit(solution)/shard_map/ppermute | solution.py:494
  107.3 2.8 %collective-permute-done.73 = bf16[336,128]{1,0:T(8,128)(2,1)S(1)} collective-permute-done((bf16[336,128]{1,0:T(8,128)(2,1)S(1)}, bf16[336,128]{1,0:T(8,128)(2,1)S(1)}, u32[]{:S(2)}, u32[]{:S(2)}) %collective-permute-start.73) | collective-permute-done | bytes 86048 | tf_op jit(solution)/shard_map/ppermute | solution.py:494
  110.3 2.1 %collective-permute-start.77 = (bf16[336,128]{1,0:T(8,128)(2,1)S(1)}, bf16[336,128]{1,0:T(8,128)(2,1)S(1)}, u32[]{:S(2)}, u32[]{:S(2)}) collective-permute-start(bf16[336,128]{1,0:T(8,128)(2,1)S(1)} %add_convert_fusion.1), channel_id=1, source_target_pairs={{0,17},{1,16},{2,19},{3,18},{4,21},{5,20},{6,23},{7,22},{8,25},{9,... | collective-permute-start | bytes 258056 | tf_op jit(solution)/shard_map/ppermute | solution.py:501
  113.0 0.9 collective-permute-start.75
  113.9 0.7 broadcast_select_fusion.north
  114.6 1.9 %collective-permute-done.77 = bf16[336,128]{1,0:T(8,128)(2,1)S(1)} collective-permute-done((bf16[336,128]{1,0:T(8,128)(2,1)S(1)}, bf16[336,128]{1,0:T(8,128)(2,1)S(1)}, u32[]{:S(2)}, u32[]{:S(2)}) %collective-permute-start.77) | collective-permute-done | bytes 86048 | tf_op jit(solution)/shard_map/ppermute | solution.py:501
  117.6 0.7 copy-done.19
  118.4 1.0 collective-permute-start.66
  119.5 3.8 %collective-permute-start.67 = (bf16[402,128]{1,0:T(8,128)(2,1)S(1)}, bf16[402,128]{1,0:T(8,128)(2,1)S(1)}, u32[]{:S(2)}, u32[]{:S(2)}) collective-permute-start(bf16[402,128]{1,0:T(8,128)(2,1)S(1)} %pad_maximum_fusion.4), channel_id=1, source_target_pairs={{0,7},{1,0},{2,1},{3,2},{4,3},{5,4},{6,5},{7,6},{8,15},{9,8},{10,9... | collective-permute-start | bytes 308744 | tf_op jit(solution)/shard_map/ppermute | solution.py:583
  123.2 0.6 pad_add_fusion.idx
  124.5 1.4 collective-permute-done.66.gl
  127.1 15.1 %conv_back.1 = bf16[128,32,128]{2,1,0:T(8,128)(2,1)} custom-call(bf16[4096,128]{1,0:T(8,128)(2,1)} %get-tuple-element.133.g, bf16[4096,128]{1,0:T(8,128)(2,1)} %get-tuple-element.134.dirin, bf16[3,32,128]{2,1,0:T(8,128)(2,1)} %get-tuple-element.137.south, bf16[3,32,128]{2,1,0:T(8,128)(2,1)} %copy-done.13, bf16[402,128]{1,0:T(8,128)(2,1)} %copy-done.14, ...), custom_call_target="tpu_custom_call" | custom-call | tf_op jit(solution)/shard_map/conv_back/pallas_call | solution.py:400
  142.2 0.7 copy-done.2
  142.9 2.5 %finish_sums.1 = (f32[49,128]{1,0:T(8,128)}, f32[128,512]{1,0:T(8,128)}, f32[512,128]{1,0:T(8,128)}, f32[3,512,128]{2,1,0:T(8,128)}) custom-call(s32[2]{0:T(128)} %pad_add_fusion.idx, bf16[4,336,128]{2,1,0:T(8,128)(2,1)} %copy-done, bf16[4,336,128]{2,1,0:T(8,128)(2,1)} %copy-done.2), custom_call_target="tpu_custom_call" | custom-call | tf_op jit(solution)/shard_map/finish_sums/pallas_call | solution.py:442
  (90 shorter events, 7.6 us)
Async XLA Ops:
  7.3 6.8 %collective-permute-start.20 = (bf16[3,32,128]{2,1,0:T(8,128)(2,1)S(1)}, bf16[3,32,128]{2,1,0:T(8,128)(2,1)}, u32[]{:S(2)}, u32[]{:S(2)}) collective-permute-start(bf16[3,32,128]{2,1,0:T(8,128)(2,1)S(1)} %get-tuple-element.78), channel_id=1, source_target_pairs={{0,8},{1,9},{2,10},{3,11},{4,12},{5,13},{6,14},{7,15},{8,16},{9,17... | collective-permute-start | bytes 73736 | tf_op jit(solution)/shard_map/cond/branch_5_fun/ppermute | solution.py:521
  10.3 4.7 %collective-permute-start.21 = (bf16[3,32,128]{2,1,0:T(8,128)(2,1)S(1)}, bf16[3,32,128]{2,1,0:T(8,128)(2,1)}, u32[]{:S(2)}, u32[]{:S(2)}) collective-permute-start(bf16[3,32,128]{2,1,0:T(8,128)(2,1)S(1)} %get-tuple-element.79), channel_id=1, source_target_pairs={{8,0},{9,1},{10,2},{11,3},{12,4},{13,5},{14,6},{15,7},{16,8},{17,9... | collective-permute-start | bytes 73736 | tf_op jit(solution)/shard_map/cond/branch_5_fun/ppermute | solution.py:522
  11.5 3.5 %collective-permute-start.22 = (bf16[3,32,128]{2,1,0:T(8,128)(2,1)S(1)}, bf16[3,32,128]{2,1,0:T(8,128)(2,1)}, u32[]{:S(2)}, u32[]{:S(2)}) collective-permute-start(bf16[3,32,128]{2,1,0:T(8,128)(2,1)S(1)} %get-tuple-element.78), channel_id=1, source_target_pairs={{24,29},{25,28},{26,27},{27,26},{28,25},{29,24},{30,31},{31,30}} | collective-permute-start | bytes 73736 | tf_op jit(solution)/shard_map/cond/branch_5_fun/ppermute | solution.py:523
  12.8 2.2 %collective-permute-start.23 = (bf16[3,32,128]{2,1,0:T(8,128)(2,1)S(1)}, bf16[3,32,128]{2,1,0:T(8,128)(2,1)}, u32[]{:S(2)}, u32[]{:S(2)}) collective-permute-start(bf16[3,32,128]{2,1,0:T(8,128)(2,1)S(1)} %get-tuple-element.78), channel_id=1, source_target_pairs={{24,28},{25,27},{26,26},{27,25},{28,24},{29,31},{30,30},{31,29}} | collective-permute-start | bytes 73736 | tf_op jit(solution)/shard_map/cond/branch_5_fun/ppermute | solution.py:524
  16.6 0.8 copy-start.11
  17.5 7.5 %collective-permute-start.64 = (bf16[3,134,128]{2,1,0:T(8,128)(2,1)S(1)}, bf16[3,134,128]{2,1,0:T(8,128)(2,1)S(1)}, u32[]{:S(2)}, u32[]{:S(2)}) collective-permute-start(bf16[3,134,128]{2,1,0:T(8,128)(2,1)S(1)} %pad_maximum_fusion.1), channel_id=1, source_target_pairs={{0,1},{1,2},{2,3},{3,4},{4,5},{5,6},{6,7},{7,0},{8,9},{9,10},{10,1... | collective-permute-start | bytes 308744 | tf_op jit(solution)/shard_map/ppermute | solution.py:562
  19.2 3.3 %copy-start.20 = (s32[128,32]{0,1:T(8,128)S(1)}, s32[128,32]{0,1:T(8,128)}, u32[]{:S(2)}) copy-start(s32[128,32]{0,1:T(8,128)} %param.30) | copy-start | bytes 49156
  19.2 3.5 %copy-start.12 = (bf16[128,512]{1,0:T(8,128)(2,1)S(1)}, bf16[128,512]{1,0:T(8,128)(2,1)}, u32[]{:S(2)}) copy-start(bf16[128,512]{1,0:T(8,128)(2,1)} %param.34) | copy-start | bytes 393220
  19.2 3.4 %copy-start.23 = (bf16[512]{0:T(512)(128)(2,1)S(1)}, bf16[512]{0:T(512)(128)(2,1)}, u32[]{:S(2)}) copy-start(bf16[512]{0:T(512)(128)(2,1)} %param.35) | copy-start | bytes 3076
  19.3 5.9 %collective-permute-start.65 = (bf16[3,134,128]{2,1,0:T(8,128)(2,1)S(1)}, bf16[3,134,128]{2,1,0:T(8,128)(2,1)S(1)}, u32[]{:S(2)}, u32[]{:S(2)}) collective-permute-start(bf16[3,134,128]{2,1,0:T(8,128)(2,1)S(1)} %pad_maximum_fusion.2), channel_id=1, source_target_pairs={{0,7},{1,0},{2,1},{3,2},{4,3},{5,4},{6,5},{7,6},{8,15},{9,8},{10,9... | collective-permute-start | bytes 308744 | tf_op jit(solution)/shard_map/ppermute | solution.py:561
  23.6 0.7 copy-start.21
  25.1 1.6 %copy-start.16 = (bf16[3,134,128]{2,1,0:T(8,128)(2,1)}, bf16[3,134,128]{2,1,0:T(8,128)(2,1)S(1)}, u32[]{:S(2)}) copy-start(bf16[3,134,128]{2,1,0:T(8,128)(2,1)S(1)} %collective-permute-done.64.left) | copy-start | bytes 308740
  25.1 1.6 %copy-start.17 = (bf16[3,134,128]{2,1,0:T(8,128)(2,1)}, bf16[3,134,128]{2,1,0:T(8,128)(2,1)S(1)}, u32[]{:S(2)}) copy-start(bf16[3,134,128]{2,1,0:T(8,128)(2,1)S(1)} %collective-permute-done.65.right) | copy-start | bytes 308740
  73.0 18.0 %copy-start.1 = (bf16[2688,128]{1,0:T(8,128)(2,1)S(1)}, bf16[2688,128]{1,0:T(8,128)(2,1)}, u32[]{:S(2)}) copy-start(bf16[2688,128]{1,0:T(8,128)(2,1)} %get-tuple-element.145) | copy-start | bytes 2064388
  74.1 16.9 %collective-permute-start.68 = (bf16[1344,128]{1,0:T(8,128)(2,1)S(1)}, bf16[1344,128]{1,0:T(8,128)(2,1)S(1)}, u32[]{:S(2)}, u32[]{:S(2)}) collective-permute-start(bf16[1344,128]{1,0:T(8,128)(2,1)S(1)} %constant_dynamic-slice_fusion), channel_id=1, source_target_pairs={{0,8},{8,0},{16,24},{24,16},{1,9},{9,1},{17,25},{25,17},{2,10},{10... | collective-permute-start | bytes 1032200 | tf_op jit(solution)/shard_map/ppermute | solution.py:482
  76.2 6.4 %collective-permute-start.52 = (bf16[3,32,128]{2,1,0:T(8,128)(2,1)S(1)}, bf16[3,32,128]{2,1,0:T(8,128)(2,1)}, u32[]{:S(2)}, u32[]{:S(2)}) collective-permute-start(bf16[3,32,128]{2,1,0:T(8,128)(2,1)S(1)} %get-tuple-element.94), channel_id=1, source_target_pairs={{0,8},{1,9},{2,10},{3,11},{4,12},{5,13},{6,14},{7,15},{8,16},{9,17... | collective-permute-start | bytes 73736 | tf_op jit(solution)/shard_map/cond/branch_5_fun/ppermute | solution.py:521
  78.8 12.1 %collective-permute-start.54 = (bf16[3,32,128]{2,1,0:T(8,128)(2,1)S(1)}, bf16[3,32,128]{2,1,0:T(8,128)(2,1)}, u32[]{:S(2)}, u32[]{:S(2)}) collective-permute-start(bf16[3,32,128]{2,1,0:T(8,128)(2,1)S(1)} %get-tuple-element.94), channel_id=1, source_target_pairs={{24,29},{25,28},{26,27},{27,26},{28,25},{29,24},{30,31},{31,30}} | collective-permute-start | bytes 73736 | tf_op jit(solution)/shard_map/cond/branch_5_fun/ppermute | solution.py:523
  80.1 10.9 %collective-permute-start.55 = (bf16[3,32,128]{2,1,0:T(8,128)(2,1)S(1)}, bf16[3,32,128]{2,1,0:T(8,128)(2,1)}, u32[]{:S(2)}, u32[]{:S(2)}) collective-permute-start(bf16[3,32,128]{2,1,0:T(8,128)(2,1)S(1)} %get-tuple-element.94), channel_id=1, source_target_pairs={{24,28},{25,27},{26,26},{27,25},{28,24},{29,31},{30,30},{31,29}} | collective-permute-start | bytes 73736 | tf_op jit(solution)/shard_map/cond/branch_5_fun/ppermute | solution.py:524
  81.3 9.6 %collective-permute-start.53 = (bf16[3,32,128]{2,1,0:T(8,128)(2,1)S(1)}, bf16[3,32,128]{2,1,0:T(8,128)(2,1)}, u32[]{:S(2)}, u32[]{:S(2)}) collective-permute-start(bf16[3,32,128]{2,1,0:T(8,128)(2,1)S(1)} %get-tuple-element.95), channel_id=1, source_target_pairs={{8,0},{9,1},{10,2},{11,3},{12,4},{13,5},{14,6},{15,7},{16,8},{17,9... | collective-permute-start | bytes 73736 | tf_op jit(solution)/shard_map/cond/branch_5_fun/ppermute | solution.py:522
  83.9 0.6 copy-start.8
  91.1 5.4 %collective-permute-start.71 = (bf16[336,128]{1,0:T(8,128)(2,1)S(1)}, bf16[336,128]{1,0:T(8,128)(2,1)S(1)}, u32[]{:S(2)}, u32[]{:S(2)}) collective-permute-start(bf16[336,128]{1,0:T(8,128)(2,1)S(1)} %get-tuple-element.175), channel_id=1, source_target_pairs={{0,17},{1,16},{2,19},{3,18},{4,21},{5,20},{6,23},{7,22},{8,25},{9,... | collective-permute-start | bytes 258056 | tf_op jit(solution)/shard_map/ppermute | solution.py:488
  92.3 6.8 %collective-permute-start.70 = (bf16[336,128]{1,0:T(8,128)(2,1)S(1)}, bf16[336,128]{1,0:T(8,128)(2,1)S(1)}, u32[]{:S(2)}, u32[]{:S(2)}) collective-permute-start(bf16[336,128]{1,0:T(8,128)(2,1)S(1)} %get-tuple-element.176), channel_id=1, source_target_pairs={{0,16},{1,17},{2,18},{3,19},{4,20},{5,21},{6,22},{7,23},{8,24},{9,... | collective-permute-start | bytes 258056 | tf_op jit(solution)/shard_map/ppermute | solution.py:488
  94.9 5.1 %collective-permute-start.69 = (bf16[336,128]{1,0:T(8,128)(2,1)S(1)}, bf16[336,128]{1,0:T(8,128)(2,1)S(1)}, u32[]{:S(2)}, u32[]{:S(2)}) collective-permute-start(bf16[336,128]{1,0:T(8,128)(2,1)S(1)} %get-tuple-element.174), channel_id=1, source_target_pairs={{0,1},{1,0},{2,3},{3,2},{4,5},{5,4},{6,7},{7,6},{8,9},{9,8},{10,11... | collective-permute-start | bytes 258056 | tf_op jit(solution)/shard_map/ppermute | solution.py:488
  100.0 7.3 %collective-permute-start.74 = (bf16[336,128]{1,0:T(8,128)(2,1)S(1)}, bf16[336,128]{1,0:T(8,128)(2,1)S(1)}, u32[]{:S(2)}, u32[]{:S(2)}) collective-permute-start(bf16[336,128]{1,0:T(8,128)(2,1)S(1)} %fusion.1), channel_id=1, source_target_pairs={{0,6},{1,7},{2,4},{3,5},{4,2},{5,3},{6,0},{7,1},{8,14},{9,15},{10,... | collective-permute-start | bytes 258056 | tf_op jit(solution)/shard_map/ppermute | solution.py:494
  103.8 6.3 %collective-permute-start.73 = (bf16[336,128]{1,0:T(8,128)(2,1)S(1)}, bf16[336,128]{1,0:T(8,128)(2,1)S(1)}, u32[]{:S(2)}, u32[]{:S(2)}) collective-permute-start(bf16[336,128]{1,0:T(8,128)(2,1)S(1)} %fusion.1), channel_id=1, source_target_pairs={{0,4},{1,5},{2,6},{3,7},{4,0},{5,1},{6,2},{7,3},{8,12},{9,13},{10,... | collective-permute-start | bytes 258056 | tf_op jit(solution)/shard_map/ppermute | solution.py:494
  103.8 6.4 %collective-permute-start.72 = (bf16[336,128]{1,0:T(8,128)(2,1)S(1)}, bf16[336,128]{1,0:T(8,128)(2,1)S(1)}, u32[]{:S(2)}, u32[]{:S(2)}) collective-permute-start(bf16[336,128]{1,0:T(8,128)(2,1)S(1)} %fusion.1), channel_id=1, source_target_pairs={{0,2},{1,3},{2,0},{3,1},{4,6},{5,7},{6,4},{7,5},{8,10},{9,11},{10,... | collective-permute-start | bytes 258056 | tf_op jit(solution)/shard_map/ppermute | solution.py:494
  110.3 6.2 %collective-permute-start.77 = (bf16[336,128]{1,0:T(8,128)(2,1)S(1)}, bf16[336,128]{1,0:T(8,128)(2,1)S(1)}, u32[]{:S(2)}, u32[]{:S(2)}) collective-permute-start(bf16[336,128]{1,0:T(8,128)(2,1)S(1)} %add_convert_fusion.1), channel_id=1, source_target_pairs={{0,17},{1,16},{2,19},{3,18},{4,21},{5,20},{6,23},{7,22},{8,25},{9,... | collective-permute-start | bytes 258056 | tf_op jit(solution)/shard_map/ppermute | solution.py:501
  112.4 4.6 %collective-permute-start.76 = (bf16[336,128]{1,0:T(8,128)(2,1)S(1)}, bf16[336,128]{1,0:T(8,128)(2,1)S(1)}, u32[]{:S(2)}, u32[]{:S(2)}) collective-permute-start(bf16[336,128]{1,0:T(8,128)(2,1)S(1)} %add_convert_fusion.1), channel_id=1, source_target_pairs={{0,16},{1,17},{2,18},{3,19},{4,20},{5,21},{6,22},{7,23},{8,24},{9,... | collective-permute-start | bytes 258056 | tf_op jit(solution)/shard_map/ppermute | solution.py:501
  113.0 4.5 %collective-permute-start.75 = (bf16[336,128]{1,0:T(8,128)(2,1)S(1)}, bf16[336,128]{1,0:T(8,128)(2,1)S(1)}, u32[]{:S(2)}, u32[]{:S(2)}) collective-permute-start(bf16[336,128]{1,0:T(8,128)(2,1)S(1)} %add_convert_fusion.1), channel_id=1, source_target_pairs={{0,1},{1,0},{2,3},{3,2},{4,5},{5,4},{6,7},{7,6},{8,9},{9,8},{10,11... | collective-permute-start | bytes 258056 | tf_op jit(solution)/shard_map/ppermute | solution.py:501
  114.6 3.0 %copy-start.13 = (bf16[3,32,128]{2,1,0:T(8,128)(2,1)}, bf16[3,32,128]{2,1,0:T(8,128)(2,1)S(1)}, u32[]{:S(2)}) copy-start(bf16[3,32,128]{2,1,0:T(8,128)(2,1)S(1)} %broadcast_select_fusion.north) | copy-start | bytes 73732
  117.5 0.9 copy-start.19
  117.5 24.7 %copy-start = (bf16[4,336,128]{2,1,0:T(8,128)(2,1)}, bf16[4,336,128]{2,1,0:T(8,128)(2,1)S(1)}, u32[]{:S(2)}) copy-start(bf16[4,336,128]{2,1,0:T(8,128)(2,1)S(1)} %pad_maximum_fusion.mine) | copy-start | bytes 1032196
  117.5 24.6 %collective-permute-start.78 = (bf16[4,336,128]{2,1,0:T(8,128)(2,1)S(1)}, bf16[4,336,128]{2,1,0:T(8,128)(2,1)S(1)}, u32[]{:S(2)}, u32[]{:S(2)}) collective-permute-start(bf16[4,336,128]{2,1,0:T(8,128)(2,1)S(1)} %pad_maximum_fusion.mine), channel_id=1, source_target_pairs={{0,8},{8,0},{16,24},{24,16},{1,9},{9,1},{17,25},{25,17},{2,10},{10... | collective-permute-start | bytes 1032200 | tf_op jit(solution)/shard_map/ppermute | solution.py:503
  118.4 1.1 copy-start.18
  118.4 7.5 %collective-permute-start.66 = (bf16[402,128]{1,0:T(8,128)(2,1)S(1)}, bf16[402,128]{1,0:T(8,128)(2,1)S(1)}, u32[]{:S(2)}, u32[]{:S(2)}) collective-permute-start(bf16[402,128]{1,0:T(8,128)(2,1)S(1)} %pad_maximum_fusion.3), channel_id=1, source_target_pairs={{0,1},{1,2},{2,3},{3,4},{4,5},{5,6},{6,7},{7,0},{8,9},{9,10},{10,1... | collective-permute-start | bytes 308744 | tf_op jit(solution)/shard_map/ppermute | solution.py:584
  119.4 4.5 %copy-start.22 = (bf16[64,128]{1,0:T(8,128)(2,1)S(1)}, bf16[64,128]{1,0:T(8,128)(2,1)}, u32[]{:S(2)}) copy-start(bf16[64,128]{1,0:T(8,128)(2,1)} %get-tuple-element.132) | copy-start | bytes 49156
  119.5 7.0 %collective-permute-start.67 = (bf16[402,128]{1,0:T(8,128)(2,1)S(1)}, bf16[402,128]{1,0:T(8,128)(2,1)S(1)}, u32[]{:S(2)}, u32[]{:S(2)}) collective-permute-start(bf16[402,128]{1,0:T(8,128)(2,1)S(1)} %pad_maximum_fusion.4), channel_id=1, source_target_pairs={{0,7},{1,0},{2,1},{3,2},{4,3},{5,4},{6,5},{7,6},{8,15},{9,8},{10,9... | collective-permute-start | bytes 308744 | tf_op jit(solution)/shard_map/ppermute | solution.py:583
  125.9 1.1 copy-start.14
  126.4 0.6 copy-start.15
  142.2 0.8 copy-start.2
where the time goes:
time: 146 us; the launch traced here: 145 us
  Pallas kernels  63.9 us (44%)
  starting transfers between devices  38.2 us (26%)
  waiting for transfers between devices  20.3 us (14%)
  local copies, waits for them, and re-layouts  14.5 us (10%)
  other arithmetic  4.92 us (3%)
  between operations  3.58 us (2%)
    pallas_call x1, Pallas kernels, block_pass(): pl.pallas_call(functools.partial(block_body, R, CW), out_shape=out_shape,...  46.3 us
    pallas_call x1, Pallas kernels, conv_back(): pl.pallas_call(functools.partial(conv_back_body, R, CW), out_shape=jax.Sh...  15.1 us
    ppermute x2, waiting for transfers between devices, run(): lax.ppermute(first, axes, down)  6.67 us
    ppermute x2, starting transfers between devices, run(): lax.ppermute(last, axes, up)  5.57 us
    ppermute x3, starting transfers between devices, all_sums(): lax.ppermute(part, ('lat', 'lon'), both_pairs(k // 2 * 2, k % 2))  5.16 us
    ppermute x3, waiting for transfers between devices, all_sums(): lax.ppermute(total, 'lon', flip_pairs('lon', bit * k))  4.98 us
    ppermute x3, starting transfers between devices, all_sums(): lax.ppermute(total, 'lon', flip_pairs('lon', bit * k))  4.46 us
    ppermute x1, starting transfers between devices, on_device(): gr = lax.ppermute(pack(lcol, 0), 'lon', shift_pairs('lon', -1))  3.79 us
  transfers between devices with their start and end apart: 23, of which 14 were waited for; matrix products, arithmetic and copies ran while one was open for 5% of the time, Pallas kernels for 10%

commit v1 on v0

--- a/solution.py
+++ b/solution.py
@@ -16,6 +16,7 @@
 VMEM = pl.BlockSpec(memory_space=pltpu.VMEM)
 SMEM = pl.BlockSpec(memory_space=pltpu.SMEM)
 PARAMS = pltpu.CompilerParams(vmem_limit_bytes=60 * 2**20)
+SMALL = pltpu.CompilerParams(vmem_limit_bytes=24 * 2**20)
 
 
 def dot(a, b):
@@ -59,12 +60,12 @@
 
 def weights_table(dw, w49, flip):
     for t in range(49):
-        w49[48 - t if flip else t] = jnp.broadcast_to(dw[t : t + 1, :].astype(f32), (S, 128))
+        w49[48 - t if flip else t] = jnp.broadcast_to(dw[t : t + 1, :].astype(f32), (S, 128)).astype(w49.dtype)
 
 
 def conv49(el, w49, emit, I, CW):
     CE = CW + 6
-    CG = 8
+    CG = 4
 
     def step(n, _):
         i = n // (CW // CG)
@@ -73,7 +74,7 @@
         for a in range(7):
             row = [el[(i + a) * CE + c0 + m].astype(f32) for m in range(CG + 6)]
             for b in range(7):
-                w = w49[a * 7 + b]
+                w = w49[a * 7 + b].astype(f32)
                 for k in range(CG):
                     pr = row[k + b] * w
                     acc[k] = pr if acc[k] is None else acc[k] + pr
@@ -88,7 +89,7 @@
     R, CW,
     field, south, north, left, right, landb, dw, gain, up, down, scale, sgain, sw, sbias, cot,
     bott, gout, dirout, first, last, lcol, rcol, sums,
-    x2d, el, w49, dep, hat, rst, nrm, act, slp, shat, srst, p1, back, tacc, downs, ups,
+    x2d, el, w49, dep, hat, rst, nrm, act, slp, shat, srst, p1, back, tacc, downs, ups, mgs,
 ):
     I = R // S
     CE = CW + 6
@@ -96,19 +97,22 @@
     n0 = R * CW
 
     def asm(r, _):
-        x2d[pl.ds((r + 3) * XW + 3, CW), :] = field[r].astype(f32)
+        x2d[pl.ds((r + 3) * XW + (r + 3) // I + 3, CW), :] = field[r].astype(f32)
         return 0
 
     lax.fori_loop(0, R, asm, 0, unroll=4)
+    PB = I * XW + 1
     for k in range(3):
         x2d[pl.ds(k * XW + 3, CW), :] = south[k].astype(f32)
-        x2d[pl.ds((R + 3 + k) * XW + 3, CW), :] = north[k].astype(f32)
-        x2d[pl.ds(k, R + 6, stride=XW), :] = left[k].astype(f32)
-        x2d[pl.ds(CW + 3 + k, R + 6, stride=XW), :] = right[k].astype(f32)
+        x2d[pl.ds((R + 3 + k) * XW + (R + 3 + k) // I + 3, CW), :] = north[k].astype(f32)
+        for m in range((R + 6 + I - 1) // I):
+            rows = min(I, R + 6 - m * I)
+            x2d[pl.ds(m * PB + k, rows, stride=XW), :] = left[k, m * I : m * I + rows, :].astype(f32)
+            x2d[pl.ds(m * PB + CW + 3 + k, rows, stride=XW), :] = right[k, m * I : m * I + rows, :].astype(f32)
 
     def tr(i, _):
         for c in range(CE):
-            el[i * CE + c] = x2d[pl.ds(i * XW + c, S, stride=I * XW), :].astype(bf16)
+            el[i * CE + c] = x2d[pl.ds(i * XW + i // I + c, S, stride=PB), :].astype(bf16)
         return 0
 
     lax.fori_loop(0, I + 6, tr, 0)
@@ -214,39 +218,50 @@
     put(0, dot_t(b1, p1[...]), 4)
     back[...] = b1
 
-    downs[...] = jnp.zeros_like(downs)
-    ups[...] = jnp.zeros_like(ups)
-    T = 256
-    TC = T // S
-
-    def bwd(n, _):
-        i2 = n // (CW // TC)
-        h = n % (CW // TC)
-        pb = pl.multiple_of((i2 * (CW // 2) + h * (TC // 2)) * S, T // 2)
-        bk = back[pl.ds(pb, T // 2), :]
+    QP = TP // 4
+
+    def bk1(i2, _):
+        pb = pl.multiple_of(i2 * QP, QP)
+        bk = back[pl.ds(pb, QP), :]
+        base = pl.multiple_of(i2 * TP, TP)
+        us = []
         for a in range(2):
-            base = pl.multiple_of(((i2 * 2 + a) * CW + h * TC) * S, T)
             sp = dot_r(bk, sw[0, a * 256 : (a + 1) * 256, :])
-            sp = jnp.stack(
-                [sp[:, :128].reshape(TC // 2, S, 128), sp[:, 128:].reshape(TC // 2, S, 128)], axis=1
-            ).reshape(T, 128)
-            b0 = norm_bwd(sp * sg0, shat[pl.ds(base, T), :], srst[pl.ds(base, T), :], pm).astype(bf16).astype(f32)
-            dr = landb[pl.ds(base, T), :].astype(f32) * b0
-            dirout[pl.ds(base, T), :] = dr.astype(bf16)
-            mg = (dr * sc).astype(bf16)
-            downs[...] += dot_t(mg, act[pl.ds(base, T), :])
-            hgs = []
-            for q in range(2):
-                ag = dot_r(mg, down[q * 256 : (q + 1) * 256, :])
-                hgs.append((ag * slp[pl.ds(base, T), q * 256 : (q + 1) * 256].astype(f32)).astype(bf16))
-            hg = jnp.concatenate(hgs, axis=1)
-            ups[...] += dot_t(nrm[pl.ds(base, T), :], hg)
-            ng = dot_r(hg, up[0:128, :])
-            dg = norm_bwd(ng * g_n, hat[pl.ds(base, T), :], rst[pl.ds(base, T), :], pm)
-            gout[pl.ds(base, T), :] = dg.astype(bf16)
-        return 0
-
-    lax.fori_loop(0, (I // 2) * (CW // TC), bwd, 0)
+            us.append(
+                jnp.stack(
+                    [sp[:, :128].reshape(CW // 2, S, 128), sp[:, 128:].reshape(CW // 2, S, 128)], axis=1
+                ).reshape(TP // 2, 128)
+            )
+        u = jnp.concatenate(us, axis=0) * sg0
+        b0 = norm_bwd(u, shat[pl.ds(base, TP), :], srst[pl.ds(base, TP), :], pm).astype(bf16).astype(f32)
+        dr = landb[pl.ds(base, TP), :].astype(f32) * b0
+        dirout[pl.ds(base, TP), :] = dr.astype(bf16)
+        mgs[pl.ds(base, TP), :] = (dr * sc).astype(bf16)
+        return 0
+
+    lax.fori_loop(0, I // 2, bk1, 0)
+
+    def bk2(n, _):
+        base = pl.multiple_of(n * T2, T2)
+        mg = mgs[pl.ds(base, T2), :]
+        for q in range(2):
+            ag = dot_r(mg, down[q * 256 : (q + 1) * 256, :])
+            sl = slp[pl.ds(base, T2), q * 256 : (q + 1) * 256].astype(f32)
+            slp[pl.ds(base, T2), q * 256 : (q + 1) * 256] = (ag * sl).astype(bf16)
+        return 0
+
+    lax.fori_loop(0, n0 // T2, bk2, 0)
+
+    def bk3(n, _):
+        base = pl.multiple_of(n * T1, T1)
+        ng = dot_r(slp[pl.ds(base, T1), :], up[0:128, :])
+        dg = norm_bwd(ng * g_n, hat[pl.ds(base, T1), :], rst[pl.ds(base, T1), :], pm)
+        gout[pl.ds(base, T1), :] = dg.astype(bf16)
+        return 0
+
+    lax.fori_loop(0, n0 // T1, bk3, 0)
+    downs[...] = dot_t(mgs[...], act[...])
+    ups[...] = dot_t(nrm[...], slp[...])
     put(1536, downs[...], 4)
     put(2048, ups[...], 4)
 
@@ -298,9 +313,9 @@
     )
     V = pltpu.VMEM
     scratch = [
-        V(((R + 6) * 40, C), f32),
+        V(((R + 6) * 40 + (R + 6) // I + 16, C), f32),
         V(((I + 6) * (CW + 6), S, C), bf16),
-        V((49, S, C), f32),
+        V((49, S, C), bf16),
         V((n, C), f32),
         V((n, C), f32),
         V((n, C), f32),
@@ -314,6 +329,7 @@
         V((49, 8, C), f32),
         V((C, 512), f32),
         V((C, 512), f32),
+        V((n, C), bf16),
     ]
     return pl.pallas_call(
         functools.partial(block_body, R, CW),
@@ -326,91 +342,162 @@
     )(field, south, north, left, right, landb, dw, gain, upx, down, scale, sgain, sw, sbias, cot)
 
 
-def conv_back_body(R, CW, g, dirin, south, north, gl, gr, dw, flag, out, gx, gext, w49, acc):
+def conv_back_body(R, CW, g, dirin, dw, out, gx, gext, w49):
     I = R // S
     CE = CW + 6
-    n0 = R * CW
-    isn = flag[...].astype(f32)
-    nots = 1.0 - isn
-    core = I * 3 * S
-
-    for i in range(I):
-        at = (i + 3) * CE * S
-        gx[pl.ds(at, 3 * S), :] = gl[i * 3 * S : (i + 1) * 3 * S, :].astype(f32)
-        gx[pl.ds(at + 3 * S, CW * S), :] = g[i * CW * S : (i + 1) * CW * S, :].astype(f32)
-        gx[pl.ds(at + (3 + CW) * S, 3 * S), :] = gr[i * 3 * S : (i + 1) * 3 * S, :].astype(f32)
     row = lax.broadcasted_iota(jnp.int32, (S, 128), 0)
-
+    zero = jnp.zeros((3, S, 128), bf16)
+
+    def cpy(i, _):
+        gext[pl.ds((i + 3) * CE, 3)] = zero
+        gext[pl.ds((i + 3) * CE + 3, CW)] = g[pl.ds(pl.multiple_of(i * CW * S, CW * S), CW * S), :].reshape(CW, S, 128)
+        gext[pl.ds((i + 3) * CE + 3 + CW, 3)] = zero
+        return 0
+
+    lax.fori_loop(0, I, cpy, 0)
     for k in range(3):
-        sk = jnp.concatenate([gl[core + k * 3 : core + k * 3 + 3, :].astype(f32), south[k].astype(f32), gr[core + k * 3 : core + k * 3 + 3, :].astype(f32)], axis=0)
-        nk = jnp.concatenate([gl[core + 9 + k * 3 : core + 12 + k * 3, :].astype(f32), north[k].astype(f32), gr[core + 9 + k * 3 : core + 12 + k * 3, :].astype(f32)], axis=0)
-        acc[k * 40 : k * 40 + CE, :] = sk
-        acc[(3 + k) * 40 : (3 + k) * 40 + CE, :] = nk
-    for k in range(3):
-        def lo(c, _, k=k):
-            v = gx[pl.ds(((I + k) * CE + c) * S, S), :]
-            v = pltpu.roll(v, 1, 0)
-            h = acc[pl.ds(k * 40 + c, 1), :]
-            gext[k * CE + c] = jnp.where(row == 0, h, v).astype(bf16)
-            v = gx[pl.ds(((3 + k) * CE + c) * S, S), :]
-            v = pltpu.roll(v, S - 1, 0)
-            h = acc[pl.ds((3 + k) * 40 + c, 1), :] * nots
-            gext[(I + 3 + k) * CE + c] = jnp.where(row == S - 1, h, v).astype(bf16)
+
+        def shift(c, _, k=k):
+            v = pltpu.roll(gext[(I + k) * CE + c].astype(f32), 1, 0)
+            gext[k * CE + c] = jnp.where(row == 0, 0.0, v).astype(bf16)
+            v = pltpu.roll(gext[(3 + k) * CE + c].astype(f32), S - 1, 0)
+            gext[(I + 3 + k) * CE + c] = jnp.where(row == S - 1, 0.0, v).astype(bf16)
             return 0
-        lax.fori_loop(0, CE, lo, 0, unroll=2)
-
-    def cpy(i, _):
-        gext[pl.ds((i + 3) * CE, CE)] = gx[pl.ds((i + 3) * CE * S, CE * S), :].astype(bf16).reshape(CE, S, 128)
-        return 0
-
-    lax.fori_loop(0, I, cpy, 0)
+
+        lax.fori_loop(0, CE, shift, 0, unroll=2)
     weights_table(dw, w49, True)
-    fold = []
-    for k in range(1, 4):
-        s = None
-        for rho in range(k - 1, 3):
-            a = 5 + k - rho
-            for b in range(7):
-                pr = acc[pl.ds((3 + rho) * 40 + b, CW), :] * w49[48 - (7 * a + b), 0:1, :]
-                s = pr if s is None else s + pr
-        fold.append(s * isn)
 
     def emit(i, c, v):
         at = pl.multiple_of((i * CW + c) * S, S)
-        gx[pl.ds(at, S), :] = v + dirin[pl.ds(at, S), :].astype(f32)
+        out[pl.ds(at, S), :] = v + dirin[pl.ds(at, S), :].astype(f32)
 
     conv49(gext, w49, emit, I, CW)
 
-    def unt(r, _):
-        s = r // I
-        i = r % I
-        out[r] = gx[pl.ds(i * CW * S + s, CW, stride=S), :].astype(bf16)
-        return 0
-
-    lax.fori_loop(0, R - 3, unt, 0, unroll=4)
-    for k in range(1, 4):
-        r = R - k
-        v = gx[pl.ds((r % I) * CW * S + r // I, CW, stride=S), :]
-        out[r] = (v + fold[k - 1]).astype(bf16)
-
-
-def conv_back(g, dirin, south, north, gl, gr, dw, flag, R, CW):
+
+def conv_back(g, dirin, dw, R, CW):
     C = g.shape[1]
     I = R // S
     return pl.pallas_call(
         functools.partial(conv_back_body, R, CW),
-        out_shape=jax.ShapeDtypeStruct((R, CW, C), bf16),
-        in_specs=[VMEM] * 8,
+        out_shape=jax.ShapeDtypeStruct((R * CW, C), f32),
+        in_specs=[VMEM] * 3,
         out_specs=VMEM,
         scratch_shapes=[
-            pltpu.VMEM(((I + 6) * (CW + 6) * S, C), f32),
+            pltpu.VMEM((8, C), f32),
             pltpu.VMEM(((I + 6) * (CW + 6), S, C), bf16),
+            pltpu.VMEM((49, S, C), bf16),
+        ],
+        compiler_params=SMALL,
+        cost_estimate=pl.CostEstimate(flops=10**8, bytes_accessed=30 * 2**20, transcendentals=0),
+        name="conv_back",
+    )(g, dirin, dw)
+
+
+def edges_body(R, CW, base, south, north, gl, gr, dw, flag, out, acc, rows, cols, w49):
+    I = R // S
+    CE = CW + 6
+    isn = flag[...].astype(f32)
+    nots = 1.0 - isn
+    core = I * 3 * S
+    row = lax.broadcasted_iota(jnp.int32, (S, 128), 0)
+    for t in range(49):
+        w49[t] = jnp.broadcast_to(dw[t : t + 1, :].astype(f32), (S, 128))
+    for side in range(2):
+        for k in range(3):
+            at = core + side * 9 + k * 3
+            mid = (north if side else south)[k]
+            rows[pl.ds((side * 3 + k) * 40, CE), :] = jnp.concatenate(
+                [gl[at : at + 3, :], mid, gr[at : at + 3, :]], axis=0
+            ).astype(f32)
+
+    def taps(k, a, flip):
+        s = None
+        for b in range(7):
+            o = 6 - b if flip else b
+            pr = rows[pl.ds(k * 40 + o, CW), :] * w49[7 * a + b, 0:1, :]
+            s = pr if s is None else s + pr
+        return s
+
+    low = []
+    for r in range(3):
+        low.append(sum(taps(k, r + 6 - k, True) for k in range(r, 3)))
+    high = []
+    for t in range(3):
+        v = sum(taps(3 + k, 2 - t - k, True) for k in range(3 - t)) * nots
+        k1 = t + 1
+        f = sum(taps(3 + rho, 5 + k1 - rho, False) for rho in range(k1 - 1, 3)) * isn
+        high.append(v + f)
+    for side in range(2):
+        src = gr if side else gl
+
+        def fill(i, _, src=src, side=side):
+            for j in range(3):
+                at = pl.multiple_of((i * 3 + j) * S, S)
+                cols[side * (I + 6) * 3 + (i + 3) * 3 + j] = src[pl.ds(at, S), :].astype(f32)
+            return 0
+
+        lax.fori_loop(0, I, fill, 0)
+        for k in range(3):
+            for j in range(3):
+                at = side * (I + 6) * 3
+                v = pltpu.roll(cols[at + (I + k) * 3 + j], 1, 0)
+                cols[at + k * 3 + j] = jnp.where(row == 0, 0.0, v)
+                v = pltpu.roll(cols[at + (3 + k) * 3 + j], S - 1, 0)
+                cols[at + (I + 3 + k) * 3 + j] = jnp.where(row == S - 1, 0.0, v)
+
+    PITCH = CW * S
+
+    def step(i, _):
+        at = pl.multiple_of(i * PITCH, PITCH)
+        acc[pl.ds(at, PITCH), :] = base[pl.ds(at, PITCH), :]
+        for side in range(2):
+            for t in range(3):
+                s = None
+                for j in range(3):
+                    b = 2 - t - j if side else t + 6 - j
+                    if b < 0 or b > 6:
+                        continue
+                    for a in range(7):
+                        pr = cols[side * (I + 6) * 3 + (i + 6 - a) * 3 + j] * w49[7 * a + b]
+                        s = pr if s is None else s + pr
+                c = CW - 1 - t if side else t
+                at = pl.multiple_of(i * PITCH + c * S, S)
+                acc[pl.ds(at, S), :] += s
+        return 0
+
+    lax.fori_loop(0, I, step, 0)
+
+    def unt(r, _):
+        s = r // I
+        i = r % I
+        out[r] = acc[pl.ds(i * PITCH + s, CW, stride=S), :].astype(bf16)
+        return 0
+
+    lax.fori_loop(3, R - 3, unt, 0, unroll=2)
+    for r in list(range(3)) + list(range(R - 3, R)):
+        v = acc[pl.ds((r % I) * PITCH + r // I, CW, stride=S), :]
+        v = v + (low[r] if r < 3 else high[R - 1 - r])
+        out[r] = v.astype(bf16)
+
+
+def edges(base, south, north, gl, gr, dw, flag, R, CW):
+    C = base.shape[1]
+    I = R // S
+    return pl.pallas_call(
+        functools.partial(edges_body, R, CW),
+        out_shape=jax.ShapeDtypeStruct((R, CW, C), bf16),
+        in_specs=[VMEM] * 7,
+        out_specs=VMEM,
+        scratch_shapes=[
+            pltpu.VMEM((R * CW, C), f32),
+            pltpu.VMEM((240, C), f32),
+            pltpu.VMEM((2 * (I + 6) * 3, S, C), f32),
             pltpu.VMEM((49, S, C), f32),
-            pltpu.VMEM((240, C), f32),
         ],
-        compiler_params=PARAMS,
-        name="conv_back",
-    )(g, dirin, south, north, gl, gr, dw, flag)
+        compiler_params=SMALL,
+        cost_estimate=pl.CostEstimate(flops=10**8, bytes_accessed=10 * 2**20, transcendentals=0),
+        name="edges",
+    )(base, south, north, gl, gr, dw, flag)
 
 
 def finish_body(factor, chunk, idx, mine, other, o_depth, o_up, o_down, o_sec, full):
@@ -470,23 +557,27 @@
     ]
 
 
-def all_sums(sums):
-    lat = lax.axis_index("lat")
-    lon = lax.axis_index("lon")
-    core = lat % 2
-    place = (lat // 2) * 2 + lon % 2
+def square_pairs(k):
+    return both_pairs((k // 2) * 2, k % 2)
+
+
+def sums_core(sums, core):
     half = sums.shape[0] // 2
-    chunk = half // 4
     keep = lax.dynamic_slice_in_dim(sums, core * half, half, 0)
     away = lax.dynamic_slice_in_dim(sums, (1 - core) * half, half, 0)
-    got = lax.ppermute(away, "lat", flip_pairs("lat", 1))
-    held = add_bf(keep, got).reshape(4, chunk, 128)
+    return add_bf(keep, lax.ppermute(away, "lat", flip_pairs("lat", 1))).reshape(4, half // 4, -1)
+
+
+def square_sum(held, place):
     own = lax.dynamic_index_in_dim(held, place, 0, keepdims=False)
     came = []
     for k in (1, 2, 3):
         part = lax.dynamic_index_in_dim(held, lax.bitwise_xor(place, k), 0, keepdims=False)
-        came.append(lax.ppermute(part, ("lat", "lon"), both_pairs((k // 2) * 2, k % 2)))
-    total = add_bf(own, *came)
+        came.append(lax.ppermute(part, ("lat", "lon"), square_pairs(k)))
+    return add_bf(own, *came)
+
+
+def line_sum(total):
     left = lax.axis_size("lon") // 2
     bit = 2
     while left > 1:
@@ -498,38 +589,35 @@
             total = add_bf(total, lax.ppermute(total, "lon", flip_pairs("lon", bit)))
             left //= 2
             bit *= 2
-    back = [lax.ppermute(total, ("lat", "lon"), both_pairs((k // 2) * 2, k % 2)) for k in (1, 2, 3)]
-    mine = jnp.stack([total, *back])
-    other = lax.ppermute(mine, "lat", flip_pairs("lat", 1))
-    return jnp.stack([core, place]).astype(jnp.int32), mine, other
-
-
-def halo_rows(first, last, quot, rem, north):
+    return total
+
+
+def halo_rows(first, last, quot, rem):
     nl = lax.axis_size("lon")
     nt = lax.axis_size("lat")
+    lat = lax.axis_index("lat")
+    odd = lat % 2 == 1
     cols = first.shape[1]
     top = (nt - 1) * nl
+    axes = ("lat", "lon")
+    near = lax.ppermute(jnp.where(odd, first, last), "lat", flip_pairs("lat", 1))
+    send = jnp.where(odd, last, first)
+    swap = [(a * nl + e, (a + 1) * nl + e) for a in range(1, nt - 1, 2) for e in range(nl)]
+    swap += [(j, i) for i, j in swap]
 
     def branch(q):
-        def run(first, last):
-            up = [(a * nl + b, (a + 1) * nl + b) for a in range(nt - 1) for b in range(nl)]
-            down = [(j, i) for i, j in up]
+        def run(send, last):
             fa = [(top + e, top + (q - e) % nl) for e in range(nl)]
             fb = [(top + e, top + (q - 1 - e) % nl) for e in range(nl)]
-            axes = ("lat", "lon")
-            return (
-                lax.ppermute(last, axes, up),
-                lax.ppermute(first, axes, down),
-                lax.ppermute(last, axes, fa),
-                lax.ppermute(last, axes, fb),
-            )
+            return lax.ppermute(send, axes, swap + fa), lax.ppermute(last, axes, fb)
 
         return run
 
-    south, above, blk_a, blk_b = lax.switch(quot, [branch(q) for q in range(nl)], first, last)
-    both = jnp.concatenate([blk_b, blk_a], axis=1)
+    far, blk_b = lax.switch(quot, [branch(q) for q in range(nl)], send, last)
+    south = jnp.where(odd, near, far)
+    both = jnp.concatenate([blk_b, far], axis=1)
     window = lax.dynamic_slice_in_dim(both, rem + 1, cols, 1)
-    return south, above, window[:, ::-1]
+    return south, jnp.where(odd, far, near), window[:, ::-1]
 
 
 def shift_pairs(axis, by):
@@ -550,7 +638,7 @@
     quot = mirror[0] // CW
     rem = mirror[0] % CW
 
-    south_f, above_f, fold_f = halo_rows(field[:3], field[R - 3 :], quot, rem, north)
+    south_f, above_f, fold_f = halo_rows(field[:3], field[R - 3 :], quot, rem)
     north_f = jnp.where(north, fold_f[::-1], above_f)
 
     def edge(lo):
@@ -572,7 +660,11 @@
     )
     level = bott.reshape(CW // 8, S, C).transpose(1, 0, 2)
 
-    south_g, above_g, fold_g = halo_rows(first, last, quot, rem, north)
+    core = lax.axis_index("lat") % 2
+    place = (lax.axis_index("lat") // 2) * 2 + lax.axis_index("lon") % 2
+    held = sums_core(sums, core)
+
+    south_g, above_g, fold_g = halo_rows(first, last, quot, rem)
     north_g = jnp.where(north, fold_g, above_g)
 
     def pack(cols, lo):
@@ -583,8 +675,18 @@
     gr = lax.ppermute(pack(lcol, 0), "lon", shift_pairs("lon", -1))
     gl = lax.ppermute(pack(rcol, CW - 3), "lon", shift_pairs("lon", 1))
     flag = jnp.broadcast_to(north.astype(bf16), (1, C))
-    idx, mine, other = all_sums(sums)
-    grad_field = conv_back(g, direct, south_g, north_g, gl, gr, depth_weight, flag, R, CW)
+    held, south_g = lax.optimization_barrier((held, south_g))
+    chunk = square_sum(held, place)
+    g, _ = lax.optimization_barrier((g, south_g))
+    base = conv_back(g, direct, depth_weight, R, CW)
+    chunk, base = lax.optimization_barrier((chunk, base))
+    chunk = line_sum(chunk)
+    grad_field = edges(base, south_g, north_g, gl, gr, depth_weight, flag, R, CW)
+    chunk, grad_field = lax.optimization_barrier((chunk, grad_field))
+    axes = ("lat", "lon")
+    mine = jnp.stack([chunk] + [lax.ppermute(chunk, axes, square_pairs(k)) for k in (1, 2, 3)])
+    other = lax.ppermute(mine, "lat", flip_pairs("lat", 1))
+    idx = jnp.stack([core, place]).astype(jnp.int32)
     g_depth, g_up, g_down, g_sec = finish(idx, mine, other, factor)
     return level, grad_field, g_depth, g_up, g_down, g_sec
 

time: 146 us -> 112 us (0.77)
  Pallas kernels: 63.9 us -> 42.4 us
  waiting for transfers between devices: 20.3 us -> 6.92 us
  local copies, waits for them, and re-layouts: 14.5 us -> 9.08 us
  other arithmetic: 4.92 us -> 9.87 us
    pallas_call x1, Pallas kernels: 46.3 us -> 32.8 us  [block_pass(): pl.pallas_call(functools.partial(block_body, R, CW), out_shape=out_shape,...]
    ppermute x19 -> x17, waiting for transfers between devices: 18.2 us -> 4.91 us  [the longest x3 3.39 us: on_device(): lax.ppermute(chunk, axes, square_pairs(k))]
    pallas_call x1, Pallas kernels: 15.1 us -> 3.45 us  [conv_back(): pl.pallas_call(functools.partial(conv_back_body, R, CW), out_shape=jax.Sh...]
    pallas_call x0 -> x1, Pallas kernels: none -> 3.71 us  [edges(): pl.pallas_call(functools.partial(edges_body, R, CW), out_shape=jax.ShapeD...]
    ppermute x1, waiting for transfers between devices: 0.09 us -> 1.69 us  [on_device(): left_f = lax.ppermute(edge(CW - 3), 'lon', shift_pairs('lon', 1))]
    concatenate x2, other arithmetic: 0.03 us -> 1.56 us  [pack(): jnp.concatenate([cols, south_g[:, lo:lo + 3].reshape(9, C), north_g[:, lo...]
    ppermute x19 -> x17, starting transfers between devices: 28.5 us -> 28.3 us  [the longest x2 7.49 us: halo_rows(): lax.ppermute(jnp.where(odd, first, last), 'lat', flip_pairs('lat', 1))]
  transfers between devices with their start and end apart: 23 -> 21, of which waited for: 14 -> 6; matrix products, arithmetic and copies ran while one was open for 5% -> 12% of each run, Pallas kernels for 10% -> 6%
where the time goes in v1:
time: 112 us; the launch traced here: 111 us
  Pallas kernels  42.4 us (38%)
  starting transfers between devices  39 us (35%)
  other arithmetic  9.87 us (9%)
  local copies, waits for them, and re-layouts  9.08 us (8%)
  waiting for transfers between devices  6.92 us (6%)
  between operations  3.65 us (3%)
    pallas_call x1, Pallas kernels, block_pass(): pl.pallas_call(functools.partial(block_body, R, CW), out_shape=out_shape,...  32.8 us
    ppermute x2, starting transfers between devices, halo_rows(): lax.ppermute(jnp.where(odd, first, last), 'lat', flip_pairs('lat', 1))  7.49 us
    ppermute x3, starting transfers between devices, square_sum(): came.append(lax.ppermute(part, ('lat', 'lon'), square_pairs(k)))  5.69 us
    ppermute x4, starting transfers between devices, run(): return (lax.ppermute(send, axes, swap + fa), lax.ppermute(last, axes, fb))  4.99 us
    ppermute x1, starting transfers between devices, on_device(): gr = lax.ppermute(pack(lcol, 0), 'lon', shift_pairs('lon', -1))  4.97 us
    ppermute x3, starting transfers between devices, line_sum(): lax.ppermute(total, 'lon', flip_pairs('lon', bit * k))  4.45 us
    pallas_call x1, Pallas kernels, edges(): pl.pallas_call(functools.partial(edges_body, R, CW), out_shape=jax.ShapeD...  3.71 us
    ppermute x3, starting transfers between devices, on_device(): lax.ppermute(chunk, axes, square_pairs(k))  3.55 us
  transfers between devices with their start and end apart: 21, of which 6 were waited for; matrix products, arithmetic and copies ran while one was open for 12% of the time, Pallas kernels for 6%

profile of v1, /device:TPU:0, one launch (start us, length us, event | category | flops | bytes accessed | tf_op | source)
XLA Modules:
  0.0 111.0 jit_solution(12587915583544691444)
XLA Ops:
  0.7 0.8 fusion.5
  1.4 0.5 collective-permute-start.32
  1.9 1.2 %slice.78 = s32[1]{0:T(128)} slice(s32[256]{0:T(256)} %param.31), slice={[0:1]} | slice | bytes 8 | tf_op jit(solution)/shard_map/slice | solution.py:638
  5.7 1.9 %fusion.4 = (bf16[128,1,128]{2,1,0:T(2,128)(2,1)S(1)}, bf16[128,1,128]{2,1,0:T(2,128)(2,1)S(1)}, bf16[128,1,128]{2,1,0:T(2,128)(2,1)S(1)}, bf16[128,1,128]{2,1,0...) fusion(bf16[128,32,128]{2,1,0:T(8,128)(2,1)} %field.1), kind=kLoop, calls=%fused_computation.56 | loop fusion | bytes 393216 | tf_op jit(solution)/shard_map/slice | solution.py:646
  7.6 0.7 broadcast_in_dim.25
  8.3 2.5 %conditional.2 = (bf16[3,32,128]{2,1,0:T(8,128)(2,1)}, bf16[3,32,128]{2,1,0:T(8,128)(2,1)}) conditional(s32[]{:T(128)} %clamp.4, (bf16[3,32,128]{2,1,0:T(8,128)(2,1)S(1)}, bf16[3,32,128]{2,1,0:T(8,128)(2,1)S(1)}) %tuple.76, (bf16[3,32,128]{2,1,0:T(8,128)(2,1)S(1)}, bf16[3,32,128]{2,1,0:T(8,128)(2,1)S(1)}) %tuple.76, ...), branch_computations={%region_0.1_spmd, %region_1.2_spmd, %region_2.3_spmd, %region_3.4_... | conditional | bytes 196704 | solution.py:616
  8.3 1.2 %collective-permute-start.8 = (bf16[3,32,128]{2,1,0:T(8,128)(2,1)S(1)}, bf16[3,32,128]{2,1,0:T(8,128)(2,1)}, u32[]{:S(2)}, u32[]{:S(2)}) collective-permute-start(bf16[3,32,128]{2,1,0:T(8,128)(2,1)S(1)} %get-tuple-element.72), channel_id=1, source_target_pairs={{8,16},{9,17},{10,18},{11,19},{12,20},{13,21},{14,22},{15,23},{16,... | collective-permute-start | bytes 73736 | tf_op jit(solution)/shard_map/cond/branch_4_fun/ppermute | solution.py:612
  9.5 1.2 %collective-permute-start.9 = (bf16[3,32,128]{2,1,0:T(8,128)(2,1)S(1)}, bf16[3,32,128]{2,1,0:T(8,128)(2,1)}, u32[]{:S(2)}, u32[]{:S(2)}) collective-permute-start(bf16[3,32,128]{2,1,0:T(8,128)(2,1)S(1)} %get-tuple-element.73), channel_id=1, source_target_pairs={{24,27},{25,26},{26,25},{27,24},{28,31},{29,30},{30,29},{31,28}} | collective-permute-start | bytes 73736 | tf_op jit(solution)/shard_map/cond/branch_4_fun/ppermute | solution.py:612
  10.9 1.7 %maximum_maximum_fusion.up = bf16[256,512]{1,0:T(8,128)(2,1)} fusion(bf16[1,512]{1,0:T(2,128)(2,1)S(1)} %broadcast_in_dim.25, bf16[128,512]{1,0:T(8,128)(2,1)} %param.34, bf16[256]{0:T(256)(128)(2,1)S(1)} %pad.16.clone), kind=kLoop, calls=%fused_computation.2 | loop fusion | flops 786432 | bytes 394752 | tf_op jit(solution)/shard_map/concatenate | solution.py:655
  12.6 0.8 fusion.3
  13.6 0.7 select_select_fusion.1
  14.5 2.6 %collective-permute-start.33 = (bf16[3,134,128]{2,1,0:T(8,128)(2,1)S(1)}, bf16[3,134,128]{2,1,0:T(8,128)(2,1)S(1)}, u32[]{:S(2)}, u32[]{:S(2)}) collective-permute-start(bf16[3,134,128]{2,1,0:T(8,128)(2,1)S(1)} %pad_maximum_fusion.1), channel_id=1, source_target_pairs={{0,1},{1,2},{2,3},{3,4},{4,5},{5,6},{6,7},{7,0},{8,9},{9,10},{10,1... | collective-permute-start | bytes 308744 | tf_op jit(solution)/shard_map/ppermute | solution.py:650
  17.2 3.1 %collective-permute-start.34 = (bf16[3,134,128]{2,1,0:T(8,128)(2,1)S(1)}, bf16[3,134,128]{2,1,0:T(8,128)(2,1)S(1)}, u32[]{:S(2)}, u32[]{:S(2)}) collective-permute-start(bf16[3,134,128]{2,1,0:T(8,128)(2,1)S(1)} %pad_maximum_fusion.2), channel_id=1, source_target_pairs={{0,7},{1,0},{2,1},{3,2},{4,3},{5,4},{6,5},{7,6},{8,15},{9,8},{10,9... | collective-permute-start | bytes 308744 | tf_op jit(solution)/shard_map/ppermute | solution.py:649
  20.6 0.6 copy.35
  21.2 1.7 %collective-permute-done.33.left = bf16[3,134,128]{2,1,0:T(8,128)(2,1)S(1)} collective-permute-done((bf16[3,134,128]{2,1,0:T(8,128)(2,1)S(1)}, bf16[3,134,128]{2,1,0:T(8,128)(2,1)S(1)}, u32[]{:S(2)}, u32[]{:S(2)}) %collective-permute-start.33) | collective-permute-done | bytes 102944 | tf_op jit(solution)/shard_map/ppermute | solution.py:650
  22.9 0.3 collective-permute-done.34.right
  23.2 1.6 %broadcast_in_dim.23.landb = bf16[4096,128]{1,0:T(8,128)(2,1)} broadcast(bf16[4096]{0:T(1024)(128)(2,1)S(1)} %broadcast_in_dim.22), dimensions={0} | broadcast | bytes 1056768 | tf_op jit(solution)/shard_map/broadcast_in_dim | solution.py:652
  24.8 32.8 %block_pass.1 = (bf16[64,128]{1,0:T(8,128)(2,1)}, bf16[4096,128]{1,0:T(8,128)(2,1)}, bf16[4096,128]{1,0:T(8,128)(2,1)}, bf16[3,32,128]{2,1,0:T(8,128)(2,1)}, bf1...) custom-call(bf16[128,32,128]{2,1,0:T(8,128)(2,1)} %field.1, ...), custom_call_target="tpu_custom_call" | custom-call | tf_op jit(solution)/shard_map/block_pass/pallas_call | solution.py:334
  57.6 1.1 constant_dynamic-slice_fusion
  58.7 2.0 %collective-permute-start.35 = (bf16[1344,128]{1,0:T(8,128)(2,1)S(1)}, bf16[1344,128]{1,0:T(8,128)(2,1)S(1)}, u32[]{:S(2)}, u32[]{:S(2)}) collective-permute-start(bf16[1344,128]{1,0:T(8,128)(2,1)S(1)} %constant_dynamic-slice_fusion), channel_id=1, source_target_pairs={{0,8},{8,0},{16,24},{24,16},{1,9},{9,1},{17,25},{25,17},{2,10},{10... | collective-permute-start | bytes 1032200 | tf_op jit(solution)/shard_map/ppermute | solution.py:568
  60.7 0.7 broadcast_select_fusion.1
  61.5 2.5 %conditional.3 = (bf16[3,32,128]{2,1,0:T(8,128)(2,1)}, bf16[3,32,128]{2,1,0:T(8,128)(2,1)}) conditional(s32[]{:T(128)} %clamp.4, (bf16[3,32,128]{2,1,0:T(8,128)(2,1)S(1)}, bf16[3,32,128]{2,1,0:T(8,128)(2,1)S(1)}) %tuple.77, (bf16[3,32,128]{2,1,0:T(8,128)(2,1)S(1)}, bf16[3,32,128]{2,1,0:T(8,128)(2,1)S(1)}) %tuple.77, ...), branch_computations={%region_8.9_spmd, %region_9.10_spmd, %region_10.11_spmd, %region_1... | conditional | bytes 196704 | solution.py:616
  61.5 1.2 %collective-permute-start.24 = (bf16[3,32,128]{2,1,0:T(8,128)(2,1)S(1)}, bf16[3,32,128]{2,1,0:T(8,128)(2,1)}, u32[]{:S(2)}, u32[]{:S(2)}) collective-permute-start(bf16[3,32,128]{2,1,0:T(8,128)(2,1)S(1)} %get-tuple-element.88), channel_id=1, source_target_pairs={{8,16},{9,17},{10,18},{11,19},{12,20},{13,21},{14,22},{15,23},{16,... | collective-permute-start | bytes 73736 | tf_op jit(solution)/shard_map/cond/branch_4_fun/ppermute | solution.py:612
  62.7 1.2 %collective-permute-start.25 = (bf16[3,32,128]{2,1,0:T(8,128)(2,1)S(1)}, bf16[3,32,128]{2,1,0:T(8,128)(2,1)}, u32[]{:S(2)}, u32[]{:S(2)}) collective-permute-start(bf16[3,32,128]{2,1,0:T(8,128)(2,1)S(1)} %get-tuple-element.89), channel_id=1, source_target_pairs={{24,27},{25,26},{26,25},{27,24},{28,31},{29,30},{30,29},{31,28}} | collective-permute-start | bytes 73736 | tf_op jit(solution)/shard_map/cond/branch_4_fun/ppermute | solution.py:612
  64.0 7.0 %collective-permute-start.36 = (bf16[3,32,128]{2,1,0:T(8,128)(2,1)S(1)}, bf16[3,32,128]{2,1,0:T(8,128)(2,1)S(1)}, u32[]{:S(2)}, u32[]{:S(2)}) collective-permute-start(bf16[3,32,128]{2,1,0:T(8,128)(2,1)S(1)} %get-tuple-element.163), channel_id=1, source_target_pairs={{0,8},{8,0},{16,24},{24,16},{1,9},{9,1},{17,25},{25,17},{2,10},{10... | collective-permute-start | bytes 73736 | tf_op jit(solution)/shard_map/ppermute | solution.py:603
  71.0 0.8 fusion.2
  71.9 0.7 select_select_fusion
  72.7 0.9 pad_maximum_fusion.3
  73.7 1.2 %add_convert_fusion = bf16[1344,128]{1,0:T(8,128)(2,1)S(1)} fusion(bf16[1344,128]{1,0:T(8,128)(2,1)S(1)} %collective-permute-done.35, bf16[2688,128]{1,0:T(8,128)(2,1)} %get-tuple-element.128, s32[]{:T(128)S(6)} %select_n.106), kind=kLoop, calls=%fused_computation | loop fusion | flops 688128 | bytes 1032196 | tf_op jit(solution)/shard_map/convert_element_type | solution.py:544
  74.9 4.0 %collective-permute-start.39 = (bf16[336,128]{1,0:T(8,128)(2,1)S(1)}, bf16[336,128]{1,0:T(8,128)(2,1)S(1)}, u32[]{:S(2)}, u32[]{:S(2)}) collective-permute-start(bf16[336,128]{1,0:T(8,128)(2,1)S(1)} %get-tuple-element.158), channel_id=1, source_target_pairs={{0,17},{1,16},{2,19},{3,18},{4,21},{5,20},{6,23},{7,22},{8,25},{9,... | collective-permute-start | bytes 258056 | tf_op jit(solution)/shard_map/ppermute | solution.py:576
  78.8 0.3 collective-permute-start.38
  79.2 1.4 %collective-permute-start.37 = (bf16[336,128]{1,0:T(8,128)(2,1)S(1)}, bf16[336,128]{1,0:T(8,128)(2,1)S(1)}, u32[]{:S(2)}, u32[]{:S(2)}) collective-permute-start(bf16[336,128]{1,0:T(8,128)(2,1)S(1)} %get-tuple-element.157), channel_id=1, source_target_pairs={{0,1},{1,0},{2,3},{3,2},{4,5},{5,4},{6,7},{7,6},{8,9},{9,8},{10,11... | collective-permute-start | bytes 258056 | tf_op jit(solution)/shard_map/ppermute | solution.py:576
  80.6 0.7 pad_maximum_fusion.4
  81.2 5.0 %collective-permute-start.44 = (bf16[402,128]{1,0:T(8,128)(2,1)}, bf16[402,128]{1,0:T(8,128)(2,1)S(1)}, u32[]{:S(2)}, u32[]{:S(2)}) collective-permute-start(bf16[402,128]{1,0:T(8,128)(2,1)} %pad_maximum_fusion.4), channel_id=1, source_target_pairs={{0,7},{1,0},{2,1},{3,2},{4,3},{5,4},{6,5},{7,6},{8,15},{9,8},{10,9... | collective-permute-start | bytes 308744 | tf_op jit(solution)/shard_map/ppermute | solution.py:675
  86.2 3.4 %conv_back.1.base = f32[4096,128]{1,0:T(8,128)S(1)} custom-call(bf16[4096,128]{1,0:T(8,128)(2,1)S(1)} %copy-done, bf16[4096,128]{1,0:T(8,128)(2,1)S(1)} %copy-done.1, bf16[49,128]{1,0:T(8,128)(2,1)S(1)} %copy-done.2), custom_call_target="tpu_custom_call" | custom-call | flops 100000000 | bytes 31457280 | tf_op jit(solution)/shard_map/conv_back/pallas_call | solution.py:380
  89.8 1.8 %collective-permute-start.42 = (bf16[336,128]{1,0:T(8,128)(2,1)S(1)}, bf16[336,128]{1,0:T(8,128)(2,1)S(1)}, u32[]{:S(2)}, u32[]{:S(2)}) collective-permute-start(bf16[336,128]{1,0:T(8,128)(2,1)S(1)} %fusion.1), channel_id=1, source_target_pairs={{0,6},{1,7},{2,4},{3,5},{4,2},{5,3},{6,0},{7,1},{8,14},{9,15},{10,... | collective-permute-start | bytes 258056 | tf_op jit(solution)/shard_map/ppermute | solution.py:585
  91.6 2.7 %collective-permute-start.40 = (bf16[336,128]{1,0:T(8,128)(2,1)S(1)}, bf16[336,128]{1,0:T(8,128)(2,1)S(1)}, u32[]{:S(2)}, u32[]{:S(2)}) collective-permute-start(bf16[336,128]{1,0:T(8,128)(2,1)S(1)} %fusion.1), channel_id=1, source_target_pairs={{0,2},{1,3},{2,0},{3,1},{4,6},{5,7},{6,4},{7,5},{8,10},{9,11},{10,... | collective-permute-start | bytes 258056 | tf_op jit(solution)/shard_map/ppermute | solution.py:585
  94.2 3.7 %edges.1 = bf16[128,32,128]{2,1,0:T(8,128)(2,1)} custom-call(f32[4096,128]{1,0:T(8,128)S(1)} %conv_back.1.base, bf16[3,32,128]{2,1,0:T(8,128)(2,1)S(1)} %get-tuple-element.134.south, bf16[3,32,128]{2,1,0:T(8,128)(2,1)S(1)} %get-tuple-element.160.north, bf16[402,128]{1,0:T(8,128)(2,1)S(1)} %collective-permute-done.43.gl, ...), custom_call_target="tpu_custom_call" | custom-call | flops 100000000 | bytes 10485760 | tf_op jit(solution)/shard_map/edges/pallas_call | solution.py:486
  98.0 1.0 collective-permute-done.41
  99.0 1.5 %collective-permute-start.47 = (bf16[336,128]{1,0:T(8,128)(2,1)S(1)}, bf16[336,128]{1,0:T(8,128)(2,1)S(1)}, u32[]{:S(2)}, u32[]{:S(2)}) collective-permute-start(bf16[336,128]{1,0:T(8,128)(2,1)S(1)} %add_convert_fusion.1), channel_id=1, source_target_pairs={{0,17},{1,16},{2,19},{3,18},{4,21},{5,20},{6,23},{7,22},{8,25},{9,... | collective-permute-start | bytes 258056 | tf_op jit(solution)/shard_map/ppermute | solution.py:687
  100.8 1.8 %collective-permute-start.45 = (bf16[336,128]{1,0:T(8,128)(2,1)S(1)}, bf16[336,128]{1,0:T(8,128)(2,1)S(1)}, u32[]{:S(2)}, u32[]{:S(2)}) collective-permute-start(bf16[336,128]{1,0:T(8,128)(2,1)S(1)} %add_convert_fusion.1), channel_id=1, source_target_pairs={{0,1},{1,0},{2,3},{3,2},{4,5},{5,4},{6,7},{7,6},{8,9},{9,8},{10,11... | collective-permute-start | bytes 258056 | tf_op jit(solution)/shard_map/ppermute | solution.py:687
  102.6 2.5 %collective-permute-done.47 = bf16[336,128]{1,0:T(8,128)(2,1)S(1)} collective-permute-done((bf16[336,128]{1,0:T(8,128)(2,1)S(1)}, bf16[336,128]{1,0:T(8,128)(2,1)S(1)}, u32[]{:S(2)}, u32[]{:S(2)}) %collective-permute-start.47) | collective-permute-done | bytes 86048 | tf_op jit(solution)/shard_map/ppermute | solution.py:687
  105.1 0.9 collective-permute-done.45
  106.1 0.6 pad_add_fusion.idx
  106.7 0.6 copy.74
  107.3 0.4 collective-permute-done.48.other
  107.8 0.7 copy-done.4
  108.5 2.5 %finish_sums.1 = (f32[49,128]{1,0:T(8,128)}, f32[128,512]{1,0:T(8,128)}, f32[512,128]{1,0:T(8,128)}, f32[3,512,128]{2,1,0:T(8,128)}) custom-call(s32[2]{0:T(128)} %pad_add_fusion.idx, bf16[4,336,128]{2,1,0:T(8,128)(2,1)} %copy-done.3, bf16[4,336,128]{2,1,0:T(8,128)(2,1)} %copy-done.4), custom_call_target="tpu_custom_call" | custom-call | tf_op jit(solution)/shard_map/finish_sums/pallas_call | solution.py:529
  (87 shorter events, 1.5 us)
Async XLA Ops:
  0.6 12.8 %copy-start.10 = (s32[128,32]{0,1:T(8,128)S(1)}, s32[128,32]{0,1:T(8,128)}, u32[]{:S(2)}) copy-start(s32[128,32]{0,1:T(8,128)} %param.30) | copy-start | bytes 49156
  0.6 19.9 %copy-start.11 = (bf16[16,4,128]{2,1,0:T(4,128)(2,1)S(1)}, bf16[16,4,128]{2,1,0:T(4,128)(2,1)}, u32[]{:S(2)}) copy-start(bf16[16,4,128]{2,1,0:T(4,128)(2,1)} %param.41) | copy-start | bytes 49156
  1.4 12.1 %collective-permute-start.32 = (bf16[3,32,128]{2,1,0:T(8,128)(2,1)S(1)}, bf16[3,32,128]{2,1,0:T(8,128)(2,1)S(1)}, u32[]{:S(2)}, u32[]{:S(2)}) collective-permute-start(bf16[3,32,128]{2,1,0:T(8,128)(2,1)S(1)} %get-tuple-element.156), channel_id=1, source_target_pairs={{0,8},{8,0},{16,24},{24,16},{1,9},{9,1},{17,25},{25,17},{2,10},{10... | collective-permute-start | bytes 73736 | tf_op jit(solution)/shard_map/ppermute | solution.py:603
  8.3 2.5 %collective-permute-start.8 = (bf16[3,32,128]{2,1,0:T(8,128)(2,1)S(1)}, bf16[3,32,128]{2,1,0:T(8,128)(2,1)}, u32[]{:S(2)}, u32[]{:S(2)}) collective-permute-start(bf16[3,32,128]{2,1,0:T(8,128)(2,1)S(1)} %get-tuple-element.72), channel_id=1, source_target_pairs={{8,16},{9,17},{10,18},{11,19},{12,20},{13,21},{14,22},{15,23},{16,... | collective-permute-start | bytes 73736 | tf_op jit(solution)/shard_map/cond/branch_4_fun/ppermute | solution.py:612
  9.5 1.3 %collective-permute-start.9 = (bf16[3,32,128]{2,1,0:T(8,128)(2,1)S(1)}, bf16[3,32,128]{2,1,0:T(8,128)(2,1)}, u32[]{:S(2)}, u32[]{:S(2)}) collective-permute-start(bf16[3,32,128]{2,1,0:T(8,128)(2,1)S(1)} %get-tuple-element.73), channel_id=1, source_target_pairs={{24,27},{25,26},{26,25},{27,24},{28,31},{29,30},{30,29},{31,28}} | collective-permute-start | bytes 73736 | tf_op jit(solution)/shard_map/cond/branch_4_fun/ppermute | solution.py:612
  14.3 10.5 %copy-start.5 = (bf16[3,32,128]{2,1,0:T(8,128)(2,1)}, bf16[3,32,128]{2,1,0:T(8,128)(2,1)S(1)}, u32[]{:S(2)}) copy-start(bf16[3,32,128]{2,1,0:T(8,128)(2,1)S(1)} %get-tuple-element.164.north) | copy-start | bytes 73732
  14.3 10.5 %copy-start.6 = (bf16[3,32,128]{2,1,0:T(8,128)(2,1)}, bf16[3,32,128]{2,1,0:T(8,128)(2,1)S(1)}, u32[]{:S(2)}) copy-start(bf16[3,32,128]{2,1,0:T(8,128)(2,1)S(1)} %get-tuple-element.165.south) | copy-start | bytes 73732
  14.5 8.4 %collective-permute-start.33 = (bf16[3,134,128]{2,1,0:T(8,128)(2,1)S(1)}, bf16[3,134,128]{2,1,0:T(8,128)(2,1)S(1)}, u32[]{:S(2)}, u32[]{:S(2)}) collective-permute-start(bf16[3,134,128]{2,1,0:T(8,128)(2,1)S(1)} %pad_maximum_fusion.1), channel_id=1, source_target_pairs={{0,1},{1,2},{2,3},{3,4},{4,5},{5,6},{6,7},{7,0},{8,9},{9,10},{10,1... | collective-permute-start | bytes 308744 | tf_op jit(solution)/shard_map/ppermute | solution.py:650
  17.2 6.0 %collective-permute-start.34 = (bf16[3,134,128]{2,1,0:T(8,128)(2,1)S(1)}, bf16[3,134,128]{2,1,0:T(8,128)(2,1)S(1)}, u32[]{:S(2)}, u32[]{:S(2)}) collective-permute-start(bf16[3,134,128]{2,1,0:T(8,128)(2,1)S(1)} %pad_maximum_fusion.2), channel_id=1, source_target_pairs={{0,7},{1,0},{2,1},{3,2},{4,3},{5,4},{6,5},{7,6},{8,15},{9,8},{10,9... | collective-permute-start | bytes 308744 | tf_op jit(solution)/shard_map/ppermute | solution.py:649
  22.9 1.9 %copy-start.7 = (bf16[3,134,128]{2,1,0:T(8,128)(2,1)}, bf16[3,134,128]{2,1,0:T(8,128)(2,1)S(1)}, u32[]{:S(2)}) copy-start(bf16[3,134,128]{2,1,0:T(8,128)(2,1)S(1)} %collective-permute-done.33.left) | copy-start | bytes 308740
  23.2 1.6 %copy-start.8 = (bf16[3,134,128]{2,1,0:T(8,128)(2,1)}, bf16[3,134,128]{2,1,0:T(8,128)(2,1)S(1)}, u32[]{:S(2)}) copy-start(bf16[3,134,128]{2,1,0:T(8,128)(2,1)S(1)} %collective-permute-done.34.right) | copy-start | bytes 308740
  57.6 23.0 %copy-start.9 = (bf16[384,128]{1,0:T(8,128)(2,1)S(1)}, bf16[384,128]{1,0:T(8,128)(2,1)}, u32[]{:S(2)}) copy-start(bf16[384,128]{1,0:T(8,128)(2,1)} %get-tuple-element.141) | copy-start | bytes 294916
  57.6 28.6 %copy-start = (bf16[4096,128]{1,0:T(8,128)(2,1)S(1)}, bf16[4096,128]{1,0:T(8,128)(2,1)}, u32[]{:S(2)}) copy-start(bf16[4096,128]{1,0:T(8,128)(2,1)} %get-tuple-element.135.g) | copy-start | bytes 3145732
  57.6 28.6 %copy-start.2 = (bf16[49,128]{1,0:T(8,128)(2,1)S(1)}, bf16[49,128]{1,0:T(8,128)(2,1)}, u32[]{:S(2)}) copy-start(bf16[49,128]{1,0:T(8,128)(2,1)} %dw.5) | copy-start | bytes 37636
  58.7 15.0 %collective-permute-start.35 = (bf16[1344,128]{1,0:T(8,128)(2,1)S(1)}, bf16[1344,128]{1,0:T(8,128)(2,1)S(1)}, u32[]{:S(2)}, u32[]{:S(2)}) collective-permute-start(bf16[1344,128]{1,0:T(8,128)(2,1)S(1)} %constant_dynamic-slice_fusion), channel_id=1, source_target_pairs={{0,8},{8,0},{16,24},{24,16},{1,9},{9,1},{17,25},{25,17},{2,10},{10... | collective-permute-start | bytes 1032200 | tf_op jit(solution)/shard_map/ppermute | solution.py:568
  61.5 2.5 %collective-permute-start.24 = (bf16[3,32,128]{2,1,0:T(8,128)(2,1)S(1)}, bf16[3,32,128]{2,1,0:T(8,128)(2,1)}, u32[]{:S(2)}, u32[]{:S(2)}) collective-permute-start(bf16[3,32,128]{2,1,0:T(8,128)(2,1)S(1)} %get-tuple-element.88), channel_id=1, source_target_pairs={{8,16},{9,17},{10,18},{11,19},{12,20},{13,21},{14,22},{15,23},{16,... | collective-permute-start | bytes 73736 | tf_op jit(solution)/shard_map/cond/branch_4_fun/ppermute | solution.py:612
  62.7 1.3 %collective-permute-start.25 = (bf16[3,32,128]{2,1,0:T(8,128)(2,1)S(1)}, bf16[3,32,128]{2,1,0:T(8,128)(2,1)}, u32[]{:S(2)}, u32[]{:S(2)}) collective-permute-start(bf16[3,32,128]{2,1,0:T(8,128)(2,1)S(1)} %get-tuple-element.89), channel_id=1, source_target_pairs={{24,27},{25,26},{26,25},{27,24},{28,31},{29,30},{30,29},{31,28}} | collective-permute-start | bytes 73736 | tf_op jit(solution)/shard_map/cond/branch_4_fun/ppermute | solution.py:612
  64.0 7.9 %collective-permute-start.36 = (bf16[3,32,128]{2,1,0:T(8,128)(2,1)S(1)}, bf16[3,32,128]{2,1,0:T(8,128)(2,1)S(1)}, u32[]{:S(2)}, u32[]{:S(2)}) collective-permute-start(bf16[3,32,128]{2,1,0:T(8,128)(2,1)S(1)} %get-tuple-element.163), channel_id=1, source_target_pairs={{0,8},{8,0},{16,24},{24,16},{1,9},{9,1},{17,25},{25,17},{2,10},{10... | collective-permute-start | bytes 73736 | tf_op jit(solution)/shard_map/ppermute | solution.py:603
  73.6 20.7 %collective-permute-start.43 = (bf16[402,128]{1,0:T(8,128)(2,1)S(1)}, bf16[402,128]{1,0:T(8,128)(2,1)S(1)}, u32[]{:S(2)}, u32[]{:S(2)}) collective-permute-start(bf16[402,128]{1,0:T(8,128)(2,1)S(1)} %pad_maximum_fusion.3), channel_id=1, source_target_pairs={{0,1},{1,2},{2,3},{3,4},{4,5},{5,6},{6,7},{7,0},{8,9},{9,10},{10,1... | collective-permute-start | bytes 308744 | tf_op jit(solution)/shard_map/ppermute | solution.py:676
  73.7 12.5 %copy-start.1 = (bf16[4096,128]{1,0:T(8,128)(2,1)S(1)}, bf16[4096,128]{1,0:T(8,128)(2,1)}, u32[]{:S(2)}) copy-start(bf16[4096,128]{1,0:T(8,128)(2,1)} %get-tuple-element.136.dirin) | copy-start | bytes 3145732
  74.9 14.8 %collective-permute-start.39 = (bf16[336,128]{1,0:T(8,128)(2,1)S(1)}, bf16[336,128]{1,0:T(8,128)(2,1)S(1)}, u32[]{:S(2)}, u32[]{:S(2)}) collective-permute-start(bf16[336,128]{1,0:T(8,128)(2,1)S(1)} %get-tuple-element.158), channel_id=1, source_target_pairs={{0,17},{1,16},{2,19},{3,18},{4,21},{5,20},{6,23},{7,22},{8,25},{9,... | collective-permute-start | bytes 258056 | tf_op jit(solution)/shard_map/ppermute | solution.py:576
  78.8 10.8 %collective-permute-start.38 = (bf16[336,128]{1,0:T(8,128)(2,1)S(1)}, bf16[336,128]{1,0:T(8,128)(2,1)S(1)}, u32[]{:S(2)}, u32[]{:S(2)}) collective-permute-start(bf16[336,128]{1,0:T(8,128)(2,1)S(1)} %get-tuple-element.159), channel_id=1, source_target_pairs={{0,16},{1,17},{2,18},{3,19},{4,20},{5,21},{6,22},{7,23},{8,24},{9,... | collective-permute-start | bytes 258056 | tf_op jit(solution)/shard_map/ppermute | solution.py:576
  79.2 10.5 %collective-permute-start.37 = (bf16[336,128]{1,0:T(8,128)(2,1)S(1)}, bf16[336,128]{1,0:T(8,128)(2,1)S(1)}, u32[]{:S(2)}, u32[]{:S(2)}) collective-permute-start(bf16[336,128]{1,0:T(8,128)(2,1)S(1)} %get-tuple-element.157), channel_id=1, source_target_pairs={{0,1},{1,0},{2,3},{3,2},{4,5},{5,4},{6,7},{7,6},{8,9},{9,8},{10,11... | collective-permute-start | bytes 258056 | tf_op jit(solution)/shard_map/ppermute | solution.py:576
  81.2 13.0 %collective-permute-start.44 = (bf16[402,128]{1,0:T(8,128)(2,1)}, bf16[402,128]{1,0:T(8,128)(2,1)S(1)}, u32[]{:S(2)}, u32[]{:S(2)}) collective-permute-start(bf16[402,128]{1,0:T(8,128)(2,1)} %pad_maximum_fusion.4), channel_id=1, source_target_pairs={{0,7},{1,0},{2,1},{3,2},{4,3},{5,4},{6,5},{7,6},{8,15},{9,8},{10,9... | collective-permute-start | bytes 308744 | tf_op jit(solution)/shard_map/ppermute | solution.py:675
  89.8 8.2 %collective-permute-start.42 = (bf16[336,128]{1,0:T(8,128)(2,1)S(1)}, bf16[336,128]{1,0:T(8,128)(2,1)S(1)}, u32[]{:S(2)}, u32[]{:S(2)}) collective-permute-start(bf16[336,128]{1,0:T(8,128)(2,1)S(1)} %fusion.1), channel_id=1, source_target_pairs={{0,6},{1,7},{2,4},{3,5},{4,2},{5,3},{6,0},{7,1},{8,14},{9,15},{10,... | collective-permute-start | bytes 258056 | tf_op jit(solution)/shard_map/ppermute | solution.py:585
  91.6 7.4 %collective-permute-start.41 = (bf16[336,128]{1,0:T(8,128)(2,1)S(1)}, bf16[336,128]{1,0:T(8,128)(2,1)S(1)}, u32[]{:S(2)}, u32[]{:S(2)}) collective-permute-start(bf16[336,128]{1,0:T(8,128)(2,1)S(1)} %fusion.1), channel_id=1, source_target_pairs={{0,4},{1,5},{2,6},{3,7},{4,0},{5,1},{6,2},{7,3},{8,12},{9,13},{10,... | collective-permute-start | bytes 258056 | tf_op jit(solution)/shard_map/ppermute | solution.py:585
  91.6 7.4 %collective-permute-start.40 = (bf16[336,128]{1,0:T(8,128)(2,1)S(1)}, bf16[336,128]{1,0:T(8,128)(2,1)S(1)}, u32[]{:S(2)}, u32[]{:S(2)}) collective-permute-start(bf16[336,128]{1,0:T(8,128)(2,1)S(1)} %fusion.1), channel_id=1, source_target_pairs={{0,2},{1,3},{2,0},{3,1},{4,6},{5,7},{6,4},{7,5},{8,10},{9,11},{10,... | collective-permute-start | bytes 258056 | tf_op jit(solution)/shard_map/ppermute | solution.py:585
  94.2 12.5 %copy-start.12 = (bf16[64,128]{1,0:T(8,128)(2,1)S(1)}, bf16[64,128]{1,0:T(8,128)(2,1)}, u32[]{:S(2)}) copy-start(bf16[64,128]{1,0:T(8,128)(2,1)} %get-tuple-element.127) | copy-start | bytes 49156
  99.0 6.1 %collective-permute-start.47 = (bf16[336,128]{1,0:T(8,128)(2,1)S(1)}, bf16[336,128]{1,0:T(8,128)(2,1)S(1)}, u32[]{:S(2)}, u32[]{:S(2)}) collective-permute-start(bf16[336,128]{1,0:T(8,128)(2,1)S(1)} %add_convert_fusion.1), channel_id=1, source_target_pairs={{0,17},{1,16},{2,19},{3,18},{4,21},{5,20},{6,23},{7,22},{8,25},{9,... | collective-permute-start | bytes 258056 | tf_op jit(solution)/shard_map/ppermute | solution.py:687
  100.5 4.6 %collective-permute-start.46 = (bf16[336,128]{1,0:T(8,128)(2,1)S(1)}, bf16[336,128]{1,0:T(8,128)(2,1)S(1)}, u32[]{:S(2)}, u32[]{:S(2)}) collective-permute-start(bf16[336,128]{1,0:T(8,128)(2,1)S(1)} %add_convert_fusion.1), channel_id=1, source_target_pairs={{0,16},{1,17},{2,18},{3,19},{4,20},{5,21},{6,22},{7,23},{8,24},{9,... | collective-permute-start | bytes 258056 | tf_op jit(solution)/shard_map/ppermute | solution.py:687
  100.8 5.2 %collective-permute-start.45 = (bf16[336,128]{1,0:T(8,128)(2,1)S(1)}, bf16[336,128]{1,0:T(8,128)(2,1)S(1)}, u32[]{:S(2)}, u32[]{:S(2)}) collective-permute-start(bf16[336,128]{1,0:T(8,128)(2,1)S(1)} %add_convert_fusion.1), channel_id=1, source_target_pairs={{0,1},{1,0},{2,3},{3,2},{4,5},{5,4},{6,7},{7,6},{8,9},{9,8},{10,11... | collective-permute-start | bytes 258056 | tf_op jit(solution)/shard_map/ppermute | solution.py:687
  106.0 1.7 %copy-start.3 = (bf16[4,336,128]{2,1,0:T(8,128)(2,1)}, bf16[4,336,128]{2,1,0:T(8,128)(2,1)S(1)}, u32[]{:S(2)}) copy-start(bf16[4,336,128]{2,1,0:T(8,128)(2,1)S(1)} %pad_maximum_fusion.mine) | copy-start | bytes 1032196
  106.0 1.7 %collective-permute-start.48 = (bf16[4,336,128]{2,1,0:T(8,128)(2,1)S(1)}, bf16[4,336,128]{2,1,0:T(8,128)(2,1)S(1)}, u32[]{:S(2)}, u32[]{:S(2)}) collective-permute-start(bf16[4,336,128]{2,1,0:T(8,128)(2,1)S(1)} %pad_maximum_fusion.mine), channel_id=1, source_target_pairs={{0,8},{8,0},{16,24},{24,16},{1,9},{9,1},{17,25},{25,17},{2,10},{10... | collective-permute-start | bytes 1032200 | tf_op jit(solution)/shard_map/ppermute | solution.py:688
  107.8 0.7 copy-start.4

commit v2 on v1

--- a/solution.py
+++ b/solution.py
@@ -13,6 +13,7 @@
 f32, bf16 = jnp.float32, jnp.bfloat16
 S = 16
 LOG2E = 1.4426950408889634
+HALF = 1344
 VMEM = pl.BlockSpec(memory_space=pltpu.VMEM)
 SMEM = pl.BlockSpec(memory_space=pltpu.SMEM)
 PARAMS = pltpu.CompilerParams(vmem_limit_bytes=60 * 2**20)
@@ -87,9 +88,9 @@
 
 def block_body(
     R, CW,
-    field, south, north, left, right, landb, dw, gain, up, down, scale, sgain, sw, sbias, cot,
-    bott, gout, dirout, first, last, lcol, rcol, sums,
-    x2d, el, w49, dep, hat, rst, nrm, act, slp, shat, srst, p1, back, tacc, downs, ups, mgs,
+    field, south, north, left, right, land, dw, gain, upw, bias, down, scale, sgain, sw, sbias, cot,
+    bott, gout, dirout, send, last, lcol, rcol, keep, away,
+    x2d, el, w49, dep, hat, rst, nrm, act, slp, shat, srst, p1, back, tacc, downs, ups, mgs, landb, up, sums,
 ):
     I = R // S
     CE = CW + 6
@@ -117,6 +118,23 @@
 
     lax.fori_loop(0, I + 6, tr, 0)
     weights_table(dw, w49, False)
+    p_at = lax.broadcasted_iota(jnp.int32, (R, R), 0)
+    p_row = lax.broadcasted_iota(jnp.int32, (R, R), 1)
+    order = (p_row == (p_at % S) * I + p_at // S).astype(f32).astype(bf16)
+    land_p = dot_r(order, land[...].astype(f32).astype(bf16)).astype(bf16)
+    spread = (
+        lax.broadcasted_iota(jnp.int32, (CW, CW * 128), 1) // 128
+        == lax.broadcasted_iota(jnp.int32, (CW, CW * 128), 0)
+    )
+    land_w = dot(land_p, spread.astype(f32).astype(bf16)).astype(bf16)
+    for i in range(I):
+        for c in range(CW):
+            at = (i * CW + c) * S
+            landb[at : at + S, :] = land_w[i * S : (i + 1) * S, c * 128 : (c + 1) * 128]
+    up[0:128, :] = upw[...]
+    up[128:256, :] = jnp.where(
+        lax.broadcasted_iota(jnp.int32, (128, 512), 0) == 0, bias[...].astype(f32).reshape(1, 512), 0.0
+    ).astype(bf16)
 
     def emit(i, c, v):
         dep[pl.ds((i * CW + c) * S, S), :] = v
@@ -124,8 +142,8 @@
     conv49(el, w49, emit, I, CW)
 
     jj, j1, pm = ones_mean(256), ones_mean(128), pair_mean()
-    g_n = gain[...].astype(f32)
-    sc = scale[...].astype(f32)
+    g_n = gain[...].astype(f32).reshape(1, 128)
+    sc = scale[...].astype(f32).reshape(1, 128)
     sg0 = sgain[0:1, :].astype(f32)
     T1 = 1024
 
@@ -207,8 +225,13 @@
     h2, r2, sn2 = sect_norm(l2, 2)
     P3 = to_patches(sn2, I // 4, CW // 4)
     l3 = (dot(P3, sw[2]) + sbias[2:3, :].astype(f32)).astype(bf16)
-    bott[...] = l3
-    b3 = cot[...]
+    Q = CW // 8
+    for c in range(Q):
+        x2d[pl.ds(c, S, stride=Q), :] = l3[c * S : (c + 1) * S, :].astype(f32)
+    for r in range(S):
+        bott[r] = x2d[r * Q : (r + 1) * Q, :].astype(bf16)
+        x2d[128 + r * Q : 128 + (r + 1) * Q, :] = cot[r].astype(f32)
+    b3 = jnp.concatenate([x2d[pl.ds(128 + c, S, stride=Q), :] for c in range(Q)], axis=0).astype(bf16)
     put(1024, dot_t(b3, P3), 4)
     u2 = from_patches(dot_r(b3, sw[2]), I // 4, CW // 4) * sgain[2:3, :].astype(f32)
     b2 = norm_bwd(u2, h2, r2, pm).astype(bf16)
@@ -287,29 +310,36 @@
     sums[2560:2624, :] = ts.astype(bf16)
     sums[2624:2688, :] = jnp.zeros((64, 128), bf16)
 
+    odd = lax.axis_index("lat") % 2
+    keep[...] = sums[pl.ds(pl.multiple_of(odd * HALF, 64), HALF), :]
+    away[0:HALF, :] = sums[pl.ds(pl.multiple_of((1 - odd) * HALF, 64), HALF), :]
     x2d[0:n0, :] = gout[...].astype(f32)
     for k in range(3):
-        first[k] = x2d[pl.ds(k * CW * S, CW, stride=S), :].astype(bf16)
-        last[k] = x2d[pl.ds((I - 3 + k) * CW * S + S - 1, CW, stride=S), :].astype(bf16)
+        lo = x2d[pl.ds(k * CW * S, CW, stride=S), :].astype(bf16)
+        hi = x2d[pl.ds((I - 3 + k) * CW * S + S - 1, CW, stride=S), :].astype(bf16)
+        last[k] = hi
+        send[k] = jnp.where(odd == 1, hi, lo)
+        away[HALF + k * CW : HALF + (k + 1) * CW, :] = jnp.where(odd == 1, lo, hi)
     for i in range(I):
         lcol[i * 3 * S : (i + 1) * 3 * S, :] = gout[i * CW * S : (i * CW + 3) * S, :]
         rcol[i * 3 * S : (i + 1) * 3 * S, :] = gout[((i + 1) * CW - 3) * S : (i + 1) * CW * S, :]
 
 
-def block_pass(field, south, north, left, right, landb, dw, gain, upx, down, scale, sgain, sw, sbias, cot):
+def block_pass(field, south, north, left, right, land, dw, gain, upw, bias, down, scale, sgain, sw, sbias, cot):
     R, CW, C = field.shape
     n = R * CW
     I = R // S
     sd = jax.ShapeDtypeStruct
     out_shape = (
-        sd((n // 64, C), bf16),
+        sd((S, CW // 8, C), bf16),
         sd((n, C), bf16),
         sd((n, C), bf16),
         sd((3, CW, C), bf16),
         sd((3, CW, C), bf16),
         sd((I * 3 * S, C), bf16),
         sd((I * 3 * S, C), bf16),
-        sd((2688, C), bf16),
+        sd((HALF, C), bf16),
+        sd((HALF + 3 * CW, C), bf16),
     )
     V = pltpu.VMEM
     scratch = [
@@ -330,16 +360,19 @@
         V((C, 512), f32),
         V((C, 512), f32),
         V((n, C), bf16),
+        V((n, C), bf16),
+        V((256, 512), bf16),
+        V((2 * HALF, C), bf16),
     ]
     return pl.pallas_call(
         functools.partial(block_body, R, CW),
         out_shape=out_shape,
-        in_specs=[VMEM] * 15,
-        out_specs=[VMEM] * 8,
+        in_specs=[VMEM] * 16,
+        out_specs=[VMEM] * 9,
         scratch_shapes=scratch,
         compiler_params=PARAMS,
         name="block_pass",
-    )(field, south, north, left, right, landb, dw, gain, upx, down, scale, sgain, sw, sbias, cot)
+    )(field, south, north, left, right, land, dw, gain, upw, bias, down, scale, sgain, sw, sbias, cot)
 
 
 def conv_back_body(R, CW, g, dirin, dw, out, gx, gext, w49):
@@ -393,10 +426,10 @@
     )(g, dirin, dw)
 
 
-def edges_body(R, CW, base, south, north, gl, gr, dw, flag, out, acc, rows, cols, w49):
+def edges_body(R, CW, base, south, north, gl, gr, dw, out, acc, rows, cols, w49):
     I = R // S
     CE = CW + 6
-    isn = flag[...].astype(f32)
+    isn = on_top().astype(f32)
     nots = 1.0 - isn
     core = I * 3 * S
     row = lax.broadcasted_iota(jnp.int32, (S, 128), 0)
@@ -480,13 +513,13 @@
         out[r] = v.astype(bf16)
 
 
-def edges(base, south, north, gl, gr, dw, flag, R, CW):
+def edges(base, south, north, gl, gr, dw, R, CW):
     C = base.shape[1]
     I = R // S
     return pl.pallas_call(
         functools.partial(edges_body, R, CW),
         out_shape=jax.ShapeDtypeStruct((R, CW, C), bf16),
-        in_specs=[VMEM] * 7,
+        in_specs=[VMEM] * 6,
         out_specs=VMEM,
         scratch_shapes=[
             pltpu.VMEM((R * CW, C), f32),
@@ -497,12 +530,12 @@
         compiler_params=SMALL,
         cost_estimate=pl.CostEstimate(flops=10**8, bytes_accessed=10 * 2**20, transcendentals=0),
         name="edges",
-    )(base, south, north, gl, gr, dw, flag)
-
-
-def finish_body(factor, chunk, idx, mine, other, o_depth, o_up, o_down, o_sec, full):
-    core = idx[0]
-    place = idx[1]
+    )(base, south, north, gl, gr, dw)
+
+
+def finish_body(factor, chunk, mine, other, o_depth, o_up, o_down, o_sec, full):
+    core = lax.axis_index("lat") % 2
+    place = (lax.axis_index("lat") // 2) * 2 + lax.axis_index("lon") % 2
     half = 4 * chunk
     for j in range(4):
         src = lax.bitwise_xor(place, j)
@@ -523,18 +556,18 @@
     o_depth[...] = block(20)[:49, :]
 
 
-def finish(idx, mine, other, factor):
+def finish(mine, other, factor):
     chunk = mine.shape[1]
     sd = jax.ShapeDtypeStruct
     return pl.pallas_call(
         functools.partial(finish_body, factor, chunk),
         out_shape=(sd((49, 128), f32), sd((128, 512), f32), sd((512, 128), f32), sd((3, 512, 128), f32)),
-        in_specs=[SMEM, VMEM, VMEM],
+        in_specs=[VMEM, VMEM],
         out_specs=[VMEM] * 4,
         scratch_shapes=[pltpu.VMEM((8 * chunk, 128), bf16)],
         compiler_params=PARAMS,
         name="finish_sums",
-    )(idx, mine, other)
+    )(mine, other)
 
 
 def add_bf(*vals):
@@ -559,13 +592,6 @@
 
 def square_pairs(k):
     return both_pairs((k // 2) * 2, k % 2)
-
-
-def sums_core(sums, core):
-    half = sums.shape[0] // 2
-    keep = lax.dynamic_slice_in_dim(sums, core * half, half, 0)
-    away = lax.dynamic_slice_in_dim(sums, (1 - core) * half, half, 0)
-    return add_bf(keep, lax.ppermute(away, "lat", flip_pairs("lat", 1))).reshape(4, half // 4, -1)
 
 
 def square_sum(held, place):
@@ -592,16 +618,100 @@
     return total
 
 
-def halo_rows(first, last, quot, rem):
+def on_top():
+    return lax.axis_index("lat") == lax.axis_size("lat") - 1
+
+
+def rim_body(R, CW, field, mirror, near, send, last, lc, rc, place, scr):
+    odd = lax.axis_index("lat") % 2
+    for k in range(3):
+        lo = field[k]
+        hi = field[R - 3 + k]
+        last[k] = hi
+        send[k] = jnp.where(odd == 1, hi, lo)
+        near[k] = jnp.where(odd == 1, lo, hi)
+    place[0] = mirror[0] // CW
+    place[1] = mirror[0] % CW
+    scr[0 : R * 8, :] = field[:, 0:8, :].astype(f32).reshape(R * 8, 128)
+    scr[R * 8 :, :] = field[:, CW - 8 : CW, :].astype(f32).reshape(R * 8, 128)
+    for k in range(3):
+        lc[k] = scr[pl.ds(k, R, stride=8), :].astype(bf16)
+        rc[k] = scr[pl.ds(R * 8 + 5 + k, R, stride=8), :].astype(bf16)
+
+
+def rim(field, mirror):
+    R, CW, C = field.shape
+    sd = jax.ShapeDtypeStruct
+    return pl.pallas_call(
+        functools.partial(rim_body, R, CW),
+        out_shape=(sd((3, CW, C), bf16),) * 3 + (sd((3, R, C), bf16),) * 2 + (sd((2,), jnp.int32),),
+        in_specs=[VMEM, SMEM],
+        out_specs=[VMEM] * 5 + [SMEM],
+        scratch_shapes=[pltpu.VMEM((2 * R * 8, C), f32)],
+        compiler_params=SMALL,
+        name="rim",
+    )(field, mirror)
+
+
+def join_body(CW, width, flip, place, near, far, blk_b, lc, rc, south, north, lp, rp, cat, scr):
+    odd = lax.axis_index("lat") % 2 == 1
+    top = on_top()
+    rem = place[1]
+    at = lax.broadcasted_iota(jnp.int32, (CW, CW), 0)
+    turn = (at + lax.broadcasted_iota(jnp.int32, (CW, CW), 1) == CW - 1).astype(f32).astype(bf16)
+    for k in range(3):
+        cat[0:CW, :] = blk_b[k].astype(f32)
+        cat[CW : 2 * CW, :] = far[k].astype(f32)
+        win = cat[pl.ds(rem + 1, CW), :].astype(bf16)
+        scr[k * CW : (k + 1) * CW, :] = dot(turn, win)
+    for k in range(3):
+        m = 2 - k if flip else k
+        beyond = scr[m * CW : (m + 1) * CW, :]
+        above = jnp.where(odd, far[k].astype(f32), near[k].astype(f32))
+        below = jnp.where(odd, near[k].astype(f32), far[k].astype(f32))
+        above = jnp.where(top, beyond, above)
+        south[k] = below.astype(bf16)
+        north[k] = above.astype(bf16)
+        scr[(3 + k) * CW : (4 + k) * CW, :] = below
+        scr[(6 + k) * CW : (7 + k) * CW, :] = above
+    for pay, core, lo in ((lp, lc, 0), (rp, rc, CW - 3)):
+        if flip:
+            for j in range(3):
+                for k in range(3):
+                    cat[k : k + 1, :] = scr[(3 + k) * CW + lo + j : (3 + k) * CW + lo + j + 1, :]
+                    cat[3 + width + k : 4 + width + k, :] = scr[(6 + k) * CW + lo + j : (6 + k) * CW + lo + j + 1, :]
+                cat[3 : 3 + width, :] = core[j].astype(f32)
+                pay[j] = cat[0 : width + 6, :].astype(bf16)
+        else:
+            pay[0:width, :] = core[...]
+            for side in range(2):
+                for k in range(3):
+                    src = (3 + 3 * side + k) * CW + lo
+                    cat[side * 9 + k * 3 : side * 9 + k * 3 + 3, :] = scr[src : src + 3, :]
+            pay[width : width + 32, :] = cat[0:32, :].astype(bf16)
+
+
+def join(place, near, far, blk_b, lc, rc, flip):
+    CW, C = near.shape[1:]
+    width = lc.shape[1] if flip else lc.shape[0]
+    sd = jax.ShapeDtypeStruct
+    pay = sd((3, width + 6, C) if flip else (width + 32, C), bf16)
+    return pl.pallas_call(
+        functools.partial(join_body, CW, width, flip),
+        out_shape=(sd((3, CW, C), bf16),) * 2 + (pay, pay),
+        in_specs=[SMEM] + [VMEM] * 5,
+        out_specs=[VMEM] * 4,
+        scratch_shapes=[pltpu.VMEM((max(2 * CW + 8, width + 8), C), f32), pltpu.VMEM((9 * CW, C), f32)],
+        compiler_params=SMALL,
+        name="join",
+    )(place, near, far, blk_b, lc, rc)
+
+
+def far_rows(send, last, quot):
     nl = lax.axis_size("lon")
     nt = lax.axis_size("lat")
-    lat = lax.axis_index("lat")
-    odd = lat % 2 == 1
-    cols = first.shape[1]
     top = (nt - 1) * nl
     axes = ("lat", "lon")
-    near = lax.ppermute(jnp.where(odd, first, last), "lat", flip_pairs("lat", 1))
-    send = jnp.where(odd, last, first)
     swap = [(a * nl + e, (a + 1) * nl + e) for a in range(1, nt - 1, 2) for e in range(nl)]
     swap += [(j, i) for i, j in swap]
 
@@ -613,11 +723,7 @@
 
         return run
 
-    far, blk_b = lax.switch(quot, [branch(q) for q in range(nl)], send, last)
-    south = jnp.where(odd, near, far)
-    both = jnp.concatenate([blk_b, far], axis=1)
-    window = lax.dynamic_slice_in_dim(both, rem + 1, cols, 1)
-    return south, jnp.where(odd, far, near), window[:, ::-1]
+    return lax.switch(quot, [branch(q) for q in range(nl)], send, last)
 
 
 def shift_pairs(axis, by):
@@ -630,64 +736,42 @@
     section_gain, section_weight, section_bias, cotangent,
 ):
     R, CW, C = field.shape
-    I = R // S
-    n = R * CW
     total = R * CW * lax.axis_size("lat") * lax.axis_size("lon")
     factor = 1.0 / math.sqrt(total / 64.0)
-    north = lax.axis_index("lat") == lax.axis_size("lat") - 1
-    quot = mirror[0] // CW
-    rem = mirror[0] % CW
-
-    south_f, above_f, fold_f = halo_rows(field[:3], field[R - 3 :], quot, rem)
-    north_f = jnp.where(north, fold_f[::-1], above_f)
-
-    def edge(lo):
-        return jnp.stack(
-            [jnp.concatenate([south_f[:, c], field[:, c], north_f[:, c]], axis=0) for c in range(lo, lo + 3)]
-        )
-
-    right_f = lax.ppermute(edge(0), "lon", shift_pairs("lon", -1))
-    left_f = lax.ppermute(edge(CW - 3), "lon", shift_pairs("lon", 1))
-
-    landb = jnp.broadcast_to(
-        land.astype(bf16).reshape(S, I, CW).transpose(1, 2, 0).reshape(n, 1), (n, C)
+    near, send, last, lc, rc, shift = rim(field, mirror)
+    near = lax.ppermute(near, "lat", flip_pairs("lat", 1))
+    far, blk_b = far_rows(send, last, shift[0])
+    south_f, north_f, lpay, rpay = join(shift, near, far, blk_b, lc, rc, True)
+    right_f = lax.ppermute(lpay, "lon", shift_pairs("lon", -1))
+    left_f = lax.ppermute(rpay, "lon", shift_pairs("lon", 1))
+    level, g, direct, send, last, lcol, rcol, keep, away = block_pass(
+        field, south_f, north_f, left_f, right_f, land.T, depth_weight, norm_gain, up_weight, up_bias, down_proj,
+        layer_scale, section_gain, section_weight, section_bias, cotangent,
     )
-    upx = jnp.concatenate([up_weight, up_bias[None, :], jnp.zeros((127, up_bias.shape[0]), bf16)], axis=0)
-    cot = cotangent.transpose(1, 0, 2).reshape(n // 64, C)
-    bott, g, direct, first, last, lcol, rcol, sums = block_pass(
-        field, south_f, north_f, left_f, right_f, landb, depth_weight, norm_gain[None, :], upx, down_proj,
-        layer_scale[None, :], section_gain, section_weight, section_bias, cot,
-    )
-    level = bott.reshape(CW // 8, S, C).transpose(1, 0, 2)
-
-    core = lax.axis_index("lat") % 2
+
     place = (lax.axis_index("lat") // 2) * 2 + lax.axis_index("lon") % 2
-    held = sums_core(sums, core)
-
-    south_g, above_g, fold_g = halo_rows(first, last, quot, rem)
-    north_g = jnp.where(north, fold_g, above_g)
-
-    def pack(cols, lo):
-        return jnp.concatenate(
-            [cols, south_g[:, lo : lo + 3].reshape(9, C), north_g[:, lo : lo + 3].reshape(9, C)], axis=0
-        )
-
-    gr = lax.ppermute(pack(lcol, 0), "lon", shift_pairs("lon", -1))
-    gl = lax.ppermute(pack(rcol, CW - 3), "lon", shift_pairs("lon", 1))
-    flag = jnp.broadcast_to(north.astype(bf16), (1, C))
-    held, south_g = lax.optimization_barrier((held, south_g))
+    got = lax.ppermute(away, "lat", flip_pairs("lat", 1))
+    near = got[HALF:].reshape(3, CW, C)
+    held = add_bf(keep, got[:HALF]).reshape(4, HALF // 4, C)
+    send, held = lax.optimization_barrier((send, held))
     chunk = square_sum(held, place)
+    far, blk_b = far_rows(send, last, shift[0])
+    chunk, far = lax.optimization_barrier((chunk, far))
+    south_g, north_g, lpay, rpay = join(shift, near, far, blk_b, lcol, rcol, False)
+    chunk, lpay = lax.optimization_barrier((chunk, lpay))
+    gr = lax.ppermute(lpay, "lon", shift_pairs("lon", -1))
+    gl = lax.ppermute(rpay, "lon", shift_pairs("lon", 1))
     g, _ = lax.optimization_barrier((g, south_g))
     base = conv_back(g, direct, depth_weight, R, CW)
+    chunk = line_sum(chunk)
     chunk, base = lax.optimization_barrier((chunk, base))
-    chunk = line_sum(chunk)
-    grad_field = edges(base, south_g, north_g, gl, gr, depth_weight, flag, R, CW)
-    chunk, grad_field = lax.optimization_barrier((chunk, grad_field))
+    grad_field = edges(base, south_g, north_g, gl, gr, depth_weight, R, CW)
     axes = ("lat", "lon")
-    mine = jnp.stack([chunk] + [lax.ppermute(chunk, axes, square_pairs(k)) for k in (1, 2, 3)])
+    back = [lax.ppermute(chunk, axes, square_pairs(k)) for k in (1, 2, 3)]
+    back[0], grad_field = lax.optimization_barrier((back[0], grad_field))
+    mine = jnp.stack([chunk] + back)
     other = lax.ppermute(mine, "lat", flip_pairs("lat", 1))
-    idx = jnp.stack([core, place]).astype(jnp.int32)
-    g_depth, g_up, g_down, g_sec = finish(idx, mine, other, factor)
+    g_depth, g_up, g_down, g_sec = finish(mine, other, factor)
     return level, grad_field, g_depth, g_up, g_down, g_sec
 
 

time: 112 us -> 98.2 us (0.88)
  other arithmetic: 9.87 us -> 1.22 us
  starting transfers between devices: 39 us -> 35.1 us
  local copies, waits for them, and re-layouts: 9.08 us -> 5.44 us
  Pallas kernels: 42.4 us -> 45.7 us
  between operations: 3.65 us -> 0.86 us
  waiting for transfers between devices: 6.92 us -> 8.68 us
    ppermute x10 -> x9, starting transfers between devices: 23.8 us -> 17.2 us  [the longest x1 4.41 us: on_device(): gr = lax.ppermute(lpay, 'lon', shift_pairs('lon', -1))]
    concatenate x5 -> x0, other arithmetic: 4.82 us -> none  [the longest x1 1.71 us: on_device(): jnp.concatenate([up_weight, up_bias[None, :], jnp.zeros((127, up_bias.sha...]
    unnamed x39 -> x26, local copies, waits for them, and re-layouts: 0.91 us -> 5.41 us
    slice x5 -> x1, local copies, waits for them, and re-layouts: 3.1 us -> 0.01 us  [on_device(): near = got[HALF:].reshape(3, CW, C)]
    pallas_call x0 -> x3, Pallas kernels: none -> 3.05 us  [the longest x2 1.89 us: join(): pl.pallas_call(functools.partial(join_body, CW, width, flip), out_shape=(...]
    ppermute x3, starting transfers between devices: 5.69 us -> 8.42 us  [square_sum(): came.append(lax.ppermute(part, ('lat', 'lon'), square_pairs(k)))]
    broadcast_in_dim x5 -> x0, local copies, waits for them, and re-layouts: 2.38 us -> none  [the longest x2 1.68 us: on_device(): jnp.broadcast_to(land.astype(bf16).reshape(S, I, CW).transpose(1, 2, 0).r...]
    select_n x3 -> x0, other arithmetic: 2.24 us -> none  [the longest x1 0.75 us: on_device(): north_f = jnp.where(north, fold_f[::-1], above_f)]
  transfers between devices with their start and end apart: 21 -> 20, of which waited for: 6 -> 6; matrix products, arithmetic and copies ran while one was open for 12% -> 0% of each run, Pallas kernels for 6% -> 7%
where the time goes in v2:
time: 98.2 us; the launch traced here: 97 us
  Pallas kernels  45.7 us (47%)
  starting transfers between devices  35.1 us (36%)
  waiting for transfers between devices  8.68 us (9%)
  local copies, waits for them, and re-layouts  5.44 us (6%)
  other arithmetic  1.22 us (1%)
    pallas_call x1, Pallas kernels, block_pass(): pl.pallas_call(functools.partial(block_body, R, CW), out_shape=out_shape,...  33 us
    ppermute x3, starting transfers between devices, square_sum(): came.append(lax.ppermute(part, ('lat', 'lon'), square_pairs(k)))  8.42 us
    unnamed x26, local copies, waits for them, and re-layouts  5.41 us
    ppermute x4, starting transfers between devices, run(): return (lax.ppermute(send, axes, swap + fa), lax.ppermute(last, axes, fb))  5.01 us
    ppermute x3, starting transfers between devices, line_sum(): lax.ppermute(total, 'lon', flip_pairs('lon', bit * k))  4.44 us
    ppermute x1, starting transfers between devices, on_device(): gr = lax.ppermute(lpay, 'lon', shift_pairs('lon', -1))  4.41 us
    ppermute x3, starting transfers between devices, on_device(): back = [lax.ppermute(chunk, axes, square_pairs(k)) for k in (1, 2, 3)]  4.35 us
    pallas_call x1, Pallas kernels, edges(): pl.pallas_call(functools.partial(edges_body, R, CW), out_shape=jax.ShapeD...  3.71 us
  transfers between devices with their start and end apart: 20, of which 6 were waited for; matrix products, arithmetic and copies ran while one was open for 0% of the time, Pallas kernels for 7%

profile of v2, /device:TPU:0, one launch (start us, length us, event | category | flops | bytes accessed | tf_op | source)
XLA Modules:
  0.0 97.0 jit_solution(9903940016476824847)
XLA Ops:
  0.6 0.0 copy-start
  0.6 1.2 %copy-done = bf16[128,32,128]{2,1,0:T(8,128)(2,1)S(1)} copy-done((bf16[128,32,128]{2,1,0:T(8,128)(2,1)S(1)}, bf16[128,32,128]{2,1,0:T(8,128)(2,1)}, u32[]{:S(2)}) %copy-start) | copy-done | bytes 1048600
  1.9 0.7 copy-done.8
  2.5 1.2 %rim.1 = (bf16[3,32,128]{2,1,0:T(8,128)(2,1)S(1)}, bf16[3,32,128]{2,1,0:T(8,128)(2,1)S(1)}, bf16[3,32,128]{2,1,0:T(8,128)(2,1)S(1)}, bf16[3,128,128]{2,1,0:T(8,1...) custom-call(bf16[128,32,128]{2,1,0:T(8,128)(2,1)S(1)} %copy-done, s32[256]{0:T(256)S(1)} %copy-done.8), custom_call_target="tpu_custom_call" | custom-call | tf_op jit(solution)/shard_map/rim/pallas_call | solution.py:645
  3.7 0.5 collective-permute-start.32
  4.3 2.5 %conditional.2 = (bf16[3,32,128]{2,1,0:T(8,128)(2,1)}, bf16[3,32,128]{2,1,0:T(8,128)(2,1)}) conditional(s32[]{:T(128)} %bitcast, (bf16[3,32,128]{2,1,0:T(8,128)(2,1)S(1)}, bf16[3,32,128]{2,1,0:T(8,128)(2,1)S(1)}) %tuple.78, (bf16[3,32,128]{2,1,0:T(8,128)(2,1)S(1)}, bf16[3,32,128]{2,1,0:T(8,128)(2,1)S(1)}) %tuple.78, ...), branch_computations={%region_0.0_spmd, %region_1.0_spmd, %region_2.0_spmd, %region_3.0_... | conditional | bytes 196704 | solution.py:726
  4.3 1.3 %collective-permute-start.10 = (bf16[3,32,128]{2,1,0:T(8,128)(2,1)S(1)}, bf16[3,32,128]{2,1,0:T(8,128)(2,1)}, u32[]{:S(2)}, u32[]{:S(2)}) collective-permute-start(bf16[3,32,128]{2,1,0:T(8,128)(2,1)S(1)} %get-tuple-element.74), channel_id=1, source_target_pairs={{8,16},{9,17},{10,18},{11,19},{12,20},{13,21},{14,22},{15,23},{16,... | collective-permute-start | bytes 73736 | tf_op jit(solution)/shard_map/cond/branch_5_fun/ppermute | solution.py:722
  5.6 1.2 %collective-permute-start.11 = (bf16[3,32,128]{2,1,0:T(8,128)(2,1)S(1)}, bf16[3,32,128]{2,1,0:T(8,128)(2,1)}, u32[]{:S(2)}, u32[]{:S(2)}) collective-permute-start(bf16[3,32,128]{2,1,0:T(8,128)(2,1)S(1)} %get-tuple-element.75), channel_id=1, source_target_pairs={{24,28},{25,27},{26,26},{27,25},{28,24},{29,31},{30,30},{31,29}} | collective-permute-start | bytes 73736 | tf_op jit(solution)/shard_map/cond/branch_5_fun/ppermute | solution.py:722
  6.8 0.0 collective-permute-done.10
  6.8 0.0 collective-permute-done.11
  6.8 0.0 collective-permute-done.32.near
  6.8 1.0 join.2
  7.8 0.0 copy-start.6
  7.8 0.6 copy-done.6
  8.4 0.6 copy-done.7
  9.0 2.5 %collective-permute-start.33 = (bf16[3,134,128]{2,1,0:T(8,128)(2,1)S(1)}, bf16[3,134,128]{2,1,0:T(8,128)(2,1)S(1)}, u32[]{:S(2)}, u32[]{:S(2)}) collective-permute-start(bf16[3,134,128]{2,1,0:T(8,128)(2,1)S(1)} %get-tuple-element.154), channel_id=1, source_target_pairs={{0,1},{1,2},{2,3},{3,4},{4,5},{5,6},{6,7},{7,0},{8,9},{9,10},{10,1... | collective-permute-start | bytes 308744 | tf_op jit(solution)/shard_map/ppermute | solution.py:746
  11.5 3.0 %collective-permute-start.34 = (bf16[3,134,128]{2,1,0:T(8,128)(2,1)S(1)}, bf16[3,134,128]{2,1,0:T(8,128)(2,1)S(1)}, u32[]{:S(2)}, u32[]{:S(2)}) collective-permute-start(bf16[3,134,128]{2,1,0:T(8,128)(2,1)S(1)} %get-tuple-element.155), channel_id=1, source_target_pairs={{0,7},{1,0},{2,1},{3,2},{4,3},{5,4},{6,5},{7,6},{8,15},{9,8},{10,9... | collective-permute-start | bytes 308744 | tf_op jit(solution)/shard_map/ppermute | solution.py:745
  14.6 2.8 %collective-permute-done.33.left = bf16[3,134,128]{2,1,0:T(8,128)(2,1)S(1)} collective-permute-done((bf16[3,134,128]{2,1,0:T(8,128)(2,1)S(1)}, bf16[3,134,128]{2,1,0:T(8,128)(2,1)S(1)}, u32[]{:S(2)}, u32[]{:S(2)}) %collective-permute-start.33) | collective-permute-done | bytes 102944 | tf_op jit(solution)/shard_map/ppermute | solution.py:746
  17.3 0.0 collective-permute-done.34.right
  17.3 0.6 copy-done.11
  18.0 0.0 copy-done.12
  18.0 33.0 %block_pass.1 = (bf16[16,4,128]{2,1,0:T(4,128)(2,1)}, bf16[4096,128]{1,0:T(8,128)(2,1)}, bf16[4096,128]{1,0:T(8,128)(2,1)}, bf16[3,32,128]{2,1,0:T(8,128)(2,1)S(...) custom-call(bf16[128,32,128]{2,1,0:T(8,128)(2,1)} %field.3, ...), custom_call_target="tpu_custom_call" | custom-call | tf_op jit(solution)/shard_map/block_pass/pallas_call | solution.py:367
  51.0 0.0 copy-start.1
  51.0 2.3 %collective-permute-start.35 = (bf16[1440,128]{1,0:T(8,128)(2,1)}, bf16[1440,128]{1,0:T(8,128)(2,1)S(1)}, u32[]{:S(2)}, u32[]{:S(2)}) collective-permute-start(bf16[1440,128]{1,0:T(8,128)(2,1)} %get-tuple-element.159), channel_id=1, source_target_pairs={{0,8},{8,0},{16,24},{24,16},{1,9},{9,1},{17,25},{25,17},{2,10},{10... | collective-permute-start | bytes 1105928 | tf_op jit(solution)/shard_map/ppermute | solution.py:753
  53.3 1.5 %collective-permute-done.35 = bf16[1440,128]{1,0:T(8,128)(2,1)S(1)} collective-permute-done((bf16[1440,128]{1,0:T(8,128)(2,1)}, bf16[1440,128]{1,0:T(8,128)(2,1)S(1)}, u32[]{:S(2)}, u32[]{:S(2)}) %collective-permute-start.35) | collective-permute-done | bytes 368672 | tf_op jit(solution)/shard_map/ppermute | solution.py:753
  54.9 1.1 %add_convert_fusion = bf16[1344,128]{1,0:T(8,128)(2,1)S(1)} fusion(bf16[1344,128]{1,0:T(8,128)(2,1)} %get-tuple-element.158, bf16[1440,128]{1,0:T(8,128)(2,1)S(1)} %collective-permute-done.35), kind=kLoop, calls=%fused_computation | loop fusion | flops 688128 | bytes 1032192 | tf_op jit(solution)/shard_map/convert_element_type | solution.py:577
  56.0 1.0 %collective-permute-start.36 = (bf16[336,128]{1,0:T(8,128)(2,1)S(1)}, bf16[336,128]{1,0:T(8,128)(2,1)S(1)}, u32[]{:S(2)}, u32[]{:S(2)}) collective-permute-start(bf16[336,128]{1,0:T(8,128)(2,1)S(1)} %get-tuple-element.186), channel_id=1, source_target_pairs={{0,1},{1,0},{2,3},{3,2},{4,5},{5,4},{6,7},{7,6},{8,9},{9,8},{10,11... | collective-permute-start | bytes 258056 | tf_op jit(solution)/shard_map/ppermute | solution.py:602
  57.0 7.4 %collective-permute-start.38 = (bf16[336,128]{1,0:T(8,128)(2,1)S(1)}, bf16[336,128]{1,0:T(8,128)(2,1)S(1)}, u32[]{:S(2)}, u32[]{:S(2)}) collective-permute-start(bf16[336,128]{1,0:T(8,128)(2,1)S(1)} %get-tuple-element.187), channel_id=1, source_target_pairs={{0,17},{1,16},{2,19},{3,18},{4,21},{5,20},{6,23},{7,22},{8,25},{9,... | collective-permute-start | bytes 258056 | tf_op jit(solution)/shard_map/ppermute | solution.py:602
  64.4 2.5 %conditional.3 = (bf16[3,32,128]{2,1,0:T(8,128)(2,1)}, bf16[3,32,128]{2,1,0:T(8,128)(2,1)}) conditional(s32[]{:T(128)} %bitcast, (bf16[3,32,128]{2,1,0:T(8,128)(2,1)S(1)}, bf16[3,32,128]{2,1,0:T(8,128)(2,1)S(1)}) %tuple.80, (bf16[3,32,128]{2,1,0:T(8,128)(2,1)S(1)}, bf16[3,32,128]{2,1,0:T(8,128)(2,1)S(1)}) %tuple.80, ...), branch_computations={%region_8.9_spmd, %region_9.10_spmd, %region_10.11_spmd, %region_1... | conditional | bytes 196704 | solution.py:726
  64.4 1.2 %collective-permute-start.26 = (bf16[3,32,128]{2,1,0:T(8,128)(2,1)S(1)}, bf16[3,32,128]{2,1,0:T(8,128)(2,1)}, u32[]{:S(2)}, u32[]{:S(2)}) collective-permute-start(bf16[3,32,128]{2,1,0:T(8,128)(2,1)S(1)} %get-tuple-element.90), channel_id=1, source_target_pairs={{8,16},{9,17},{10,18},{11,19},{12,20},{13,21},{14,22},{15,23},{16,... | collective-permute-start | bytes 73736 | tf_op jit(solution)/shard_map/cond/branch_5_fun/ppermute | solution.py:722
  65.7 1.2 %collective-permute-start.27 = (bf16[3,32,128]{2,1,0:T(8,128)(2,1)S(1)}, bf16[3,32,128]{2,1,0:T(8,128)(2,1)}, u32[]{:S(2)}, u32[]{:S(2)}) collective-permute-start(bf16[3,32,128]{2,1,0:T(8,128)(2,1)S(1)} %get-tuple-element.91), channel_id=1, source_target_pairs={{24,28},{25,27},{26,26},{27,25},{28,24},{29,31},{30,30},{31,29}} | collective-permute-start | bytes 73736 | tf_op jit(solution)/shard_map/cond/branch_5_fun/ppermute | solution.py:722
  66.9 0.8 collective-permute-done.38
  67.7 1.2 %collective-permute-done.37 = bf16[336,128]{1,0:T(8,128)(2,1)S(1)} collective-permute-done((bf16[336,128]{1,0:T(8,128)(2,1)S(1)}, bf16[336,128]{1,0:T(8,128)(2,1)S(1)}, u32[]{:S(2)}, u32[]{:S(2)}) %collective-permute-start.37) | collective-permute-done | bytes 86048 | tf_op jit(solution)/shard_map/ppermute | solution.py:602
  69.0 0.9 copy-done.5
  69.8 0.9 join.3
  70.8 3.7 %collective-permute-start.41 = (bf16[336,128]{1,0:T(8,128)(2,1)S(1)}, bf16[336,128]{1,0:T(8,128)(2,1)S(1)}, u32[]{:S(2)}, u32[]{:S(2)}) collective-permute-start(bf16[336,128]{1,0:T(8,128)(2,1)S(1)} %fusion.1), channel_id=1, source_target_pairs={{0,6},{1,7},{2,4},{3,5},{4,2},{5,3},{6,0},{7,1},{8,14},{9,15},{10,... | collective-permute-start | bytes 258056 | tf_op jit(solution)/shard_map/ppermute | solution.py:611
  74.5 0.8 collective-permute-start.39
  75.2 4.4 %collective-permute-start.44 = (bf16[416,128]{1,0:T(8,128)(2,1)S(1)}, bf16[416,128]{1,0:T(8,128)(2,1)S(1)}, u32[]{:S(2)}, u32[]{:S(2)}) collective-permute-start(bf16[416,128]{1,0:T(8,128)(2,1)S(1)} %get-tuple-element.179), channel_id=1, source_target_pairs={{0,7},{1,0},{2,1},{3,2},{4,3},{5,4},{6,5},{7,6},{8,15},{9,8},{10,9... | collective-permute-start | bytes 319496 | tf_op jit(solution)/shard_map/ppermute | solution.py:762
  79.7 3.5 %conv_back.1.base = f32[4096,128]{1,0:T(8,128)S(1)} custom-call(bf16[4096,128]{1,0:T(8,128)(2,1)S(1)} %copy-done.1, bf16[4096,128]{1,0:T(8,128)(2,1)S(1)} %copy-done.2, bf16[49,128]{1,0:T(8,128)(2,1)S(1)} %copy-done.3), custom_call_target="tpu_custom_call" | custom-call | flops 100000000 | bytes 31457280 | tf_op jit(solution)/shard_map/conv_back/pallas_call | solution.py:413
  83.1 0.1 add_convert_fusion.1
  83.2 0.1 collective-permute-start.42
  83.3 4.3 %collective-permute-start.46 = (bf16[336,128]{1,0:T(8,128)(2,1)S(1)}, bf16[336,128]{1,0:T(8,128)(2,1)S(1)}, u32[]{:S(2)}, u32[]{:S(2)}) collective-permute-start(bf16[336,128]{1,0:T(8,128)(2,1)S(1)} %add_convert_fusion.1), channel_id=1, source_target_pairs={{0,17},{1,16},{2,19},{3,18},{4,21},{5,20},{6,23},{7,22},{8,25},{9,... | collective-permute-start | bytes 258056 | tf_op jit(solution)/shard_map/ppermute | solution.py:770
  87.6 3.7 %edges.1 = bf16[128,32,128]{2,1,0:T(8,128)(2,1)} custom-call(f32[4096,128]{1,0:T(8,128)S(1)} %conv_back.1.base, bf16[3,32,128]{2,1,0:T(8,128)(2,1)S(1)} %get-tuple-element.172.south, bf16[3,32,128]{2,1,0:T(8,128)(2,1)S(1)} %get-tuple-element.177.north, bf16[416,128]{1,0:T(8,128)(2,1)S(1)} %collective-permute-done.43.gl, ...), custom_call_target="tpu_custom_call" | custom-call | flops 100000000 | bytes 10485760 | tf_op jit(solution)/shard_map/edges/pallas_call | solution.py:519
  91.3 0.8 collective-permute-done.45
  92.1 0.1 collective-permute-start.47
  92.2 1.6 %collective-permute-done.47.other = bf16[4,336,128]{2,1,0:T(8,128)(2,1)S(1)} collective-permute-done((bf16[4,336,128]{2,1,0:T(8,128)(2,1)S(1)}, bf16[4,336,128]{2,1,0:T(8,128)(2,1)S(1)}, u32[]{:S(2)}, u32[]{:S(2)}) %collective-permute-start.47) | collective-permute-done | bytes 344096 | tf_op jit(solution)/shard_map/ppermute | solution.py:773
  93.8 0.7 copy-done.10
  94.6 2.4 %finish_sums.1 = (f32[49,128]{1,0:T(8,128)}, f32[128,512]{1,0:T(8,128)}, f32[512,128]{1,0:T(8,128)}, f32[3,512,128]{2,1,0:T(8,128)}) custom-call(bf16[4,336,128]{2,1,0:T(8,128)(2,1)} %copy-done.9, bf16[4,336,128]{2,1,0:T(8,128)(2,1)} %copy-done.10), custom_call_target="tpu_custom_call" | custom-call | tf_op jit(solution)/shard_map/finish_sums/pallas_call | solution.py:562
  (33 shorter events, 0.2 us)
Async XLA Ops:
  0.6 1.2 %copy-start = (bf16[128,32,128]{2,1,0:T(8,128)(2,1)S(1)}, bf16[128,32,128]{2,1,0:T(8,128)(2,1)}, u32[]{:S(2)}) copy-start(bf16[128,32,128]{2,1,0:T(8,128)(2,1)} %field.3) | copy-start | bytes 3145732
  1.9 0.7 copy-start.8
  3.7 3.1 %collective-permute-start.32 = (bf16[3,32,128]{2,1,0:T(8,128)(2,1)S(1)}, bf16[3,32,128]{2,1,0:T(8,128)(2,1)S(1)}, u32[]{:S(2)}, u32[]{:S(2)}) collective-permute-start(bf16[3,32,128]{2,1,0:T(8,128)(2,1)S(1)} %get-tuple-element.145), channel_id=1, source_target_pairs={{0,8},{8,0},{16,24},{24,16},{1,9},{9,1},{17,25},{25,17},{2,10},{10... | collective-permute-start | bytes 73736 | tf_op jit(solution)/shard_map/ppermute | solution.py:742
  4.3 2.5 %collective-permute-start.10 = (bf16[3,32,128]{2,1,0:T(8,128)(2,1)S(1)}, bf16[3,32,128]{2,1,0:T(8,128)(2,1)}, u32[]{:S(2)}, u32[]{:S(2)}) collective-permute-start(bf16[3,32,128]{2,1,0:T(8,128)(2,1)S(1)} %get-tuple-element.74), channel_id=1, source_target_pairs={{8,16},{9,17},{10,18},{11,19},{12,20},{13,21},{14,22},{15,23},{16,... | collective-permute-start | bytes 73736 | tf_op jit(solution)/shard_map/cond/branch_5_fun/ppermute | solution.py:722
  5.6 1.3 %collective-permute-start.11 = (bf16[3,32,128]{2,1,0:T(8,128)(2,1)S(1)}, bf16[3,32,128]{2,1,0:T(8,128)(2,1)}, u32[]{:S(2)}, u32[]{:S(2)}) collective-permute-start(bf16[3,32,128]{2,1,0:T(8,128)(2,1)S(1)} %get-tuple-element.75), channel_id=1, source_target_pairs={{24,28},{25,27},{26,26},{27,25},{28,24},{29,31},{30,30},{31,29}} | collective-permute-start | bytes 73736 | tf_op jit(solution)/shard_map/cond/branch_5_fun/ppermute | solution.py:722
  7.8 0.6 copy-start.6
  8.4 0.6 copy-start.7
  9.0 8.3 %collective-permute-start.33 = (bf16[3,134,128]{2,1,0:T(8,128)(2,1)S(1)}, bf16[3,134,128]{2,1,0:T(8,128)(2,1)S(1)}, u32[]{:S(2)}, u32[]{:S(2)}) collective-permute-start(bf16[3,134,128]{2,1,0:T(8,128)(2,1)S(1)} %get-tuple-element.154), channel_id=1, source_target_pairs={{0,1},{1,2},{2,3},{3,4},{4,5},{5,6},{6,7},{7,0},{8,9},{9,10},{10,1... | collective-permute-start | bytes 308744 | tf_op jit(solution)/shard_map/ppermute | solution.py:746
  11.5 5.8 %collective-permute-start.34 = (bf16[3,134,128]{2,1,0:T(8,128)(2,1)S(1)}, bf16[3,134,128]{2,1,0:T(8,128)(2,1)S(1)}, u32[]{:S(2)}, u32[]{:S(2)}) collective-permute-start(bf16[3,134,128]{2,1,0:T(8,128)(2,1)S(1)} %get-tuple-element.155), channel_id=1, source_target_pairs={{0,7},{1,0},{2,1},{3,2},{4,3},{5,4},{6,5},{7,6},{8,15},{9,8},{10,9... | collective-permute-start | bytes 308744 | tf_op jit(solution)/shard_map/ppermute | solution.py:745
  17.3 0.6 copy-start.11
  17.3 0.7 copy-start.12
  18.0 61.6 %copy-start.3 = (bf16[49,128]{1,0:T(8,128)(2,1)S(1)}, bf16[49,128]{1,0:T(8,128)(2,1)}, u32[]{:S(2)}) copy-start(bf16[49,128]{1,0:T(8,128)(2,1)} %dw.5) | copy-start | bytes 37636
  51.0 17.9 %copy-start.4 = (bf16[384,128]{1,0:T(8,128)(2,1)S(1)}, bf16[384,128]{1,0:T(8,128)(2,1)}, u32[]{:S(2)}) copy-start(bf16[384,128]{1,0:T(8,128)(2,1)} %get-tuple-element.167.lc) | copy-start | bytes 294916
  51.0 28.6 %copy-start.1 = (bf16[4096,128]{1,0:T(8,128)(2,1)S(1)}, bf16[4096,128]{1,0:T(8,128)(2,1)}, u32[]{:S(2)}) copy-start(bf16[4096,128]{1,0:T(8,128)(2,1)} %get-tuple-element.173.g) | copy-start | bytes 3145732
  51.0 28.6 %copy-start.2 = (bf16[4096,128]{1,0:T(8,128)(2,1)S(1)}, bf16[4096,128]{1,0:T(8,128)(2,1)}, u32[]{:S(2)}) copy-start(bf16[4096,128]{1,0:T(8,128)(2,1)} %get-tuple-element.174.dirin) | copy-start | bytes 3145732
  51.0 3.8 %collective-permute-start.35 = (bf16[1440,128]{1,0:T(8,128)(2,1)}, bf16[1440,128]{1,0:T(8,128)(2,1)S(1)}, u32[]{:S(2)}, u32[]{:S(2)}) collective-permute-start(bf16[1440,128]{1,0:T(8,128)(2,1)} %get-tuple-element.159), channel_id=1, source_target_pairs={{0,8},{8,0},{16,24},{24,16},{1,9},{9,1},{17,25},{25,17},{2,10},{10... | collective-permute-start | bytes 1105928 | tf_op jit(solution)/shard_map/ppermute | solution.py:753
  56.0 10.9 %collective-permute-start.36 = (bf16[336,128]{1,0:T(8,128)(2,1)S(1)}, bf16[336,128]{1,0:T(8,128)(2,1)S(1)}, u32[]{:S(2)}, u32[]{:S(2)}) collective-permute-start(bf16[336,128]{1,0:T(8,128)(2,1)S(1)} %get-tuple-element.186), channel_id=1, source_target_pairs={{0,1},{1,0},{2,3},{3,2},{4,5},{5,4},{6,7},{7,6},{8,9},{9,8},{10,11... | collective-permute-start | bytes 258056 | tf_op jit(solution)/shard_map/ppermute | solution.py:602
  57.0 10.8 %collective-permute-start.38 = (bf16[336,128]{1,0:T(8,128)(2,1)S(1)}, bf16[336,128]{1,0:T(8,128)(2,1)S(1)}, u32[]{:S(2)}, u32[]{:S(2)}) collective-permute-start(bf16[336,128]{1,0:T(8,128)(2,1)S(1)} %get-tuple-element.187), channel_id=1, source_target_pairs={{0,17},{1,16},{2,19},{3,18},{4,21},{5,20},{6,23},{7,22},{8,25},{9,... | collective-permute-start | bytes 258056 | tf_op jit(solution)/shard_map/ppermute | solution.py:602
  64.4 4.5 %collective-permute-start.37 = (bf16[336,128]{1,0:T(8,128)(2,1)S(1)}, bf16[336,128]{1,0:T(8,128)(2,1)S(1)}, u32[]{:S(2)}, u32[]{:S(2)}) collective-permute-start(bf16[336,128]{1,0:T(8,128)(2,1)S(1)} %get-tuple-element.188), channel_id=1, source_target_pairs={{0,16},{1,17},{2,18},{3,19},{4,20},{5,21},{6,22},{7,23},{8,24},{9,... | collective-permute-start | bytes 258056 | tf_op jit(solution)/shard_map/ppermute | solution.py:602
  64.4 2.5 %collective-permute-start.26 = (bf16[3,32,128]{2,1,0:T(8,128)(2,1)S(1)}, bf16[3,32,128]{2,1,0:T(8,128)(2,1)}, u32[]{:S(2)}, u32[]{:S(2)}) collective-permute-start(bf16[3,32,128]{2,1,0:T(8,128)(2,1)S(1)} %get-tuple-element.90), channel_id=1, source_target_pairs={{8,16},{9,17},{10,18},{11,19},{12,20},{13,21},{14,22},{15,23},{16,... | collective-permute-start | bytes 73736 | tf_op jit(solution)/shard_map/cond/branch_5_fun/ppermute | solution.py:722
  65.7 1.3 %collective-permute-start.27 = (bf16[3,32,128]{2,1,0:T(8,128)(2,1)S(1)}, bf16[3,32,128]{2,1,0:T(8,128)(2,1)}, u32[]{:S(2)}, u32[]{:S(2)}) collective-permute-start(bf16[3,32,128]{2,1,0:T(8,128)(2,1)S(1)} %get-tuple-element.91), channel_id=1, source_target_pairs={{24,28},{25,27},{26,26},{27,25},{28,24},{29,31},{30,30},{31,29}} | collective-permute-start | bytes 73736 | tf_op jit(solution)/shard_map/cond/branch_5_fun/ppermute | solution.py:722
  69.0 0.9 copy-start.5
  70.8 12.3 %collective-permute-start.41 = (bf16[336,128]{1,0:T(8,128)(2,1)S(1)}, bf16[336,128]{1,0:T(8,128)(2,1)S(1)}, u32[]{:S(2)}, u32[]{:S(2)}) collective-permute-start(bf16[336,128]{1,0:T(8,128)(2,1)S(1)} %fusion.1), channel_id=1, source_target_pairs={{0,6},{1,7},{2,4},{3,5},{4,2},{5,3},{6,0},{7,1},{8,14},{9,15},{10,... | collective-permute-start | bytes 258056 | tf_op jit(solution)/shard_map/ppermute | solution.py:611
  74.5 8.7 %collective-permute-start.40 = (bf16[336,128]{1,0:T(8,128)(2,1)S(1)}, bf16[336,128]{1,0:T(8,128)(2,1)S(1)}, u32[]{:S(2)}, u32[]{:S(2)}) collective-permute-start(bf16[336,128]{1,0:T(8,128)(2,1)S(1)} %fusion.1), channel_id=1, source_target_pairs={{0,4},{1,5},{2,6},{3,7},{4,0},{5,1},{6,2},{7,3},{8,12},{9,13},{10,... | collective-permute-start | bytes 258056 | tf_op jit(solution)/shard_map/ppermute | solution.py:611
  74.5 8.7 %collective-permute-start.39 = (bf16[336,128]{1,0:T(8,128)(2,1)S(1)}, bf16[336,128]{1,0:T(8,128)(2,1)S(1)}, u32[]{:S(2)}, u32[]{:S(2)}) collective-permute-start(bf16[336,128]{1,0:T(8,128)(2,1)S(1)} %fusion.1), channel_id=1, source_target_pairs={{0,2},{1,3},{2,0},{3,1},{4,6},{5,7},{6,4},{7,5},{8,10},{9,11},{10,... | collective-permute-start | bytes 258056 | tf_op jit(solution)/shard_map/ppermute | solution.py:611
  75.2 12.3 %collective-permute-start.44 = (bf16[416,128]{1,0:T(8,128)(2,1)S(1)}, bf16[416,128]{1,0:T(8,128)(2,1)S(1)}, u32[]{:S(2)}, u32[]{:S(2)}) collective-permute-start(bf16[416,128]{1,0:T(8,128)(2,1)S(1)} %get-tuple-element.179), channel_id=1, source_target_pairs={{0,7},{1,0},{2,1},{3,2},{4,3},{5,4},{6,5},{7,6},{8,15},{9,8},{10,9... | collective-permute-start | bytes 319496 | tf_op jit(solution)/shard_map/ppermute | solution.py:762
  79.6 7.9 %collective-permute-start.43 = (bf16[416,128]{1,0:T(8,128)(2,1)S(1)}, bf16[416,128]{1,0:T(8,128)(2,1)S(1)}, u32[]{:S(2)}, u32[]{:S(2)}) collective-permute-start(bf16[416,128]{1,0:T(8,128)(2,1)S(1)} %get-tuple-element.178), channel_id=1, source_target_pairs={{0,1},{1,2},{2,3},{3,4},{4,5},{5,6},{6,7},{7,0},{8,9},{9,10},{10,1... | collective-permute-start | bytes 319496 | tf_op jit(solution)/shard_map/ppermute | solution.py:763
  83.2 8.1 %collective-permute-start.42 = (bf16[336,128]{1,0:T(8,128)(2,1)S(1)}, bf16[336,128]{1,0:T(8,128)(2,1)S(1)}, u32[]{:S(2)}, u32[]{:S(2)}) collective-permute-start(bf16[336,128]{1,0:T(8,128)(2,1)S(1)} %add_convert_fusion.1), channel_id=1, source_target_pairs={{0,1},{1,0},{2,3},{3,2},{4,5},{5,4},{6,7},{7,6},{8,9},{9,8},{10,11... | collective-permute-start | bytes 258056 | tf_op jit(solution)/shard_map/ppermute | solution.py:770
  83.3 8.0 %collective-permute-start.46 = (bf16[336,128]{1,0:T(8,128)(2,1)S(1)}, bf16[336,128]{1,0:T(8,128)(2,1)S(1)}, u32[]{:S(2)}, u32[]{:S(2)}) collective-permute-start(bf16[336,128]{1,0:T(8,128)(2,1)S(1)} %add_convert_fusion.1), channel_id=1, source_target_pairs={{0,17},{1,16},{2,19},{3,18},{4,21},{5,20},{6,23},{7,22},{8,25},{9,... | collective-permute-start | bytes 258056 | tf_op jit(solution)/shard_map/ppermute | solution.py:770
  87.6 4.5 %collective-permute-start.45 = (bf16[336,128]{1,0:T(8,128)(2,1)S(1)}, bf16[336,128]{1,0:T(8,128)(2,1)S(1)}, u32[]{:S(2)}, u32[]{:S(2)}) collective-permute-start(bf16[336,128]{1,0:T(8,128)(2,1)S(1)} %add_convert_fusion.1), channel_id=1, source_target_pairs={{0,16},{1,17},{2,18},{3,19},{4,20},{5,21},{6,22},{7,23},{8,24},{9,... | collective-permute-start | bytes 258056 | tf_op jit(solution)/shard_map/ppermute | solution.py:770
  92.1 1.7 %copy-start.9 = (bf16[4,336,128]{2,1,0:T(8,128)(2,1)}, bf16[4,336,128]{2,1,0:T(8,128)(2,1)S(1)}, u32[]{:S(2)}) copy-start(bf16[4,336,128]{2,1,0:T(8,128)(2,1)S(1)} %pad_maximum_fusion.mine) | copy-start | bytes 1032196
  92.1 1.7 %collective-permute-start.47 = (bf16[4,336,128]{2,1,0:T(8,128)(2,1)S(1)}, bf16[4,336,128]{2,1,0:T(8,128)(2,1)S(1)}, u32[]{:S(2)}, u32[]{:S(2)}) collective-permute-start(bf16[4,336,128]{2,1,0:T(8,128)(2,1)S(1)} %pad_maximum_fusion.mine), channel_id=1, source_target_pairs={{0,8},{8,0},{16,24},{24,16},{1,9},{9,1},{17,25},{25,17},{2,10},{10... | collective-permute-start | bytes 1032200 | tf_op jit(solution)/shard_map/ppermute | solution.py:773
  93.8 0.7 copy-start.10

commit v3 on v2

--- a/solution.py
+++ b/solution.py
@@ -13,10 +13,12 @@
 f32, bf16 = jnp.float32, jnp.bfloat16
 S = 16
 LOG2E = 1.4426950408889634
+LOG2_DENS = -0.3257480647361593
 HALF = 1344
 VMEM = pl.BlockSpec(memory_space=pltpu.VMEM)
 SMEM = pl.BlockSpec(memory_space=pltpu.SMEM)
-PARAMS = pltpu.CompilerParams(vmem_limit_bytes=60 * 2**20)
+PARAMS = pltpu.CompilerParams(vmem_limit_bytes=44 * 2**20)
+WHOLE = pltpu.CompilerParams(vmem_limit_bytes=63 * 2**20 + 2**19)
 SMALL = pltpu.CompilerParams(vmem_limit_bytes=24 * 2**20)
 
 
@@ -53,10 +55,11 @@
     return rstd * (u - m[:, :128] - hat * m[:, 128:])
 
 
-def gelu(h):
-    cdf = 0.5 + 0.5 * lax.erf(h * 0.7071067811865476)
-    e = jnp.exp2(h * h * (-0.5 * LOG2E))
-    return h * cdf, cdf + h * (e * 0.3989422804014327)
+def gelu2(h):
+    g = h * 0.7071067811865476
+    c = 1.0 + lax.erf(g)
+    e = jnp.exp2(g * g * (-LOG2E) + LOG2_DENS)
+    return h * c, c + h * e
 
 
 def weights_table(dw, w49, flip):
@@ -90,7 +93,7 @@
     R, CW,
     field, south, north, left, right, land, dw, gain, upw, bias, down, scale, sgain, sw, sbias, cot,
     bott, gout, dirout, send, last, lcol, rcol, keep, away,
-    x2d, el, w49, dep, hat, rst, nrm, act, slp, shat, srst, p1, back, tacc, downs, ups, mgs, landb, up, sums,
+    x2d, el, w49, dep, hat, rst, nrm, act, slp, shat, srst, p1, back, tacc, downs, ups, mgs, landb, up, dn, sums,
 ):
     I = R // S
     CE = CW + 6
@@ -131,6 +134,7 @@
         for c in range(CW):
             at = (i * CW + c) * S
             landb[at : at + S, :] = land_w[i * S : (i + 1) * S, c * 128 : (c + 1) * 128]
+    dn[...] = (down[...].astype(f32) * 0.5).astype(bf16)
     up[0:128, :] = upw[...]
     up[128:256, :] = jnp.where(
         lax.broadcasted_iota(jnp.int32, (128, 512), 0) == 0, bias[...].astype(f32).reshape(1, 512), 0.0
@@ -145,7 +149,7 @@
     g_n = gain[...].astype(f32).reshape(1, 128)
     sc = scale[...].astype(f32).reshape(1, 128)
     sg0 = sgain[0:1, :].astype(f32)
-    T1 = 1024
+    T1 = n0 // 2
 
     def nfwd(n, _):
         base = pl.multiple_of(n * T1, T1)
@@ -160,7 +164,7 @@
 
     lax.fori_loop(0, n0 // T1, nfwd, 0)
 
-    T2 = 512
+    T2 = n0 // 4
     onec = (lax.broadcasted_iota(jnp.int32, (T2, 128), 1) == 0).astype(f32).astype(bf16)
 
     def upf(n, _):
@@ -168,7 +172,7 @@
         lhs = jnp.concatenate([nrm[pl.ds(base, T2), :], onec], axis=1)
         for q in range(2):
             hid = dot(lhs, up[:, q * 256 : (q + 1) * 256])
-            ac, sl = gelu(hid)
+            ac, sl = gelu2(hid)
             act[pl.ds(base, T2), q * 256 : (q + 1) * 256] = ac.astype(bf16)
             slp[pl.ds(base, T2), q * 256 : (q + 1) * 256] = sl.astype(bf16)
         return 0
@@ -185,7 +189,7 @@
 
     def dnf(i2, _):
         base = pl.multiple_of(i2 * TP, TP)
-        mixed = dot(act[pl.ds(base, TP), :], down[...])
+        mixed = dot(act[pl.ds(base, TP), :], dn[...])
         xs = jnp.concatenate(
             [el[pl.ds((i2 * 2 + a + 3) * CE + 3, CW)].reshape(CW * S, 128) for a in range(2)], axis=0
         ).astype(f32)
@@ -262,13 +266,13 @@
         mgs[pl.ds(base, TP), :] = (dr * sc).astype(bf16)
         return 0
 
-    lax.fori_loop(0, I // 2, bk1, 0)
+    lax.fori_loop(0, I // 2, bk1, 0, unroll=2)
 
     def bk2(n, _):
         base = pl.multiple_of(n * T2, T2)
         mg = mgs[pl.ds(base, T2), :]
         for q in range(2):
-            ag = dot_r(mg, down[q * 256 : (q + 1) * 256, :])
+            ag = dot_r(mg, dn[q * 256 : (q + 1) * 256, :])
             sl = slp[pl.ds(base, T2), q * 256 : (q + 1) * 256].astype(f32)
             slp[pl.ds(base, T2), q * 256 : (q + 1) * 256] = (ag * sl).astype(bf16)
         return 0
@@ -283,7 +287,7 @@
         return 0
 
     lax.fori_loop(0, n0 // T1, bk3, 0)
-    downs[...] = dot_t(mgs[...], act[...])
+    downs[...] = dot_t(mgs[...], act[...]) * 0.5
     ups[...] = dot_t(nrm[...], slp[...])
     put(1536, downs[...], 4)
     put(2048, ups[...], 4)
@@ -362,6 +366,7 @@
         V((n, C), bf16),
         V((n, C), bf16),
         V((256, 512), bf16),
+        V((512, 128), bf16),
         V((2 * HALF, C), bf16),
     ]
     return pl.pallas_call(
@@ -565,7 +570,7 @@
         in_specs=[VMEM, VMEM],
         out_specs=[VMEM] * 4,
         scratch_shapes=[pltpu.VMEM((8 * chunk, 128), bf16)],
-        compiler_params=PARAMS,
+        compiler_params=SMALL,
         name="finish_sums",
     )(mine, other)
 
@@ -622,35 +627,80 @@
     return lax.axis_index("lat") == lax.axis_size("lat") - 1
 
 
-def rim_body(R, CW, field, mirror, near, send, last, lc, rc, place, scr):
+def rim_body(R, CW, field, mirror, near, send, last, place, low, high, mir, sems):
     odd = lax.axis_index("lat") % 2
+    copies = [
+        pltpu.make_async_copy(mirror, mir, sems.at[0]),
+        pltpu.make_async_copy(field.at[0:3], low, sems.at[1]),
+        pltpu.make_async_copy(field.at[R - 3 : R], high, sems.at[2]),
+    ]
+    for c in copies:
+        c.start()
+    for c in copies:
+        c.wait()
     for k in range(3):
-        lo = field[k]
-        hi = field[R - 3 + k]
+        lo = low[k]
+        hi = high[k]
         last[k] = hi
         send[k] = jnp.where(odd == 1, hi, lo)
         near[k] = jnp.where(odd == 1, lo, hi)
-    place[0] = mirror[0] // CW
-    place[1] = mirror[0] % CW
-    scr[0 : R * 8, :] = field[:, 0:8, :].astype(f32).reshape(R * 8, 128)
-    scr[R * 8 :, :] = field[:, CW - 8 : CW, :].astype(f32).reshape(R * 8, 128)
-    for k in range(3):
-        lc[k] = scr[pl.ds(k, R, stride=8), :].astype(bf16)
-        rc[k] = scr[pl.ds(R * 8 + 5 + k, R, stride=8), :].astype(bf16)
+    place[0] = mir[0] // CW
+    place[1] = mir[0] % CW
 
 
 def rim(field, mirror):
     R, CW, C = field.shape
     sd = jax.ShapeDtypeStruct
+    hbm = pl.BlockSpec(memory_space=pltpu.HBM)
     return pl.pallas_call(
         functools.partial(rim_body, R, CW),
-        out_shape=(sd((3, CW, C), bf16),) * 3 + (sd((3, R, C), bf16),) * 2 + (sd((2,), jnp.int32),),
-        in_specs=[VMEM, SMEM],
-        out_specs=[VMEM] * 5 + [SMEM],
-        scratch_shapes=[pltpu.VMEM((2 * R * 8, C), f32)],
-        compiler_params=SMALL,
+        out_shape=(sd((3, CW, C), bf16),) * 3 + (sd((2,), jnp.int32),),
+        in_specs=[hbm, hbm],
+        out_specs=[VMEM] * 3 + [SMEM],
+        scratch_shapes=[
+            pltpu.VMEM((3, CW, C), bf16),
+            pltpu.VMEM((3, CW, C), bf16),
+            pltpu.SMEM(mirror.shape, jnp.int32),
+            pltpu.SemaphoreType.DMA((3,)),
+        ],
+        compiler_params=WHOLE,
         name="rim",
     )(field, mirror)
+
+
+def sides_body(R, CW, field, lc, rc, low, high, cols, sems):
+    copies = [
+        pltpu.make_async_copy(field.at[:, 0:16], low, sems.at[0]),
+        pltpu.make_async_copy(field.at[:, CW - 16 : CW], high, sems.at[1]),
+    ]
+    for c in copies:
+        c.start()
+    for c in copies:
+        c.wait()
+    cols[0 : R * 8, :] = low[:, 0:8, :].astype(f32).reshape(R * 8, 128)
+    cols[R * 8 :, :] = high[:, 8:16, :].astype(f32).reshape(R * 8, 128)
+    for k in range(3):
+        lc[k] = cols[pl.ds(k, R, stride=8), :].astype(bf16)
+        rc[k] = cols[pl.ds(R * 8 + 5 + k, R, stride=8), :].astype(bf16)
+
+
+def sides(field):
+    R, CW, C = field.shape
+    sd = jax.ShapeDtypeStruct
+    return pl.pallas_call(
+        functools.partial(sides_body, R, CW),
+        out_shape=(sd((3, R, C), bf16),) * 2,
+        in_specs=[pl.BlockSpec(memory_space=pltpu.HBM)],
+        out_specs=[VMEM] * 2,
+        scratch_shapes=[
+            pltpu.VMEM((R, 16, C), bf16),
+            pltpu.VMEM((R, 16, C), bf16),
+            pltpu.VMEM((2 * R * 8, C), f32),
+            pltpu.SemaphoreType.DMA((2,)),
+        ],
+        compiler_params=SMALL,
+        name="sides",
+    )(field)
 
 
 def join_body(CW, width, flip, place, near, far, blk_b, lc, rc, south, north, lp, rp, cat, scr):
@@ -684,10 +734,10 @@
                 pay[j] = cat[0 : width + 6, :].astype(bf16)
         else:
             pay[0:width, :] = core[...]
-            for side in range(2):
+            for end in range(2):
                 for k in range(3):
-                    src = (3 + 3 * side + k) * CW + lo
-                    cat[side * 9 + k * 3 : side * 9 + k * 3 + 3, :] = scr[src : src + 3, :]
+                    src = (3 + 3 * end + k) * CW + lo
+                    cat[end * 9 + k * 3 : end * 9 + k * 3 + 3, :] = scr[src : src + 3, :]
             pay[width : width + 32, :] = cat[0:32, :].astype(bf16)
 
 
@@ -707,7 +757,7 @@
     )(place, near, far, blk_b, lc, rc)
 
 
-def far_rows(send, last, quot):
+def far_rows(send, last, quot, work=lambda: ()):
     nl = lax.axis_size("lon")
     nt = lax.axis_size("lat")
     top = (nt - 1) * nl
@@ -716,14 +766,14 @@
     swap += [(j, i) for i, j in swap]
 
     def branch(q):
-        def run(send, last):
+        def run():
             fa = [(top + e, top + (q - e) % nl) for e in range(nl)]
             fb = [(top + e, top + (q - 1 - e) % nl) for e in range(nl)]
-            return lax.ppermute(send, axes, swap + fa), lax.ppermute(last, axes, fb)
+            return lax.ppermute(send, axes, swap + fa), lax.ppermute(last, axes, fb), work()
 
         return run
 
-    return lax.switch(quot, [branch(q) for q in range(nl)], send, last)
+    return lax.switch(quot, [branch(q) for q in range(nl)])
 
 
 def shift_pairs(axis, by):
@@ -738,9 +788,9 @@
     R, CW, C = field.shape
     total = R * CW * lax.axis_size("lat") * lax.axis_size("lon")
     factor = 1.0 / math.sqrt(total / 64.0)
-    near, send, last, lc, rc, shift = rim(field, mirror)
+    near, send, last, shift = rim(field, mirror)
     near = lax.ppermute(near, "lat", flip_pairs("lat", 1))
-    far, blk_b = far_rows(send, last, shift[0])
+    far, blk_b, (lc, rc) = far_rows(send, last, shift[0], lambda: sides(field))
     south_f, north_f, lpay, rpay = join(shift, near, far, blk_b, lc, rc, True)
     right_f = lax.ppermute(lpay, "lon", shift_pairs("lon", -1))
     left_f = lax.ppermute(rpay, "lon", shift_pairs("lon", 1))
@@ -755,16 +805,15 @@
     held = add_bf(keep, got[:HALF]).reshape(4, HALF // 4, C)
     send, held = lax.optimization_barrier((send, held))
     chunk = square_sum(held, place)
-    far, blk_b = far_rows(send, last, shift[0])
+    far, blk_b, base = far_rows(
+        send, last, shift[0], lambda: conv_back(g, direct, depth_weight, R, CW)
+    )
     chunk, far = lax.optimization_barrier((chunk, far))
     south_g, north_g, lpay, rpay = join(shift, near, far, blk_b, lcol, rcol, False)
     chunk, lpay = lax.optimization_barrier((chunk, lpay))
     gr = lax.ppermute(lpay, "lon", shift_pairs("lon", -1))
     gl = lax.ppermute(rpay, "lon", shift_pairs("lon", 1))
-    g, _ = lax.optimization_barrier((g, south_g))
-    base = conv_back(g, direct, depth_weight, R, CW)
     chunk = line_sum(chunk)
-    chunk, base = lax.optimization_barrier((chunk, base))
     grad_field = edges(base, south_g, north_g, gl, gr, depth_weight, R, CW)
     axes = ("lat", "lon")
     back = [lax.ppermute(chunk, axes, square_pairs(k)) for k in (1, 2, 3)]

time: 98.2 us -> 93.3 us (0.950)
  local copies, waits for them, and re-layouts: 5.44 us -> 1.61 us
  Pallas kernels: 45.7 us -> 43.1 us
  waiting for transfers between devices: 8.68 us -> 10.2 us
  starting transfers between devices: 35.1 us -> 33.9 us
    unnamed x26 -> x28, local copies, waits for them, and re-layouts: 5.41 us -> 0.08 us
    pallas_call x1, Pallas kernels: 33 us -> 28.7 us  [block_pass(): pl.pallas_call(functools.partial(block_body, R, CW), out_shape=out_shape,...]
    ppermute x1, waiting for transfers between devices: 0.01 us -> 2.58 us  [on_device(): gl = lax.ppermute(rpay, 'lon', shift_pairs('lon', 1))]
    ppermute x3, waiting for transfers between devices: 0.01 us -> 2.23 us  [line_sum(): lax.ppermute(total, 'lon', flip_pairs('lon', bit * k))]
    ppermute x3, waiting for transfers between devices: 1.96 us -> 0.01 us  [square_sum(): came.append(lax.ppermute(part, ('lat', 'lon'), square_pairs(k)))]
    pallas_call x0 -> x1, Pallas kernels: none -> 1.34 us  [sides(): pl.pallas_call(functools.partial(sides_body, R, CW), out_shape=(sd((3, R,...]
    ppermute x3, starting transfers between devices: 8.42 us -> 7.18 us  [square_sum(): came.append(lax.ppermute(part, ('lat', 'lon'), square_pairs(k)))]
    pallas_call x1, Pallas kernels: 3.45 us -> 4.67 us  [conv_back(): pl.pallas_call(functools.partial(conv_back_body, R, CW), out_shape=jax.Sh...]
  transfers between devices with their start and end apart: 20 -> 20, of which waited for: 6 -> 7; matrix products, arithmetic and copies ran while one was open for 0% -> 1% of each run, Pallas kernels for 7% -> 11%
where the time goes in v3:
time: 93.3 us; the launch traced here: 91.9 us
  Pallas kernels  43.1 us (46%)
  starting transfers between devices  33.9 us (36%)
  waiting for transfers between devices  10.2 us (11%)
  local copies, waits for them, and re-layouts  1.61 us (2%)
  between operations  1.54 us (2%)
  other arithmetic  1.26 us (1%)
    pallas_call x1, Pallas kernels, block_pass(): pl.pallas_call(functools.partial(block_body, R, CW), out_shape=out_shape,...  28.7 us
    ppermute x3, starting transfers between devices, square_sum(): came.append(lax.ppermute(part, ('lat', 'lon'), square_pairs(k)))  7.18 us
    pallas_call x1, Pallas kernels, conv_back(): pl.pallas_call(functools.partial(conv_back_body, R, CW), out_shape=jax.Sh...  4.67 us
    ppermute x3, starting transfers between devices, line_sum(): lax.ppermute(total, 'lon', flip_pairs('lon', bit * k))  4.44 us
    ppermute x1, starting transfers between devices, on_device(): gr = lax.ppermute(lpay, 'lon', shift_pairs('lon', -1))  4.44 us
    ppermute x3, starting transfers between devices, on_device(): back = [lax.ppermute(chunk, axes, square_pairs(k)) for k in (1, 2, 3)]  3.86 us
    pallas_call x1, Pallas kernels, edges(): pl.pallas_call(functools.partial(edges_body, R, CW), out_shape=jax.ShapeD...  3.74 us
    ppermute x1, starting transfers between devices, on_device(): right_f = lax.ppermute(lpay, 'lon', shift_pairs('lon', -1))  3.1 us
  transfers between devices with their start and end apart: 20, of which 7 were waited for; matrix products, arithmetic and copies ran while one was open for 1% of the time, Pallas kernels for 11%

profile of v3, /device:TPU:0, one launch (start us, length us, event | category | flops | bytes accessed | tf_op | source)
XLA Modules:
  0.0 91.9 jit_solution(4909645901280346589)
XLA Ops:
  0.6 1.4 %rim.1 = (bf16[3,32,128]{2,1,0:T(8,128)(2,1)}, bf16[3,32,128]{2,1,0:T(8,128)(2,1)S(1)}, bf16[3,32,128]{2,1,0:T(8,128)(2,1)S(1)}, s32[2]{0:T(128)}) custom-call(bf16[128,32,128]{2,1,0:T(8,128)(2,1)} %field.3, s32[256]{0:T(256)} %mirror.1), custom_call_target="tpu_custom_call" | custom-call | tf_op jit(solution)/shard_map/rim/pallas_call | solution.py:655
  2.0 0.5 collective-permute-start.32
  3.2 0.0 copy-start
  3.2 0.0 copy-start.1
  3.3 0.0 copy-start.2
  3.3 0.0 copy-start.3
  3.3 0.0 copy-start.4
  3.3 0.0 copy-start.6
  3.3 0.0 copy-start.7
  3.3 0.0 copy-start.8
  3.3 0.0 copy-start.9
  3.3 0.0 copy-start.10
  3.4 0.0 copy-start.11
  3.4 4.1 %conditional.2 = (bf16[3,32,128]{2,1,0:T(8,128)(2,1)}, bf16[3,32,128]{2,1,0:T(8,128)(2,1)}, bf16[3,128,128]{2,1,0:T(8,128)(2,1)S(1)}, bf16[3,128,128]{2,1,0:T(8,128)(2,1)S(1)}) conditional(s32[]{:T(128)} %bitcast, (bf16[3,32,128]{2,1,0:T(8,128)(2,1)S(1)}, bf16[3,32,128]{2,1,0:T(8,128)(2,1)S(1)}, ...), branch_computations={%region_0.0_spmd, %region_1.0_spmd, %region_2.0_spmd, %region_3.0_... | conditional | bytes 196720 | solution.py:776
  3.4 1.4 %collective-permute-start.10 = (bf16[3,32,128]{2,1,0:T(8,128)(2,1)S(1)}, bf16[3,32,128]{2,1,0:T(8,128)(2,1)}, u32[]{:S(2)}, u32[]{:S(2)}) collective-permute-start(bf16[3,32,128]{2,1,0:T(8,128)(2,1)S(1)} %get-tuple-element.153), channel_id=1, source_target_pairs={{8,16},{9,17},{10,18},{11,19},{12,20},{13,21},{14,22},{15,23},{16,... | collective-permute-start | bytes 73736 | tf_op jit(solution)/shard_map/cond/branch_5_fun/ppermute | solution.py:772
  4.8 1.3 %collective-permute-start.11 = (bf16[3,32,128]{2,1,0:T(8,128)(2,1)S(1)}, bf16[3,32,128]{2,1,0:T(8,128)(2,1)}, u32[]{:S(2)}, u32[]{:S(2)}) collective-permute-start(bf16[3,32,128]{2,1,0:T(8,128)(2,1)S(1)} %get-tuple-element.154), channel_id=1, source_target_pairs={{24,28},{25,27},{26,26},{27,25},{28,24},{29,31},{30,30},{31,29}} | collective-permute-start | bytes 73736 | tf_op jit(solution)/shard_map/cond/branch_5_fun/ppermute | solution.py:772
  6.1 1.3 %sides.13 = (bf16[3,128,128]{2,1,0:T(8,128)(2,1)S(1)}, bf16[3,128,128]{2,1,0:T(8,128)(2,1)S(1)}) custom-call(bf16[128,32,128]{2,1,0:T(8,128)(2,1)} %get-tuple-element.155.field), custom_call_target="tpu_custom_call" | custom-call | tf_op jit(solution)/shard_map/cond/branch_5_fun/sides/pallas_call | solution.py:690
  7.5 1.0 %join.2 = (bf16[3,32,128]{2,1,0:T(8,128)(2,1)S(1)}, bf16[3,32,128]{2,1,0:T(8,128)(2,1)S(1)}, bf16[3,134,128]{2,1,0:T(8,128)(2,1)S(1)}, bf16[3,134,128]{2,1,0:T(8,128)(2,1)S(1)}) custom-call(s32[2]{0:T(128)S(1)} %copy-done.5, bf16[3,32,128]{2,1,0:T(8,128)(2,1)S(1)} %collective-permute-done.32.near, bf16[3,32,128]{2,1,0:T(8,128)(2,1)} %get-tuple-element.258.far, ...), custom_call_target="tpu_custom_call" | custom-call | tf_op jit(solution)/shard_map/join/pallas_call | solution.py:749
  8.4 2.6 %collective-permute-start.33 = (bf16[3,134,128]{2,1,0:T(8,128)(2,1)S(1)}, bf16[3,134,128]{2,1,0:T(8,128)(2,1)S(1)}, u32[]{:S(2)}, u32[]{:S(2)}) collective-permute-start(bf16[3,134,128]{2,1,0:T(8,128)(2,1)S(1)} %get-tuple-element.264), channel_id=1, source_target_pairs={{0,1},{1,2},{2,3},{3,4},{4,5},{5,6},{6,7},{7,0},{8,9},{9,10},{10,1... | collective-permute-start | bytes 308744 | tf_op jit(solution)/shard_map/ppermute | solution.py:796
  11.0 3.1 %collective-permute-start.34 = (bf16[3,134,128]{2,1,0:T(8,128)(2,1)S(1)}, bf16[3,134,128]{2,1,0:T(8,128)(2,1)S(1)}, u32[]{:S(2)}, u32[]{:S(2)}) collective-permute-start(bf16[3,134,128]{2,1,0:T(8,128)(2,1)S(1)} %get-tuple-element.265), channel_id=1, source_target_pairs={{0,7},{1,0},{2,1},{3,2},{4,3},{5,4},{6,5},{7,6},{8,15},{9,8},{10,9... | collective-permute-start | bytes 308744 | tf_op jit(solution)/shard_map/ppermute | solution.py:795
  14.1 2.7 %collective-permute-done.33.left = bf16[3,134,128]{2,1,0:T(8,128)(2,1)S(1)} collective-permute-done((bf16[3,134,128]{2,1,0:T(8,128)(2,1)S(1)}, bf16[3,134,128]{2,1,0:T(8,128)(2,1)S(1)}, u32[]{:S(2)}, u32[]{:S(2)}) %collective-permute-start.33) | collective-permute-done | bytes 102944 | tf_op jit(solution)/shard_map/ppermute | solution.py:796
  16.8 0.1 collective-permute-done.34.right
  17.0 28.7 %block_pass.1 = (bf16[16,4,128]{2,1,0:T(4,128)(2,1)}, bf16[4096,128]{1,0:T(8,128)(2,1)S(1)}, bf16[4096,128]{1,0:T(8,128)(2,1)}, bf16[3,32,128]{2,1,0:T(8,128)(2,...) custom-call(bf16[128,32,128]{2,1,0:T(8,128)(2,1)} %field.3, ...), custom_call_target="tpu_custom_call" | custom-call | tf_op jit(solution)/shard_map/block_pass/pallas_call | solution.py:372
  45.6 1.9 %collective-permute-start.35 = (bf16[1440,128]{1,0:T(8,128)(2,1)S(1)}, bf16[1440,128]{1,0:T(8,128)(2,1)S(1)}, u32[]{:S(2)}, u32[]{:S(2)}) collective-permute-start(bf16[1440,128]{1,0:T(8,128)(2,1)S(1)} %get-tuple-element.269), channel_id=1, source_target_pairs={{0,8},{8,0},{16,24},{24,16},{1,9},{9,1},{17,25},{25,17},{2,10},{10... | collective-permute-start | bytes 1105928 | tf_op jit(solution)/shard_map/ppermute | solution.py:803
  47.6 1.3 %collective-permute-done.35 = bf16[1440,128]{1,0:T(8,128)(2,1)S(1)} collective-permute-done((bf16[1440,128]{1,0:T(8,128)(2,1)S(1)}, bf16[1440,128]{1,0:T(8,128)(2,1)S(1)}, u32[]{:S(2)}, u32[]{:S(2)}) %collective-permute-start.35) | collective-permute-done | bytes 368672 | tf_op jit(solution)/shard_map/ppermute | solution.py:803
  48.9 0.1 add_convert_fusion
  49.0 0.8 dynamic-slice_bitcast_fusion.2
  49.8 0.2 collective-permute-start.36
  50.0 7.0 %collective-permute-start.38 = (bf16[336,128]{1,0:T(8,128)(2,1)S(1)}, bf16[336,128]{1,0:T(8,128)(2,1)}, u32[]{:S(2)}, u32[]{:S(2)}) collective-permute-start(bf16[336,128]{1,0:T(8,128)(2,1)S(1)} %get-tuple-element.295), channel_id=1, source_target_pairs={{0,17},{1,16},{2,19},{3,18},{4,21},{5,20},{6,23},{7,22},{8,25},{9,... | collective-permute-start | bytes 258056 | tf_op jit(solution)/shard_map/ppermute | solution.py:607
  57.0 7.4 %conditional.3 = (bf16[3,32,128]{2,1,0:T(8,128)(2,1)}, bf16[3,32,128]{2,1,0:T(8,128)(2,1)}, f32[4096,128]{1,0:T(8,128)S(1)}) conditional(s32[]{:T(128)} %bitcast, (bf16[3,32,128]{2,1,0:T(8,128)(2,1)}, bf16[3,32,128]{2,1,0:T(8,128)(2,1)}, bf16[4096,128]{1,0:T(8,128)(2,1)S(1)}, bf16[4096,128]{1,0:T(8,128)(2,1)}, ...), branch_computations={%region_8.9_spmd, %region_9.10_spmd, %region_10.11_spmd, %region_1... | conditional | flops 100000000 | bytes 31653992 | solution.py:776
  57.2 1.3 %collective-permute-start.26 = (bf16[3,32,128]{2,1,0:T(8,128)(2,1)}, bf16[3,32,128]{2,1,0:T(8,128)(2,1)}, u32[]{:S(2)}, u32[]{:S(2)}) collective-permute-start(bf16[3,32,128]{2,1,0:T(8,128)(2,1)} %get-tuple-element.193), channel_id=1, source_target_pairs={{8,16},{9,17},{10,18},{11,19},{12,20},{13,21},{14,22},{15,23},{16,... | collective-permute-start | bytes 73736 | tf_op jit(solution)/shard_map/cond/branch_5_fun/ppermute | solution.py:772
  58.5 1.2 %collective-permute-start.27 = (bf16[3,32,128]{2,1,0:T(8,128)(2,1)}, bf16[3,32,128]{2,1,0:T(8,128)(2,1)}, u32[]{:S(2)}, u32[]{:S(2)}) collective-permute-start(bf16[3,32,128]{2,1,0:T(8,128)(2,1)} %get-tuple-element.194), channel_id=1, source_target_pairs={{24,28},{25,27},{26,26},{27,25},{28,24},{29,31},{30,30},{31,29}} | collective-permute-start | bytes 73736 | tf_op jit(solution)/shard_map/cond/branch_5_fun/ppermute | solution.py:772
  59.7 4.7 %conv_back.13 = f32[4096,128]{1,0:T(8,128)S(1)} custom-call(bf16[4096,128]{1,0:T(8,128)(2,1)S(1)} %get-tuple-element.195.g, bf16[4096,128]{1,0:T(8,128)(2,1)} %get-tuple-element.196.dirin, bf16[49,128]{1,0:T(8,128)(2,1)S(1)} %get-tuple-element.197.dw), custom_call_target="tpu_custom_call" | custom-call | flops 100000000 | bytes 31457280 | tf_op jit(solution)/shard_map/cond/branch_5_fun/conv_back/pallas_call | solution.py:418
  64.4 0.7 slice.14
  65.2 1.1 %fusion.1 = bf16[336,128]{1,0:T(8,128)(2,1)S(1)} fusion(bf16[336,128]{1,0:T(8,128)(2,1)} %collective-permute-done.38, bf16[336,128]{1,0:T(8,128)(2,1)} %collective-permute-done.37, bf16[336,128]{1,0:T(8,128)(2,1)} %collective-permute-done.36, bf16[4,336,128]{2,1,0:T(8,128)(2,1)} %bitcast.22, s32[]{:T(128)S(6)} %select_n.26), kind=kLoop, calls=%fused_computation.4 | loop fusion | flops 344064 | bytes 430084 | tf_op jit(solution)/shard_map/convert_element_type | solution.py:582
  66.2 0.9 %join.3 = (bf16[3,32,128]{2,1,0:T(8,128)(2,1)S(1)}, bf16[3,32,128]{2,1,0:T(8,128)(2,1)S(1)}, bf16[416,128]{1,0:T(8,128)(2,1)S(1)}, bf16[416,128]{1,0:T(8,128)(2,1)S(1)}) custom-call(s32[2]{0:T(128)S(1)} %copy-done.5, bf16[3,32,128]{2,1,0:T(8,128)(2,1)S(1)} %bitcast.18, bf16[3,32,128]{2,1,0:T(8,128)(2,1)} %get-tuple-element.277.far, ...), custom_call_target="tpu_custom_call" | custom-call | tf_op jit(solution)/shard_map/join/pallas_call | solution.py:749
  67.2 3.4 %collective-permute-start.41 = (bf16[336,128]{1,0:T(8,128)(2,1)S(1)}, bf16[336,128]{1,0:T(8,128)(2,1)S(1)}, u32[]{:S(2)}, u32[]{:S(2)}) collective-permute-start(bf16[336,128]{1,0:T(8,128)(2,1)S(1)} %fusion.1), channel_id=1, source_target_pairs={{0,6},{1,7},{2,4},{3,5},{4,2},{5,3},{6,0},{7,1},{8,14},{9,15},{10,... | collective-permute-start | bytes 258056 | tf_op jit(solution)/shard_map/ppermute | solution.py:616
  70.5 1.1 %collective-permute-start.39 = (bf16[336,128]{1,0:T(8,128)(2,1)S(1)}, bf16[336,128]{1,0:T(8,128)(2,1)S(1)}, u32[]{:S(2)}, u32[]{:S(2)}) collective-permute-start(bf16[336,128]{1,0:T(8,128)(2,1)S(1)} %fusion.1), channel_id=1, source_target_pairs={{0,2},{1,3},{2,0},{3,1},{4,6},{5,7},{6,4},{7,5},{8,10},{9,11},{10,... | collective-permute-start | bytes 258056 | tf_op jit(solution)/shard_map/ppermute | solution.py:616
  71.6 4.4 %collective-permute-start.44 = (bf16[416,128]{1,0:T(8,128)(2,1)S(1)}, bf16[416,128]{1,0:T(8,128)(2,1)S(1)}, u32[]{:S(2)}, u32[]{:S(2)}) collective-permute-start(bf16[416,128]{1,0:T(8,128)(2,1)S(1)} %get-tuple-element.287), channel_id=1, source_target_pairs={{0,7},{1,0},{2,1},{3,2},{4,3},{5,4},{6,5},{7,6},{8,15},{9,8},{10,9... | collective-permute-start | bytes 319496 | tf_op jit(solution)/shard_map/ppermute | solution.py:814
  76.1 2.0 %collective-permute-done.40 = bf16[336,128]{1,0:T(8,128)(2,1)S(1)} collective-permute-done((bf16[336,128]{1,0:T(8,128)(2,1)S(1)}, bf16[336,128]{1,0:T(8,128)(2,1)S(1)}, u32[]{:S(2)}, u32[]{:S(2)}) %collective-permute-start.40) | collective-permute-done | bytes 86048 | tf_op jit(solution)/shard_map/ppermute | solution.py:616
  78.1 0.2 collective-permute-done.39
  78.3 1.5 %collective-permute-start.42 = (bf16[336,128]{1,0:T(8,128)(2,1)S(1)}, bf16[336,128]{1,0:T(8,128)(2,1)S(1)}, u32[]{:S(2)}, u32[]{:S(2)}) collective-permute-start(bf16[336,128]{1,0:T(8,128)(2,1)S(1)} %add_convert_fusion.1), channel_id=1, source_target_pairs={{0,1},{1,0},{2,3},{3,2},{4,5},{5,4},{6,7},{7,6},{8,9},{9,8},{10,11... | collective-permute-start | bytes 258056 | tf_op jit(solution)/shard_map/ppermute | solution.py:819
  79.8 2.4 %collective-permute-start.46 = (bf16[336,128]{1,0:T(8,128)(2,1)S(1)}, bf16[336,128]{1,0:T(8,128)(2,1)S(1)}, u32[]{:S(2)}, u32[]{:S(2)}) collective-permute-start(bf16[336,128]{1,0:T(8,128)(2,1)S(1)} %add_convert_fusion.1), channel_id=1, source_target_pairs={{0,17},{1,16},{2,19},{3,18},{4,21},{5,20},{6,23},{7,22},{8,25},{9,... | collective-permute-start | bytes 258056 | tf_op jit(solution)/shard_map/ppermute | solution.py:819
  82.2 2.6 %collective-permute-done.43.gl = bf16[416,128]{1,0:T(8,128)(2,1)S(1)} collective-permute-done((bf16[416,128]{1,0:T(8,128)(2,1)S(1)}, bf16[416,128]{1,0:T(8,128)(2,1)S(1)}, u32[]{:S(2)}, u32[]{:S(2)}) %collective-permute-start.43) | collective-permute-done | bytes 106528 | tf_op jit(solution)/shard_map/ppermute | solution.py:815
  84.8 3.7 %edges.1 = bf16[128,32,128]{2,1,0:T(8,128)(2,1)} custom-call(f32[4096,128]{1,0:T(8,128)S(1)} %get-tuple-element.283.base, bf16[3,32,128]{2,1,0:T(8,128)(2,1)S(1)} %get-tuple-element.284.south, bf16[3,32,128]{2,1,0:T(8,128)(2,1)S(1)} %get-tuple-element.285.north, bf16[416,128]{1,0:T(8,128)(2,1)S(1)} %collective-permute-done.43.gl, ...), custom_call_target="tpu_custom_call" | custom-call | flops 100000000 | bytes 10485760 | tf_op jit(solution)/shard_map/edges/pallas_call | solution.py:524
  88.6 0.7 collective-permute-start.47
  89.3 1.3 %collective-permute-done.47.other = bf16[4,336,128]{2,1,0:T(8,128)(2,1)S(1)} collective-permute-done((bf16[4,336,128]{2,1,0:T(8,128)(2,1)S(1)}, bf16[4,336,128]{2,1,0:T(8,128)(2,1)S(1)}, u32[]{:S(2)}, u32[]{:S(2)}) %collective-permute-start.47) | collective-permute-done | bytes 344096 | tf_op jit(solution)/shard_map/ppermute | solution.py:822
  90.6 1.4 %finish_sums.1 = (f32[49,128]{1,0:T(8,128)}, f32[128,512]{1,0:T(8,128)}, f32[512,128]{1,0:T(8,128)}, f32[3,512,128]{2,1,0:T(8,128)}) custom-call(bf16[4,336,128]{2,1,0:T(8,128)(2,1)S(1)} %pad_maximum_fusion.mine, bf16[4,336,128]{2,1,0:T(8,128)(2,1)S(1)} %collective-permute-done.47.other), custom_call_target="tpu_custom_call" | custom-call | tf_op jit(solution)/shard_map/finish_sums/pallas_call | solution.py:567
  (36 shorter events, 0.2 us)
Async XLA Ops:
  2.0 5.4 %collective-permute-start.32 = (bf16[3,32,128]{2,1,0:T(8,128)(2,1)}, bf16[3,32,128]{2,1,0:T(8,128)(2,1)S(1)}, u32[]{:S(2)}, u32[]{:S(2)}) collective-permute-start(bf16[3,32,128]{2,1,0:T(8,128)(2,1)} %get-tuple-element.255), channel_id=1, source_target_pairs={{0,8},{8,0},{16,24},{24,16},{1,9},{9,1},{17,25},{25,17},{2,10},{10... | collective-permute-start | bytes 73736 | tf_op jit(solution)/shard_map/ppermute | solution.py:792
  3.2 4.2 %copy-start.5 = (s32[2]{0:T(128)S(1)}, s32[2]{0:T(128)}, u32[]{:S(2)}) copy-start(s32[2]{0:T(128)} %get-tuple-element.254.place) | copy-start | bytes 28
  3.2 13.7 %copy-start = (bf16[3,512,128]{2,1,0:T(8,128)(2,1)S(1)}, bf16[3,512,128]{2,1,0:T(8,128)(2,1)}, u32[]{:S(2)}) copy-start(bf16[3,512,128]{2,1,0:T(8,128)(2,1)} %sw.1) | copy-start | bytes 1179652
  3.2 13.7 %copy-start.1 = (bf16[128,512]{1,0:T(8,128)(2,1)S(1)}, bf16[128,512]{1,0:T(8,128)(2,1)}, u32[]{:S(2)}) copy-start(bf16[128,512]{1,0:T(8,128)(2,1)} %upw.1) | copy-start | bytes 393220
  3.3 13.6 %copy-start.2 = (bf16[512,128]{1,0:T(8,128)(2,1)S(1)}, bf16[512,128]{1,0:T(8,128)(2,1)}, u32[]{:S(2)}) copy-start(bf16[512,128]{1,0:T(8,128)(2,1)} %down.1) | copy-start | bytes 393220
  3.3 13.6 %copy-start.3 = (s32[128,32]{0,1:T(8,128)S(1)}, s32[128,32]{0,1:T(8,128)}, u32[]{:S(2)}) copy-start(s32[128,32]{0,1:T(8,128)} %param.30) | copy-start | bytes 49156
  3.3 13.6 %copy-start.4 = (bf16[16,4,128]{2,1,0:T(4,128)(2,1)S(1)}, bf16[16,4,128]{2,1,0:T(4,128)(2,1)}, u32[]{:S(2)}) copy-start(bf16[16,4,128]{2,1,0:T(4,128)(2,1)} %cot.1) | copy-start | bytes 49156
  3.3 13.6 %copy-start.6 = (bf16[512]{0:T(512)(128)(2,1)S(1)}, bf16[512]{0:T(512)(128)(2,1)}, u32[]{:S(2)}) copy-start(bf16[512]{0:T(512)(128)(2,1)} %bias.1) | copy-start | bytes 3076
  3.3 13.6 %copy-start.7 = (bf16[3,128]{1,0:T(4,128)(2,1)S(1)}, bf16[3,128]{1,0:T(4,128)(2,1)}, u32[]{:S(2)}) copy-start(bf16[3,128]{1,0:T(4,128)(2,1)} %sgain.1) | copy-start | bytes 2308
  3.3 13.6 %copy-start.8 = (bf16[3,128]{1,0:T(4,128)(2,1)S(1)}, bf16[3,128]{1,0:T(4,128)(2,1)}, u32[]{:S(2)}) copy-start(bf16[3,128]{1,0:T(4,128)(2,1)} %sbias.1) | copy-start | bytes 2308
  3.3 13.6 %copy-start.9 = (bf16[128]{0:T(256)(128)(2,1)S(1)}, bf16[128]{0:T(256)(128)(2,1)}, u32[]{:S(2)}) copy-start(bf16[128]{0:T(256)(128)(2,1)} %gain.1) | copy-start | bytes 772
  3.3 13.6 %copy-start.10 = (bf16[128]{0:T(256)(128)(2,1)S(1)}, bf16[128]{0:T(256)(128)(2,1)}, u32[]{:S(2)}) copy-start(bf16[128]{0:T(256)(128)(2,1)} %scale.1) | copy-start | bytes 772
  3.4 13.6 %copy-start.11 = (bf16[49,128]{1,0:T(8,128)(2,1)S(1)}, bf16[49,128]{1,0:T(8,128)(2,1)}, u32[]{:S(2)}) copy-start(bf16[49,128]{1,0:T(8,128)(2,1)} %dw.3) | copy-start | bytes 37636
  3.4 4.0 %collective-permute-start.10 = (bf16[3,32,128]{2,1,0:T(8,128)(2,1)S(1)}, bf16[3,32,128]{2,1,0:T(8,128)(2,1)}, u32[]{:S(2)}, u32[]{:S(2)}) collective-permute-start(bf16[3,32,128]{2,1,0:T(8,128)(2,1)S(1)} %get-tuple-element.153), channel_id=1, source_target_pairs={{8,16},{9,17},{10,18},{11,19},{12,20},{13,21},{14,22},{15,23},{16,... | collective-permute-start | bytes 73736 | tf_op jit(solution)/shard_map/cond/branch_5_fun/ppermute | solution.py:772
  4.8 2.6 %collective-permute-start.11 = (bf16[3,32,128]{2,1,0:T(8,128)(2,1)S(1)}, bf16[3,32,128]{2,1,0:T(8,128)(2,1)}, u32[]{:S(2)}, u32[]{:S(2)}) collective-permute-start(bf16[3,32,128]{2,1,0:T(8,128)(2,1)S(1)} %get-tuple-element.154), channel_id=1, source_target_pairs={{24,28},{25,27},{26,26},{27,25},{28,24},{29,31},{30,30},{31,29}} | collective-permute-start | bytes 73736 | tf_op jit(solution)/shard_map/cond/branch_5_fun/ppermute | solution.py:772
  8.4 8.4 %collective-permute-start.33 = (bf16[3,134,128]{2,1,0:T(8,128)(2,1)S(1)}, bf16[3,134,128]{2,1,0:T(8,128)(2,1)S(1)}, u32[]{:S(2)}, u32[]{:S(2)}) collective-permute-start(bf16[3,134,128]{2,1,0:T(8,128)(2,1)S(1)} %get-tuple-element.264), channel_id=1, source_target_pairs={{0,1},{1,2},{2,3},{3,4},{4,5},{5,6},{6,7},{7,0},{8,9},{9,10},{10,1... | collective-permute-start | bytes 308744 | tf_op jit(solution)/shard_map/ppermute | solution.py:796
  11.0 5.9 %collective-permute-start.34 = (bf16[3,134,128]{2,1,0:T(8,128)(2,1)S(1)}, bf16[3,134,128]{2,1,0:T(8,128)(2,1)S(1)}, u32[]{:S(2)}, u32[]{:S(2)}) collective-permute-start(bf16[3,134,128]{2,1,0:T(8,128)(2,1)S(1)} %get-tuple-element.265), channel_id=1, source_target_pairs={{0,7},{1,0},{2,1},{3,2},{4,3},{5,4},{6,5},{7,6},{8,15},{9,8},{10,9... | collective-permute-start | bytes 308744 | tf_op jit(solution)/shard_map/ppermute | solution.py:795
  45.6 3.3 %collective-permute-start.35 = (bf16[1440,128]{1,0:T(8,128)(2,1)S(1)}, bf16[1440,128]{1,0:T(8,128)(2,1)S(1)}, u32[]{:S(2)}, u32[]{:S(2)}) collective-permute-start(bf16[1440,128]{1,0:T(8,128)(2,1)S(1)} %get-tuple-element.269), channel_id=1, source_target_pairs={{0,8},{8,0},{16,24},{24,16},{1,9},{9,1},{17,25},{25,17},{2,10},{10... | collective-permute-start | bytes 1105928 | tf_op jit(solution)/shard_map/ppermute | solution.py:803
  48.9 8.1 %copy-start.13 = (bf16[1440,128]{1,0:T(8,128)(2,1)}, bf16[1440,128]{1,0:T(8,128)(2,1)S(1)}, u32[]{:S(2)}) copy-start(bf16[1440,128]{1,0:T(8,128)(2,1)S(1)} %collective-permute-done.35) | copy-start | bytes 1105924
  49.0 8.0 %copy-start.12 = (bf16[1344,128]{1,0:T(8,128)(2,1)}, bf16[1344,128]{1,0:T(8,128)(2,1)S(1)}, u32[]{:S(2)}) copy-start(bf16[1344,128]{1,0:T(8,128)(2,1)S(1)} %add_convert_fusion) | copy-start | bytes 1032196
  49.8 15.4 %collective-permute-start.36 = (bf16[336,128]{1,0:T(8,128)(2,1)}, bf16[336,128]{1,0:T(8,128)(2,1)}, u32[]{:S(2)}, u32[]{:S(2)}) collective-permute-start(bf16[336,128]{1,0:T(8,128)(2,1)} %get-tuple-element.294), channel_id=1, source_target_pairs={{0,1},{1,0},{2,3},{3,2},{4,5},{5,4},{6,7},{7,6},{8,9},{9,8},{10,11... | collective-permute-start | bytes 258056 | tf_op jit(solution)/shard_map/ppermute | solution.py:607
  50.0 15.2 %collective-permute-start.38 = (bf16[336,128]{1,0:T(8,128)(2,1)S(1)}, bf16[336,128]{1,0:T(8,128)(2,1)}, u32[]{:S(2)}, u32[]{:S(2)}) collective-permute-start(bf16[336,128]{1,0:T(8,128)(2,1)S(1)} %get-tuple-element.295), channel_id=1, source_target_pairs={{0,17},{1,16},{2,19},{3,18},{4,21},{5,20},{6,23},{7,22},{8,25},{9,... | collective-permute-start | bytes 258056 | tf_op jit(solution)/shard_map/ppermute | solution.py:607
  57.0 8.2 %collective-permute-start.37 = (bf16[336,128]{1,0:T(8,128)(2,1)S(1)}, bf16[336,128]{1,0:T(8,128)(2,1)}, u32[]{:S(2)}, u32[]{:S(2)}) collective-permute-start(bf16[336,128]{1,0:T(8,128)(2,1)S(1)} %get-tuple-element.296), channel_id=1, source_target_pairs={{0,16},{1,17},{2,18},{3,19},{4,20},{5,21},{6,22},{7,23},{8,24},{9,... | collective-permute-start | bytes 258056 | tf_op jit(solution)/shard_map/ppermute | solution.py:607
  57.2 7.2 %collective-permute-start.26 = (bf16[3,32,128]{2,1,0:T(8,128)(2,1)}, bf16[3,32,128]{2,1,0:T(8,128)(2,1)}, u32[]{:S(2)}, u32[]{:S(2)}) collective-permute-start(bf16[3,32,128]{2,1,0:T(8,128)(2,1)} %get-tuple-element.193), channel_id=1, source_target_pairs={{8,16},{9,17},{10,18},{11,19},{12,20},{13,21},{14,22},{15,23},{16,... | collective-permute-start | bytes 73736 | tf_op jit(solution)/shard_map/cond/branch_5_fun/ppermute | solution.py:772
  58.5 5.9 %collective-permute-start.27 = (bf16[3,32,128]{2,1,0:T(8,128)(2,1)}, bf16[3,32,128]{2,1,0:T(8,128)(2,1)}, u32[]{:S(2)}, u32[]{:S(2)}) collective-permute-start(bf16[3,32,128]{2,1,0:T(8,128)(2,1)} %get-tuple-element.194), channel_id=1, source_target_pairs={{24,28},{25,27},{26,26},{27,25},{28,24},{29,31},{30,30},{31,29}} | collective-permute-start | bytes 73736 | tf_op jit(solution)/shard_map/cond/branch_5_fun/ppermute | solution.py:772
  67.2 8.9 %collective-permute-start.41 = (bf16[336,128]{1,0:T(8,128)(2,1)S(1)}, bf16[336,128]{1,0:T(8,128)(2,1)S(1)}, u32[]{:S(2)}, u32[]{:S(2)}) collective-permute-start(bf16[336,128]{1,0:T(8,128)(2,1)S(1)} %fusion.1), channel_id=1, source_target_pairs={{0,6},{1,7},{2,4},{3,5},{4,2},{5,3},{6,0},{7,1},{8,14},{9,15},{10,... | collective-permute-start | bytes 258056 | tf_op jit(solution)/shard_map/ppermute | solution.py:616
  70.5 7.5 %collective-permute-start.40 = (bf16[336,128]{1,0:T(8,128)(2,1)S(1)}, bf16[336,128]{1,0:T(8,128)(2,1)S(1)}, u32[]{:S(2)}, u32[]{:S(2)}) collective-permute-start(bf16[336,128]{1,0:T(8,128)(2,1)S(1)} %fusion.1), channel_id=1, source_target_pairs={{0,4},{1,5},{2,6},{3,7},{4,0},{5,1},{6,2},{7,3},{8,12},{9,13},{10,... | collective-permute-start | bytes 258056 | tf_op jit(solution)/shard_map/ppermute | solution.py:616
  70.5 7.7 %collective-permute-start.39 = (bf16[336,128]{1,0:T(8,128)(2,1)S(1)}, bf16[336,128]{1,0:T(8,128)(2,1)S(1)}, u32[]{:S(2)}, u32[]{:S(2)}) collective-permute-start(bf16[336,128]{1,0:T(8,128)(2,1)S(1)} %fusion.1), channel_id=1, source_target_pairs={{0,2},{1,3},{2,0},{3,1},{4,6},{5,7},{6,4},{7,5},{8,10},{9,11},{10,... | collective-permute-start | bytes 258056 | tf_op jit(solution)/shard_map/ppermute | solution.py:616
  71.6 10.6 %collective-permute-start.44 = (bf16[416,128]{1,0:T(8,128)(2,1)S(1)}, bf16[416,128]{1,0:T(8,128)(2,1)S(1)}, u32[]{:S(2)}, u32[]{:S(2)}) collective-permute-start(bf16[416,128]{1,0:T(8,128)(2,1)S(1)} %get-tuple-element.287), channel_id=1, source_target_pairs={{0,7},{1,0},{2,1},{3,2},{4,3},{5,4},{6,5},{7,6},{8,15},{9,8},{10,9... | collective-permute-start | bytes 319496 | tf_op jit(solution)/shard_map/ppermute | solution.py:814
  76.1 8.7 %collective-permute-start.43 = (bf16[416,128]{1,0:T(8,128)(2,1)S(1)}, bf16[416,128]{1,0:T(8,128)(2,1)S(1)}, u32[]{:S(2)}, u32[]{:S(2)}) collective-permute-start(bf16[416,128]{1,0:T(8,128)(2,1)S(1)} %get-tuple-element.286), channel_id=1, source_target_pairs={{0,1},{1,2},{2,3},{3,4},{4,5},{5,6},{6,7},{7,0},{8,9},{9,10},{10,1... | collective-permute-start | bytes 319496 | tf_op jit(solution)/shard_map/ppermute | solution.py:815
  78.3 10.2 %collective-permute-start.42 = (bf16[336,128]{1,0:T(8,128)(2,1)S(1)}, bf16[336,128]{1,0:T(8,128)(2,1)S(1)}, u32[]{:S(2)}, u32[]{:S(2)}) collective-permute-start(bf16[336,128]{1,0:T(8,128)(2,1)S(1)} %add_convert_fusion.1), channel_id=1, source_target_pairs={{0,1},{1,0},{2,3},{3,2},{4,5},{5,4},{6,7},{7,6},{8,9},{9,8},{10,11... | collective-permute-start | bytes 258056 | tf_op jit(solution)/shard_map/ppermute | solution.py:819
  79.8 8.7 %collective-permute-start.46 = (bf16[336,128]{1,0:T(8,128)(2,1)S(1)}, bf16[336,128]{1,0:T(8,128)(2,1)S(1)}, u32[]{:S(2)}, u32[]{:S(2)}) collective-permute-start(bf16[336,128]{1,0:T(8,128)(2,1)S(1)} %add_convert_fusion.1), channel_id=1, source_target_pairs={{0,17},{1,16},{2,19},{3,18},{4,21},{5,20},{6,23},{7,22},{8,25},{9,... | collective-permute-start | bytes 258056 | tf_op jit(solution)/shard_map/ppermute | solution.py:819
  82.2 6.3 %collective-permute-start.45 = (bf16[336,128]{1,0:T(8,128)(2,1)S(1)}, bf16[336,128]{1,0:T(8,128)(2,1)S(1)}, u32[]{:S(2)}, u32[]{:S(2)}) collective-permute-start(bf16[336,128]{1,0:T(8,128)(2,1)S(1)} %add_convert_fusion.1), channel_id=1, source_target_pairs={{0,16},{1,17},{2,18},{3,19},{4,20},{5,21},{6,22},{7,23},{8,24},{9,... | collective-permute-start | bytes 258056 | tf_op jit(solution)/shard_map/ppermute | solution.py:819
  88.6 2.0 %collective-permute-start.47 = (bf16[4,336,128]{2,1,0:T(8,128)(2,1)S(1)}, bf16[4,336,128]{2,1,0:T(8,128)(2,1)S(1)}, u32[]{:S(2)}, u32[]{:S(2)}) collective-permute-start(bf16[4,336,128]{2,1,0:T(8,128)(2,1)S(1)} %pad_maximum_fusion.mine), channel_id=1, source_target_pairs={{0,8},{8,0},{16,24},{24,16},{1,9},{9,1},{17,25},{25,17},{2,10},{10... | collective-permute-start | bytes 1032200 | tf_op jit(solution)/shard_map/ppermute | solution.py:822

commit v4 on v3

--- a/solution.py
+++ b/solution.py
@@ -149,7 +149,7 @@
     g_n = gain[...].astype(f32).reshape(1, 128)
     sc = scale[...].astype(f32).reshape(1, 128)
     sg0 = sgain[0:1, :].astype(f32)
-    T1 = n0 // 2
+    T1 = n0
 
     def nfwd(n, _):
         base = pl.multiple_of(n * T1, T1)
@@ -266,7 +266,7 @@
         mgs[pl.ds(base, TP), :] = (dr * sc).astype(bf16)
         return 0
 
-    lax.fori_loop(0, I // 2, bk1, 0, unroll=2)
+    lax.fori_loop(0, I // 2, bk1, 0, unroll=4)
 
     def bk2(n, _):
         base = pl.multiple_of(n * T2, T2)
@@ -407,7 +407,7 @@
 
     def emit(i, c, v):
         at = pl.multiple_of((i * CW + c) * S, S)
-        out[pl.ds(at, S), :] = v + dirin[pl.ds(at, S), :].astype(f32)
+        out[pl.ds(at, S), :] = (v + dirin[pl.ds(at, S), :].astype(f32)).astype(bf16)
 
     conv49(gext, w49, emit, I, CW)
 
@@ -417,7 +417,7 @@
     I = R // S
     return pl.pallas_call(
         functools.partial(conv_back_body, R, CW),
-        out_shape=jax.ShapeDtypeStruct((R * CW, C), f32),
+        out_shape=jax.ShapeDtypeStruct((R * CW, C), bf16),
         in_specs=[VMEM] * 3,
         out_specs=VMEM,
         scratch_shapes=[
@@ -487,7 +487,7 @@
 
     def step(i, _):
         at = pl.multiple_of(i * PITCH, PITCH)
-        acc[pl.ds(at, PITCH), :] = base[pl.ds(at, PITCH), :]
+        acc[pl.ds(at, PITCH), :] = base[pl.ds(at, PITCH), :].astype(f32)
         for side in range(2):
             for t in range(3):
                 s = None
@@ -717,8 +717,9 @@
     for k in range(3):
         m = 2 - k if flip else k
         beyond = scr[m * CW : (m + 1) * CW, :]
-        above = jnp.where(odd, far[k].astype(f32), near[k].astype(f32))
-        below = jnp.where(odd, near[k].astype(f32), far[k].astype(f32))
+        close = (near[k] if flip else near[HALF + k * CW : HALF + (k + 1) * CW, :]).astype(f32)
+        above = jnp.where(odd, far[k].astype(f32), close)
+        below = jnp.where(odd, close, far[k].astype(f32))
         above = jnp.where(top, beyond, above)
         south[k] = below.astype(bf16)
         north[k] = above.astype(bf16)
@@ -742,7 +743,7 @@
 
 
 def join(place, near, far, blk_b, lc, rc, flip):
-    CW, C = near.shape[1:]
+    CW, C = far.shape[1:]
     width = lc.shape[1] if flip else lc.shape[0]
     sd = jax.ShapeDtypeStruct
     pay = sd((3, width + 6, C) if flip else (width + 32, C), bf16)
@@ -801,7 +802,6 @@
 
     place = (lax.axis_index("lat") // 2) * 2 + lax.axis_index("lon") % 2
     got = lax.ppermute(away, "lat", flip_pairs("lat", 1))
-    near = got[HALF:].reshape(3, CW, C)
     held = add_bf(keep, got[:HALF]).reshape(4, HALF // 4, C)
     send, held = lax.optimization_barrier((send, held))
     chunk = square_sum(held, place)
@@ -809,7 +809,7 @@
         send, last, shift[0], lambda: conv_back(g, direct, depth_weight, R, CW)
     )
     chunk, far = lax.optimization_barrier((chunk, far))
-    south_g, north_g, lpay, rpay = join(shift, near, far, blk_b, lcol, rcol, False)
+    south_g, north_g, lpay, rpay = join(shift, got, far, blk_b, lcol, rcol, False)
     chunk, lpay = lax.optimization_barrier((chunk, lpay))
     gr = lax.ppermute(lpay, "lon", shift_pairs("lon", -1))
     gl = lax.ppermute(rpay, "lon", shift_pairs("lon", 1))

time: 93.3 us -> 87.8 us (0.941)
  Pallas kernels: 43.1 us -> 41.5 us
  waiting for transfers between devices: 10.2 us -> 8.79 us
  starting transfers between devices: 33.9 us -> 32.6 us
    ppermute x1, waiting for transfers between devices: 2.58 us -> 0.01 us  [on_device(): gl = lax.ppermute(rpay, 'lon', shift_pairs('lon', 1))]
    ppermute x3, starting transfers between devices: 7.18 us -> 5.28 us  [square_sum(): came.append(lax.ppermute(part, ('lat', 'lon'), square_pairs(k)))]
    ppermute x3, waiting for transfers between devices: 0.01 us -> 1.56 us  [on_device(): back = [lax.ppermute(chunk, axes, square_pairs(k)) for k in (1, 2, 3)]]
    unnamed x28 -> x32, local copies, waits for them, and re-layouts: 0.08 us -> 1.34 us
    ppermute x1, starting transfers between devices: 0.01 us -> 1.26 us  [on_device(): gl = lax.ppermute(rpay, 'lon', shift_pairs('lon', 1))]
    pallas_call x1, Pallas kernels: 4.67 us -> 3.55 us  [conv_back(): pl.pallas_call(functools.partial(conv_back_body, R, CW), out_shape=jax.Sh...]
    ppermute x1, starting transfers between devices: 4.44 us -> 3.46 us  [on_device(): gr = lax.ppermute(lpay, 'lon', shift_pairs('lon', -1))]
  transfers between devices with their start and end apart: 20 -> 20, of which waited for: 7 -> 7; matrix products, arithmetic and copies ran while one was open for 1% -> 0% of each run, Pallas kernels for 11% -> 10%
where the time goes in v4:
time: 87.8 us; the launch traced here: 86.6 us
  Pallas kernels  41.5 us (47%)
  starting transfers between devices  32.6 us (37%)
  waiting for transfers between devices  8.79 us (10%)
  local copies, waits for them, and re-layouts  1.37 us (2%)
  other arithmetic  1.25 us (1%)
  between operations  0.95 us (1%)
    pallas_call x1, Pallas kernels, block_pass(): pl.pallas_call(functools.partial(block_body, R, CW), out_shape=out_shape,...  28.1 us
    ppermute x3, starting transfers between devices, square_sum(): came.append(lax.ppermute(part, ('lat', 'lon'), square_pairs(k)))  5.28 us
    ppermute x3, starting transfers between devices, line_sum(): lax.ppermute(total, 'lon', flip_pairs('lon', bit * k))  4.44 us
    ppermute x3, starting transfers between devices, on_device(): back = [lax.ppermute(chunk, axes, square_pairs(k)) for k in (1, 2, 3)]  4.24 us
    pallas_call x1, Pallas kernels, edges(): pl.pallas_call(functools.partial(edges_body, R, CW), out_shape=jax.ShapeD...  3.74 us
    pallas_call x1, Pallas kernels, conv_back(): pl.pallas_call(functools.partial(conv_back_body, R, CW), out_shape=jax.Sh...  3.55 us
    ppermute x1, starting transfers between devices, on_device(): gr = lax.ppermute(lpay, 'lon', shift_pairs('lon', -1))  3.46 us
    ppermute x1, starting transfers between devices, on_device(): right_f = lax.ppermute(lpay, 'lon', shift_pairs('lon', -1))  3.28 us
  transfers between devices with their start and end apart: 20, of which 7 were waited for; matrix products, arithmetic and copies ran while one was open for 0% of the time, Pallas kernels for 10%

profile of v4, /device:TPU:0, one launch (start us, length us, event | category | flops | bytes accessed | tf_op | source)
XLA Modules:
  0.0 86.6 jit_solution(9021568382327557997)
XLA Ops:
  0.6 1.4 %rim.1 = (bf16[3,32,128]{2,1,0:T(8,128)(2,1)}, bf16[3,32,128]{2,1,0:T(8,128)(2,1)S(1)}, bf16[3,32,128]{2,1,0:T(8,128)(2,1)S(1)}, s32[2]{0:T(128)}) custom-call(bf16[128,32,128]{2,1,0:T(8,128)(2,1)} %field.3, s32[256]{0:T(256)} %mirror.1), custom_call_target="tpu_custom_call" | custom-call | tf_op jit(solution)/shard_map/rim/pallas_call | solution.py:655
  2.0 0.5 collective-permute-start.32
  2.6 0.7 copy-done.5
  3.3 0.0 copy-start
  3.3 0.0 copy-start.4
  3.3 0.0 copy-start.10
  3.3 0.0 copy-start.13
  3.3 4.1 %conditional.2 = (bf16[3,32,128]{2,1,0:T(8,128)(2,1)}, bf16[3,32,128]{2,1,0:T(8,128)(2,1)}, bf16[3,128,128]{2,1,0:T(8,128)(2,1)S(1)}, bf16[3,128,128]{2,1,0:T(8,128)(2,1)S(1)}) conditional(s32[]{:T(128)} %bitcast, (bf16[3,32,128]{2,1,0:T(8,128)(2,1)S(1)}, bf16[3,32,128]{2,1,0:T(8,128)(2,1)S(1)}, ...), branch_computations={%region_0.0_spmd, %region_1.0_spmd, %region_2.0_spmd, %region_3.0_... | conditional | bytes 196720 | solution.py:777
  3.4 1.4 %collective-permute-start.6 = (bf16[3,32,128]{2,1,0:T(8,128)(2,1)S(1)}, bf16[3,32,128]{2,1,0:T(8,128)(2,1)}, u32[]{:S(2)}, u32[]{:S(2)}) collective-permute-start(bf16[3,32,128]{2,1,0:T(8,128)(2,1)S(1)} %get-tuple-element.143), channel_id=1, source_target_pairs={{8,16},{9,17},{10,18},{11,19},{12,20},{13,21},{14,22},{15,23},{16,... | collective-permute-start | bytes 73736 | tf_op jit(solution)/shard_map/cond/branch_3_fun/ppermute | solution.py:773
  4.8 1.3 %collective-permute-start.7 = (bf16[3,32,128]{2,1,0:T(8,128)(2,1)S(1)}, bf16[3,32,128]{2,1,0:T(8,128)(2,1)}, u32[]{:S(2)}, u32[]{:S(2)}) collective-permute-start(bf16[3,32,128]{2,1,0:T(8,128)(2,1)S(1)} %get-tuple-element.144), channel_id=1, source_target_pairs={{24,26},{25,25},{26,24},{27,31},{28,30},{29,29},{30,28},{31,27}} | collective-permute-start | bytes 73736 | tf_op jit(solution)/shard_map/cond/branch_3_fun/ppermute | solution.py:773
  6.0 1.3 %sides.11 = (bf16[3,128,128]{2,1,0:T(8,128)(2,1)S(1)}, bf16[3,128,128]{2,1,0:T(8,128)(2,1)S(1)}) custom-call(bf16[128,32,128]{2,1,0:T(8,128)(2,1)} %get-tuple-element.145.field), custom_call_target="tpu_custom_call" | custom-call | tf_op jit(solution)/shard_map/cond/branch_3_fun/sides/pallas_call | solution.py:690
  7.4 0.0 copy-start.1
  7.5 1.0 %join.2 = (bf16[3,32,128]{2,1,0:T(8,128)(2,1)S(1)}, bf16[3,32,128]{2,1,0:T(8,128)(2,1)S(1)}, bf16[3,134,128]{2,1,0:T(8,128)(2,1)S(1)}, bf16[3,134,128]{2,1,0:T(8,128)(2,1)S(1)}) custom-call(s32[2]{0:T(128)S(1)} %copy-done.5, bf16[3,32,128]{2,1,0:T(8,128)(2,1)S(1)} %collective-permute-done.32.near, bf16[3,32,128]{2,1,0:T(8,128)(2,1)} %get-tuple-element.258.far, ...), custom_call_target="tpu_custom_call" | custom-call | tf_op jit(solution)/shard_map/join/pallas_call | solution.py:750
  8.5 2.6 %collective-permute-start.33 = (bf16[3,134,128]{2,1,0:T(8,128)(2,1)S(1)}, bf16[3,134,128]{2,1,0:T(8,128)(2,1)S(1)}, u32[]{:S(2)}, u32[]{:S(2)}) collective-permute-start(bf16[3,134,128]{2,1,0:T(8,128)(2,1)S(1)} %get-tuple-element.264), channel_id=1, source_target_pairs={{0,1},{1,2},{2,3},{3,4},{4,5},{5,6},{6,7},{7,0},{8,9},{9,10},{10,1... | collective-permute-start | bytes 308744 | tf_op jit(solution)/shard_map/ppermute | solution.py:797
  11.1 3.3 %collective-permute-start.34 = (bf16[3,134,128]{2,1,0:T(8,128)(2,1)S(1)}, bf16[3,134,128]{2,1,0:T(8,128)(2,1)S(1)}, u32[]{:S(2)}, u32[]{:S(2)}) collective-permute-start(bf16[3,134,128]{2,1,0:T(8,128)(2,1)S(1)} %get-tuple-element.265), channel_id=1, source_target_pairs={{0,7},{1,0},{2,1},{3,2},{4,3},{5,4},{6,5},{7,6},{8,15},{9,8},{10,9... | collective-permute-start | bytes 308744 | tf_op jit(solution)/shard_map/ppermute | solution.py:796
  14.4 2.5 %collective-permute-done.33.left = bf16[3,134,128]{2,1,0:T(8,128)(2,1)S(1)} collective-permute-done((bf16[3,134,128]{2,1,0:T(8,128)(2,1)S(1)}, bf16[3,134,128]{2,1,0:T(8,128)(2,1)S(1)}, u32[]{:S(2)}, u32[]{:S(2)}) %collective-permute-start.33) | collective-permute-done | bytes 102944 | tf_op jit(solution)/shard_map/ppermute | solution.py:797
  16.9 0.1 collective-permute-done.34.right
  17.1 0.6 copy-done.6
  17.7 28.1 %block_pass.1 = (bf16[16,4,128]{2,1,0:T(4,128)(2,1)}, bf16[4096,128]{1,0:T(8,128)(2,1)S(1)}, bf16[4096,128]{1,0:T(8,128)(2,1)S(1)}, bf16[3,32,128]{2,1,0:T(8,128...) custom-call(bf16[128,32,128]{2,1,0:T(8,128)(2,1)} %field.3, ...), custom_call_target="tpu_custom_call" | custom-call | tf_op jit(solution)/shard_map/block_pass/pallas_call | solution.py:372
  45.7 1.9 %collective-permute-start.35 = (bf16[1440,128]{1,0:T(8,128)(2,1)S(1)}, bf16[1440,128]{1,0:T(8,128)(2,1)S(1)}, u32[]{:S(2)}, u32[]{:S(2)}) collective-permute-start(bf16[1440,128]{1,0:T(8,128)(2,1)S(1)} %get-tuple-element.269), channel_id=1, source_target_pairs={{0,8},{8,0},{16,24},{24,16},{1,9},{9,1},{17,25},{25,17},{2,10},{10... | collective-permute-start | bytes 1105928 | tf_op jit(solution)/shard_map/ppermute | solution.py:804
  47.7 1.3 %collective-permute-done.35.near = bf16[1440,128]{1,0:T(8,128)(2,1)S(1)} collective-permute-done((bf16[1440,128]{1,0:T(8,128)(2,1)S(1)}, bf16[1440,128]{1,0:T(8,128)(2,1)S(1)}, u32[]{:S(2)}, u32[]{:S(2)}) %collective-permute-start.35) | collective-permute-done | bytes 368672 | tf_op jit(solution)/shard_map/ppermute | solution.py:804
  49.0 0.1 add_convert_fusion
  49.1 0.0 copy-start.14
  49.1 0.0 copy-start.15
  49.2 3.1 %collective-permute-start.38 = (bf16[336,128]{1,0:T(8,128)(2,1)S(1)}, bf16[336,128]{1,0:T(8,128)(2,1)S(1)}, u32[]{:S(2)}, u32[]{:S(2)}) collective-permute-start(bf16[336,128]{1,0:T(8,128)(2,1)S(1)} %get-tuple-element.295), channel_id=1, source_target_pairs={{0,17},{1,16},{2,19},{3,18},{4,21},{5,20},{6,23},{7,22},{8,25},{9,... | collective-permute-start | bytes 258056 | tf_op jit(solution)/shard_map/ppermute | solution.py:607
  52.3 0.8 collective-permute-start.37
  53.1 1.4 %collective-permute-start.36 = (bf16[336,128]{1,0:T(8,128)(2,1)S(1)}, bf16[336,128]{1,0:T(8,128)(2,1)}, u32[]{:S(2)}, u32[]{:S(2)}) collective-permute-start(bf16[336,128]{1,0:T(8,128)(2,1)S(1)} %get-tuple-element.294), channel_id=1, source_target_pairs={{0,1},{1,0},{2,3},{3,2},{4,5},{5,4},{6,7},{7,6},{8,9},{9,8},{10,11... | collective-permute-start | bytes 258056 | tf_op jit(solution)/shard_map/ppermute | solution.py:607
  54.5 6.1 %conditional.3 = (bf16[3,32,128]{2,1,0:T(8,128)(2,1)}, bf16[3,32,128]{2,1,0:T(8,128)(2,1)}, bf16[4096,128]{1,0:T(8,128)(2,1)S(1)}) conditional(s32[]{:T(128)} %bitcast, (bf16[3,32,128]{2,1,0:T(8,128)(2,1)S(1)}, bf16[3,32,128]{2,1,0:T(8,128)(2,1)S(1)}, bf16[4096,128]{1,0:T(8,128)(2,1)S(1)}, ...), branch_computations={%region_8.9_spmd, %region_9.10_spmd, %region_10.11_spmd, %region_1... | conditional | flops 100000000 | bytes 31653992 | solution.py:777
  54.5 1.2 %collective-permute-start.22 = (bf16[3,32,128]{2,1,0:T(8,128)(2,1)S(1)}, bf16[3,32,128]{2,1,0:T(8,128)(2,1)}, u32[]{:S(2)}, u32[]{:S(2)}) collective-permute-start(bf16[3,32,128]{2,1,0:T(8,128)(2,1)S(1)} %get-tuple-element.183), channel_id=1, source_target_pairs={{8,16},{9,17},{10,18},{11,19},{12,20},{13,21},{14,22},{15,23},{16,... | collective-permute-start | bytes 73736 | tf_op jit(solution)/shard_map/cond/branch_3_fun/ppermute | solution.py:773
  55.7 1.3 %collective-permute-start.23 = (bf16[3,32,128]{2,1,0:T(8,128)(2,1)S(1)}, bf16[3,32,128]{2,1,0:T(8,128)(2,1)}, u32[]{:S(2)}, u32[]{:S(2)}) collective-permute-start(bf16[3,32,128]{2,1,0:T(8,128)(2,1)S(1)} %get-tuple-element.184), channel_id=1, source_target_pairs={{24,26},{25,25},{26,24},{27,31},{28,30},{29,29},{30,28},{31,27}} | collective-permute-start | bytes 73736 | tf_op jit(solution)/shard_map/cond/branch_3_fun/ppermute | solution.py:773
  57.0 3.5 %conv_back.11 = bf16[4096,128]{1,0:T(8,128)(2,1)S(1)} custom-call(bf16[4096,128]{1,0:T(8,128)(2,1)S(1)} %get-tuple-element.185.g, bf16[4096,128]{1,0:T(8,128)(2,1)S(1)} %get-tuple-element.186.dirin, bf16[49,128]{1,0:T(8,128)(2,1)S(1)} %get-tuple-element.187.dw), custom_call_target="tpu_custom_call" | custom-call | flops 100000000 | bytes 31457280 | tf_op jit(solution)/shard_map/cond/branch_3_fun/conv_back/pallas_call | solution.py:418
  60.5 0.0 copy-start.11
  60.6 1.1 %fusion.1 = bf16[336,128]{1,0:T(8,128)(2,1)S(1)} fusion(bf16[336,128]{1,0:T(8,128)(2,1)S(1)} %collective-permute-done.38, bf16[336,128]{1,0:T(8,128)(2,1)S(1)} %collective-permute-done.37, bf16[336,128]{1,0:T(8,128)(2,1)} %collective-permute-done.36, bf16[4,336,128]{2,1,0:T(8,128)(2,1)S(1)} %bitcast.20, s32[]{:T(128)S(6)} %select_n.26), kind=kLoop, calls=%fused_computation.4 | loop fusion | flops 344064 | bytes 430084 | tf_op jit(solution)/shard_map/convert_element_type | solution.py:582
  61.7 1.0 %join.3 = (bf16[3,32,128]{2,1,0:T(8,128)(2,1)S(1)}, bf16[3,32,128]{2,1,0:T(8,128)(2,1)S(1)}, bf16[416,128]{1,0:T(8,128)(2,1)S(1)}, bf16[416,128]{1,0:T(8,128)(2,1)S(1)}) custom-call(s32[2]{0:T(128)S(1)} %copy-done.5, bf16[1440,128]{1,0:T(8,128)(2,1)S(1)} %collective-permute-done.35.near, bf16[3,32,128]{2,1,0:T(8,128)(2,1)} %get-tuple-element.277.far, ...), custom_call_target="tpu_custom_call" | custom-call | tf_op jit(solution)/shard_map/join/pallas_call | solution.py:750
  62.7 3.7 %collective-permute-start.41 = (bf16[336,128]{1,0:T(8,128)(2,1)S(1)}, bf16[336,128]{1,0:T(8,128)(2,1)S(1)}, u32[]{:S(2)}, u32[]{:S(2)}) collective-permute-start(bf16[336,128]{1,0:T(8,128)(2,1)S(1)} %fusion.1), channel_id=1, source_target_pairs={{0,6},{1,7},{2,4},{3,5},{4,2},{5,3},{6,0},{7,1},{8,14},{9,15},{10,... | collective-permute-start | bytes 258056 | tf_op jit(solution)/shard_map/ppermute | solution.py:616
  66.4 0.8 collective-permute-start.39
  67.1 1.3 %collective-permute-start.43 = (bf16[416,128]{1,0:T(8,128)(2,1)S(1)}, bf16[416,128]{1,0:T(8,128)(2,1)S(1)}, u32[]{:S(2)}, u32[]{:S(2)}) collective-permute-start(bf16[416,128]{1,0:T(8,128)(2,1)S(1)} %get-tuple-element.286), channel_id=1, source_target_pairs={{0,1},{1,2},{2,3},{3,4},{4,5},{5,6},{6,7},{7,0},{8,9},{9,10},{10,1... | collective-permute-start | bytes 319496 | tf_op jit(solution)/shard_map/ppermute | solution.py:815
  68.4 3.5 %collective-permute-start.44 = (bf16[416,128]{1,0:T(8,128)(2,1)S(1)}, bf16[416,128]{1,0:T(8,128)(2,1)S(1)}, u32[]{:S(2)}, u32[]{:S(2)}) collective-permute-start(bf16[416,128]{1,0:T(8,128)(2,1)S(1)} %get-tuple-element.287), channel_id=1, source_target_pairs={{0,7},{1,0},{2,1},{3,2},{4,3},{5,4},{6,5},{7,6},{8,15},{9,8},{10,9... | collective-permute-start | bytes 319496 | tf_op jit(solution)/shard_map/ppermute | solution.py:814
  71.9 2.0 %collective-permute-done.40 = bf16[336,128]{1,0:T(8,128)(2,1)S(1)} collective-permute-done((bf16[336,128]{1,0:T(8,128)(2,1)S(1)}, bf16[336,128]{1,0:T(8,128)(2,1)S(1)}, u32[]{:S(2)}, u32[]{:S(2)}) %collective-permute-start.40) | collective-permute-done | bytes 86048 | tf_op jit(solution)/shard_map/ppermute | solution.py:616
  73.8 0.1 add_convert_fusion.1
  73.9 2.5 %collective-permute-start.42 = (bf16[336,128]{1,0:T(8,128)(2,1)S(1)}, bf16[336,128]{1,0:T(8,128)(2,1)S(1)}, u32[]{:S(2)}, u32[]{:S(2)}) collective-permute-start(bf16[336,128]{1,0:T(8,128)(2,1)S(1)} %add_convert_fusion.1), channel_id=1, source_target_pairs={{0,1},{1,0},{2,3},{3,2},{4,5},{5,4},{6,7},{7,6},{8,9},{9,8},{10,11... | collective-permute-start | bytes 258056 | tf_op jit(solution)/shard_map/ppermute | solution.py:819
  76.3 1.8 %collective-permute-start.46 = (bf16[336,128]{1,0:T(8,128)(2,1)S(1)}, bf16[336,128]{1,0:T(8,128)(2,1)S(1)}, u32[]{:S(2)}, u32[]{:S(2)}) collective-permute-start(bf16[336,128]{1,0:T(8,128)(2,1)S(1)} %add_convert_fusion.1), channel_id=1, source_target_pairs={{0,17},{1,16},{2,19},{3,18},{4,21},{5,20},{6,23},{7,22},{8,25},{9,... | collective-permute-start | bytes 258056 | tf_op jit(solution)/shard_map/ppermute | solution.py:819
  78.1 3.7 %edges.1 = bf16[128,32,128]{2,1,0:T(8,128)(2,1)} custom-call(bf16[4096,128]{1,0:T(8,128)(2,1)S(1)} %copy-done.12, bf16[3,32,128]{2,1,0:T(8,128)(2,1)S(1)} %get-tuple-element.284.south, bf16[3,32,128]{2,1,0:T(8,128)(2,1)S(1)} %get-tuple-element.285.north, bf16[416,128]{1,0:T(8,128)(2,1)S(1)} %collective-permute-done.43.gl, ...), custom_call_target="tpu_custom_call" | custom-call | flops 100000000 | bytes 10485760 | tf_op jit(solution)/shard_map/edges/pallas_call | solution.py:524
  81.9 0.1 collective-permute-done.46
  82.0 1.5 %collective-permute-done.45 = bf16[336,128]{1,0:T(8,128)(2,1)S(1)} collective-permute-done((bf16[336,128]{1,0:T(8,128)(2,1)S(1)}, bf16[336,128]{1,0:T(8,128)(2,1)S(1)}, u32[]{:S(2)}, u32[]{:S(2)}) %collective-permute-start.45) | collective-permute-done | bytes 86048 | tf_op jit(solution)/shard_map/ppermute | solution.py:819
  83.5 0.4 collective-permute-start.47
  83.9 1.3 %collective-permute-done.47.other = bf16[4,336,128]{2,1,0:T(8,128)(2,1)S(1)} collective-permute-done((bf16[4,336,128]{2,1,0:T(8,128)(2,1)S(1)}, bf16[4,336,128]{2,1,0:T(8,128)(2,1)S(1)}, u32[]{:S(2)}, u32[]{:S(2)}) %collective-permute-start.47) | collective-permute-done | bytes 344096 | tf_op jit(solution)/shard_map/ppermute | solution.py:822
  85.2 1.4 %finish_sums.1 = (f32[49,128]{1,0:T(8,128)}, f32[128,512]{1,0:T(8,128)}, f32[512,128]{1,0:T(8,128)}, f32[3,512,128]{2,1,0:T(8,128)}) custom-call(bf16[4,336,128]{2,1,0:T(8,128)(2,1)S(1)} %pad_maximum_fusion.mine, bf16[4,336,128]{2,1,0:T(8,128)(2,1)S(1)} %collective-permute-done.47.other), custom_call_target="tpu_custom_call" | custom-call | tf_op jit(solution)/shard_map/finish_sums/pallas_call | solution.py:567
  (39 shorter events, 0.2 us)
Async XLA Ops:
  2.0 5.4 %collective-permute-start.32 = (bf16[3,32,128]{2,1,0:T(8,128)(2,1)}, bf16[3,32,128]{2,1,0:T(8,128)(2,1)S(1)}, u32[]{:S(2)}, u32[]{:S(2)}) collective-permute-start(bf16[3,32,128]{2,1,0:T(8,128)(2,1)} %get-tuple-element.255), channel_id=1, source_target_pairs={{0,8},{8,0},{16,24},{24,16},{1,9},{9,1},{17,25},{25,17},{2,10},{10... | collective-permute-start | bytes 73736 | tf_op jit(solution)/shard_map/ppermute | solution.py:793
  2.6 0.7 copy-start.5
  3.3 13.7 %copy-start = (bf16[3,512,128]{2,1,0:T(8,128)(2,1)S(1)}, bf16[3,512,128]{2,1,0:T(8,128)(2,1)}, u32[]{:S(2)}) copy-start(bf16[3,512,128]{2,1,0:T(8,128)(2,1)} %sw.1) | copy-start | bytes 1179652
  3.3 13.7 %copy-start.4 = (bf16[16,4,128]{2,1,0:T(4,128)(2,1)S(1)}, bf16[16,4,128]{2,1,0:T(4,128)(2,1)}, u32[]{:S(2)}) copy-start(bf16[16,4,128]{2,1,0:T(4,128)(2,1)} %cot.1) | copy-start | bytes 49156
  3.3 13.7 %copy-start.7 = (bf16[3,128]{1,0:T(4,128)(2,1)S(1)}, bf16[3,128]{1,0:T(4,128)(2,1)}, u32[]{:S(2)}) copy-start(bf16[3,128]{1,0:T(4,128)(2,1)} %sgain.1) | copy-start | bytes 2308
  3.3 13.7 %copy-start.8 = (bf16[3,128]{1,0:T(4,128)(2,1)S(1)}, bf16[3,128]{1,0:T(4,128)(2,1)}, u32[]{:S(2)}) copy-start(bf16[3,128]{1,0:T(4,128)(2,1)} %sbias.1) | copy-start | bytes 2308
  3.3 13.7 %copy-start.10 = (bf16[128]{0:T(256)(128)(2,1)S(1)}, bf16[128]{0:T(256)(128)(2,1)}, u32[]{:S(2)}) copy-start(bf16[128]{0:T(256)(128)(2,1)} %scale.1) | copy-start | bytes 772
  3.3 13.7 %copy-start.13 = (bf16[49,128]{1,0:T(8,128)(2,1)S(1)}, bf16[49,128]{1,0:T(8,128)(2,1)}, u32[]{:S(2)}) copy-start(bf16[49,128]{1,0:T(8,128)(2,1)} %dw.3) | copy-start | bytes 37636
  3.4 4.0 %collective-permute-start.6 = (bf16[3,32,128]{2,1,0:T(8,128)(2,1)S(1)}, bf16[3,32,128]{2,1,0:T(8,128)(2,1)}, u32[]{:S(2)}, u32[]{:S(2)}) collective-permute-start(bf16[3,32,128]{2,1,0:T(8,128)(2,1)S(1)} %get-tuple-element.143), channel_id=1, source_target_pairs={{8,16},{9,17},{10,18},{11,19},{12,20},{13,21},{14,22},{15,23},{16,... | collective-permute-start | bytes 73736 | tf_op jit(solution)/shard_map/cond/branch_3_fun/ppermute | solution.py:773
  4.8 2.6 %collective-permute-start.7 = (bf16[3,32,128]{2,1,0:T(8,128)(2,1)S(1)}, bf16[3,32,128]{2,1,0:T(8,128)(2,1)}, u32[]{:S(2)}, u32[]{:S(2)}) collective-permute-start(bf16[3,32,128]{2,1,0:T(8,128)(2,1)S(1)} %get-tuple-element.144), channel_id=1, source_target_pairs={{24,26},{25,25},{26,24},{27,31},{28,30},{29,29},{30,28},{31,27}} | collective-permute-start | bytes 73736 | tf_op jit(solution)/shard_map/cond/branch_3_fun/ppermute | solution.py:773
  7.4 9.6 %copy-start.1 = (bf16[128,512]{1,0:T(8,128)(2,1)S(1)}, bf16[128,512]{1,0:T(8,128)(2,1)}, u32[]{:S(2)}) copy-start(bf16[128,512]{1,0:T(8,128)(2,1)} %upw.1) | copy-start | bytes 393220
  7.4 9.6 %copy-start.2 = (bf16[512,128]{1,0:T(8,128)(2,1)S(1)}, bf16[512,128]{1,0:T(8,128)(2,1)}, u32[]{:S(2)}) copy-start(bf16[512,128]{1,0:T(8,128)(2,1)} %down.1) | copy-start | bytes 393220
  7.5 9.6 %copy-start.3 = (s32[128,32]{0,1:T(8,128)S(1)}, s32[128,32]{0,1:T(8,128)}, u32[]{:S(2)}) copy-start(s32[128,32]{0,1:T(8,128)} %param.30) | copy-start | bytes 49156
  8.5 8.4 %collective-permute-start.33 = (bf16[3,134,128]{2,1,0:T(8,128)(2,1)S(1)}, bf16[3,134,128]{2,1,0:T(8,128)(2,1)S(1)}, u32[]{:S(2)}, u32[]{:S(2)}) collective-permute-start(bf16[3,134,128]{2,1,0:T(8,128)(2,1)S(1)} %get-tuple-element.264), channel_id=1, source_target_pairs={{0,1},{1,2},{2,3},{3,4},{4,5},{5,6},{6,7},{7,0},{8,9},{9,10},{10,1... | collective-permute-start | bytes 308744 | tf_op jit(solution)/shard_map/ppermute | solution.py:797
  11.1 5.9 %collective-permute-start.34 = (bf16[3,134,128]{2,1,0:T(8,128)(2,1)S(1)}, bf16[3,134,128]{2,1,0:T(8,128)(2,1)S(1)}, u32[]{:S(2)}, u32[]{:S(2)}) collective-permute-start(bf16[3,134,128]{2,1,0:T(8,128)(2,1)S(1)} %get-tuple-element.265), channel_id=1, source_target_pairs={{0,7},{1,0},{2,1},{3,2},{4,3},{5,4},{6,5},{7,6},{8,15},{9,8},{10,9... | collective-permute-start | bytes 308744 | tf_op jit(solution)/shard_map/ppermute | solution.py:796
  17.0 0.7 copy-start.6
  17.0 0.7 copy-start.9
  45.7 3.3 %collective-permute-start.35 = (bf16[1440,128]{1,0:T(8,128)(2,1)S(1)}, bf16[1440,128]{1,0:T(8,128)(2,1)S(1)}, u32[]{:S(2)}, u32[]{:S(2)}) collective-permute-start(bf16[1440,128]{1,0:T(8,128)(2,1)S(1)} %get-tuple-element.269), channel_id=1, source_target_pairs={{0,8},{8,0},{16,24},{24,16},{1,9},{9,1},{17,25},{25,17},{2,10},{10... | collective-permute-start | bytes 1105928 | tf_op jit(solution)/shard_map/ppermute | solution.py:804
  49.1 5.3 %copy-start.14 = (bf16[3,32,128]{2,1,0:T(8,128)(2,1)S(1)}, bf16[3,32,128]{2,1,0:T(8,128)(2,1)}, u32[]{:S(2)}) copy-start(bf16[3,32,128]{2,1,0:T(8,128)(2,1)} %get-tuple-element.271) | copy-start | bytes 73732
  49.1 5.3 %copy-start.15 = (bf16[3,32,128]{2,1,0:T(8,128)(2,1)S(1)}, bf16[3,32,128]{2,1,0:T(8,128)(2,1)}, u32[]{:S(2)}) copy-start(bf16[3,32,128]{2,1,0:T(8,128)(2,1)} %get-tuple-element.272) | copy-start | bytes 73732
  49.2 11.4 %collective-permute-start.38 = (bf16[336,128]{1,0:T(8,128)(2,1)S(1)}, bf16[336,128]{1,0:T(8,128)(2,1)S(1)}, u32[]{:S(2)}, u32[]{:S(2)}) collective-permute-start(bf16[336,128]{1,0:T(8,128)(2,1)S(1)} %get-tuple-element.295), channel_id=1, source_target_pairs={{0,17},{1,16},{2,19},{3,18},{4,21},{5,20},{6,23},{7,22},{8,25},{9,... | collective-permute-start | bytes 258056 | tf_op jit(solution)/shard_map/ppermute | solution.py:607
  52.3 8.3 %collective-permute-start.37 = (bf16[336,128]{1,0:T(8,128)(2,1)S(1)}, bf16[336,128]{1,0:T(8,128)(2,1)S(1)}, u32[]{:S(2)}, u32[]{:S(2)}) collective-permute-start(bf16[336,128]{1,0:T(8,128)(2,1)S(1)} %get-tuple-element.296), channel_id=1, source_target_pairs={{0,16},{1,17},{2,18},{3,19},{4,20},{5,21},{6,22},{7,23},{8,24},{9,... | collective-permute-start | bytes 258056 | tf_op jit(solution)/shard_map/ppermute | solution.py:607
  53.1 7.5 %collective-permute-start.36 = (bf16[336,128]{1,0:T(8,128)(2,1)S(1)}, bf16[336,128]{1,0:T(8,128)(2,1)}, u32[]{:S(2)}, u32[]{:S(2)}) collective-permute-start(bf16[336,128]{1,0:T(8,128)(2,1)S(1)} %get-tuple-element.294), channel_id=1, source_target_pairs={{0,1},{1,0},{2,3},{3,2},{4,5},{5,4},{6,7},{7,6},{8,9},{9,8},{10,11... | collective-permute-start | bytes 258056 | tf_op jit(solution)/shard_map/ppermute | solution.py:607
  54.5 6.1 %collective-permute-start.22 = (bf16[3,32,128]{2,1,0:T(8,128)(2,1)S(1)}, bf16[3,32,128]{2,1,0:T(8,128)(2,1)}, u32[]{:S(2)}, u32[]{:S(2)}) collective-permute-start(bf16[3,32,128]{2,1,0:T(8,128)(2,1)S(1)} %get-tuple-element.183), channel_id=1, source_target_pairs={{8,16},{9,17},{10,18},{11,19},{12,20},{13,21},{14,22},{15,23},{16,... | collective-permute-start | bytes 73736 | tf_op jit(solution)/shard_map/cond/branch_3_fun/ppermute | solution.py:773
  55.7 4.8 %collective-permute-start.23 = (bf16[3,32,128]{2,1,0:T(8,128)(2,1)S(1)}, bf16[3,32,128]{2,1,0:T(8,128)(2,1)}, u32[]{:S(2)}, u32[]{:S(2)}) collective-permute-start(bf16[3,32,128]{2,1,0:T(8,128)(2,1)S(1)} %get-tuple-element.184), channel_id=1, source_target_pairs={{24,26},{25,25},{26,24},{27,31},{28,30},{29,29},{30,28},{31,27}} | collective-permute-start | bytes 73736 | tf_op jit(solution)/shard_map/cond/branch_3_fun/ppermute | solution.py:773
  60.5 1.1 %copy-start.11 = (bf16[4096,128]{1,0:T(8,128)(2,1)}, bf16[4096,128]{1,0:T(8,128)(2,1)S(1)}, u32[]{:S(2)}) copy-start(bf16[4096,128]{1,0:T(8,128)(2,1)S(1)} %get-tuple-element.283.base) | copy-start | bytes 3145732
  61.7 16.5 %copy-start.12 = (bf16[4096,128]{1,0:T(8,128)(2,1)S(1)}, bf16[4096,128]{1,0:T(8,128)(2,1)}, u32[]{:S(2)}) copy-start(bf16[4096,128]{1,0:T(8,128)(2,1)} %copy-done.11) | copy-start | bytes 3145732
  62.7 9.2 %collective-permute-start.41 = (bf16[336,128]{1,0:T(8,128)(2,1)S(1)}, bf16[336,128]{1,0:T(8,128)(2,1)S(1)}, u32[]{:S(2)}, u32[]{:S(2)}) collective-permute-start(bf16[336,128]{1,0:T(8,128)(2,1)S(1)} %fusion.1), channel_id=1, source_target_pairs={{0,6},{1,7},{2,4},{3,5},{4,2},{5,3},{6,0},{7,1},{8,14},{9,15},{10,... | collective-permute-start | bytes 258056 | tf_op jit(solution)/shard_map/ppermute | solution.py:616
  66.4 7.5 %collective-permute-start.40 = (bf16[336,128]{1,0:T(8,128)(2,1)S(1)}, bf16[336,128]{1,0:T(8,128)(2,1)S(1)}, u32[]{:S(2)}, u32[]{:S(2)}) collective-permute-start(bf16[336,128]{1,0:T(8,128)(2,1)S(1)} %fusion.1), channel_id=1, source_target_pairs={{0,4},{1,5},{2,6},{3,7},{4,0},{5,1},{6,2},{7,3},{8,12},{9,13},{10,... | collective-permute-start | bytes 258056 | tf_op jit(solution)/shard_map/ppermute | solution.py:616
  66.4 7.5 %collective-permute-start.39 = (bf16[336,128]{1,0:T(8,128)(2,1)S(1)}, bf16[336,128]{1,0:T(8,128)(2,1)S(1)}, u32[]{:S(2)}, u32[]{:S(2)}) collective-permute-start(bf16[336,128]{1,0:T(8,128)(2,1)S(1)} %fusion.1), channel_id=1, source_target_pairs={{0,2},{1,3},{2,0},{3,1},{4,6},{5,7},{6,4},{7,5},{8,10},{9,11},{10,... | collective-permute-start | bytes 258056 | tf_op jit(solution)/shard_map/ppermute | solution.py:616
  67.1 11.0 %collective-permute-start.43 = (bf16[416,128]{1,0:T(8,128)(2,1)S(1)}, bf16[416,128]{1,0:T(8,128)(2,1)S(1)}, u32[]{:S(2)}, u32[]{:S(2)}) collective-permute-start(bf16[416,128]{1,0:T(8,128)(2,1)S(1)} %get-tuple-element.286), channel_id=1, source_target_pairs={{0,1},{1,2},{2,3},{3,4},{4,5},{5,6},{6,7},{7,0},{8,9},{9,10},{10,1... | collective-permute-start | bytes 319496 | tf_op jit(solution)/shard_map/ppermute | solution.py:815
  68.4 9.7 %collective-permute-start.44 = (bf16[416,128]{1,0:T(8,128)(2,1)S(1)}, bf16[416,128]{1,0:T(8,128)(2,1)S(1)}, u32[]{:S(2)}, u32[]{:S(2)}) collective-permute-start(bf16[416,128]{1,0:T(8,128)(2,1)S(1)} %get-tuple-element.287), channel_id=1, source_target_pairs={{0,7},{1,0},{2,1},{3,2},{4,3},{5,4},{6,5},{7,6},{8,15},{9,8},{10,9... | collective-permute-start | bytes 319496 | tf_op jit(solution)/shard_map/ppermute | solution.py:814
  73.9 8.0 %collective-permute-start.42 = (bf16[336,128]{1,0:T(8,128)(2,1)S(1)}, bf16[336,128]{1,0:T(8,128)(2,1)S(1)}, u32[]{:S(2)}, u32[]{:S(2)}) collective-permute-start(bf16[336,128]{1,0:T(8,128)(2,1)S(1)} %add_convert_fusion.1), channel_id=1, source_target_pairs={{0,1},{1,0},{2,3},{3,2},{4,5},{5,4},{6,7},{7,6},{8,9},{9,8},{10,11... | collective-permute-start | bytes 258056 | tf_op jit(solution)/shard_map/ppermute | solution.py:819
  76.3 5.7 %collective-permute-start.46 = (bf16[336,128]{1,0:T(8,128)(2,1)S(1)}, bf16[336,128]{1,0:T(8,128)(2,1)S(1)}, u32[]{:S(2)}, u32[]{:S(2)}) collective-permute-start(bf16[336,128]{1,0:T(8,128)(2,1)S(1)} %add_convert_fusion.1), channel_id=1, source_target_pairs={{0,17},{1,16},{2,19},{3,18},{4,21},{5,20},{6,23},{7,22},{8,25},{9,... | collective-permute-start | bytes 258056 | tf_op jit(solution)/shard_map/ppermute | solution.py:819
  78.1 5.3 %collective-permute-start.45 = (bf16[336,128]{1,0:T(8,128)(2,1)S(1)}, bf16[336,128]{1,0:T(8,128)(2,1)S(1)}, u32[]{:S(2)}, u32[]{:S(2)}) collective-permute-start(bf16[336,128]{1,0:T(8,128)(2,1)S(1)} %add_convert_fusion.1), channel_id=1, source_target_pairs={{0,16},{1,17},{2,18},{3,19},{4,20},{5,21},{6,22},{7,23},{8,24},{9,... | collective-permute-start | bytes 258056 | tf_op jit(solution)/shard_map/ppermute | solution.py:819
  83.5 1.7 %collective-permute-start.47 = (bf16[4,336,128]{2,1,0:T(8,128)(2,1)S(1)}, bf16[4,336,128]{2,1,0:T(8,128)(2,1)S(1)}, u32[]{:S(2)}, u32[]{:S(2)}) collective-permute-start(bf16[4,336,128]{2,1,0:T(8,128)(2,1)S(1)} %pad_maximum_fusion.mine), channel_id=1, source_target_pairs={{0,8},{8,0},{16,24},{24,16},{1,9},{9,1},{17,25},{25,17},{2,10},{10... | collective-permute-start | bytes 1032200 | tf_op jit(solution)/shard_map/ppermute | solution.py:822

commit v5 on v4

--- a/solution.py
+++ b/solution.py
@@ -164,7 +164,7 @@
 
     lax.fori_loop(0, n0 // T1, nfwd, 0)
 
-    T2 = n0 // 4
+    T2 = n0 // 2
     onec = (lax.broadcasted_iota(jnp.int32, (T2, 128), 1) == 0).astype(f32).astype(bf16)
 
     def upf(n, _):
@@ -205,7 +205,7 @@
                 p1[pl.ds(pb, TP // 4), k * 128 : (k + 1) * 128] = sn[a, :, b].reshape(TP // 4, 128)
         return 0
 
-    lax.fori_loop(0, I // 2, dnf, 0)
+    lax.fori_loop(0, I // 2, dnf, 0, unroll=2)
 
     def to_patches(sn, ii, cc):
         v = sn.reshape(ii // 2, 2, cc // 2, 2, S, 128)

time: 87.8 us -> 88.8 us (1.011)
    ppermute x3, starting transfers between devices: 5.28 us -> 6.22 us  [square_sum(): came.append(lax.ppermute(part, ('lat', 'lon'), square_pairs(k)))]
  transfers between devices with their start and end apart: 20 -> 20, of which waited for: 7 -> 8; matrix products, arithmetic and copies ran while one was open for 0% -> 0% of each run, Pallas kernels for 10% -> 10%
where the time goes in v5:
time: 88.8 us; the launch traced here: 87.2 us
  Pallas kernels  41.2 us (46%)
  starting transfers between devices  32.8 us (37%)
  waiting for transfers between devices  9.48 us (11%)
  local copies, waits for them, and re-layouts  1.37 us (2%)
  other arithmetic  1.25 us (1%)
  between operations  0.95 us (1%)
    pallas_call x1, Pallas kernels, block_pass(): pl.pallas_call(functools.partial(block_body, R, CW), out_shape=out_shape,...  27.8 us
    ppermute x3, starting transfers between devices, square_sum(): came.append(lax.ppermute(part, ('lat', 'lon'), square_pairs(k)))  6.22 us
    ppermute x3, starting transfers between devices, line_sum(): lax.ppermute(total, 'lon', flip_pairs('lon', bit * k))  4.44 us
    pallas_call x1, Pallas kernels, edges(): pl.pallas_call(functools.partial(edges_body, R, CW), out_shape=jax.ShapeD...  3.74 us
    ppermute x3, starting transfers between devices, on_device(): back = [lax.ppermute(chunk, axes, square_pairs(k)) for k in (1, 2, 3)]  3.65 us
    pallas_call x1, Pallas kernels, conv_back(): pl.pallas_call(functools.partial(conv_back_body, R, CW), out_shape=jax.Sh...  3.55 us
    ppermute x1, starting transfers between devices, on_device(): gr = lax.ppermute(lpay, 'lon', shift_pairs('lon', -1))  3.45 us
    ppermute x1, starting transfers between devices, on_device(): right_f = lax.ppermute(lpay, 'lon', shift_pairs('lon', -1))  3.28 us
  transfers between devices with their start and end apart: 20, of which 8 were waited for; matrix products, arithmetic and copies ran while one was open for 0% of the time, Pallas kernels for 10%

profile of v5, /device:TPU:0, one launch (start us, length us, event | category | flops | bytes accessed | tf_op | source)
XLA Modules:
  0.0 87.2 jit_solution(16837376201035024414)
XLA Ops:
  0.6 1.4 %rim.1 = (bf16[3,32,128]{2,1,0:T(8,128)(2,1)}, bf16[3,32,128]{2,1,0:T(8,128)(2,1)S(1)}, bf16[3,32,128]{2,1,0:T(8,128)(2,1)S(1)}, s32[2]{0:T(128)}) custom-call(bf16[128,32,128]{2,1,0:T(8,128)(2,1)} %field.3, s32[256]{0:T(256)} %mirror.1), custom_call_target="tpu_custom_call" | custom-call | tf_op jit(solution)/shard_map/rim/pallas_call | solution.py:655
  2.0 0.5 collective-permute-start.32
  2.6 0.7 copy-done.5
  3.3 0.0 copy-start
  3.3 0.0 copy-start.4
  3.3 0.0 copy-start.7
  3.3 0.0 copy-start.8
  3.3 4.1 %conditional.2 = (bf16[3,32,128]{2,1,0:T(8,128)(2,1)}, bf16[3,32,128]{2,1,0:T(8,128)(2,1)}, bf16[3,128,128]{2,1,0:T(8,128)(2,1)S(1)}, bf16[3,128,128]{2,1,0:T(8,128)(2,1)S(1)}) conditional(s32[]{:T(128)} %bitcast, (bf16[3,32,128]{2,1,0:T(8,128)(2,1)S(1)}, bf16[3,32,128]{2,1,0:T(8,128)(2,1)S(1)}, ...), branch_computations={%region_0.0_spmd, %region_1.0_spmd, %region_2.0_spmd, %region_3.0_... | conditional | bytes 196720 | solution.py:777
  3.4 1.4 %collective-permute-start.8 = (bf16[3,32,128]{2,1,0:T(8,128)(2,1)S(1)}, bf16[3,32,128]{2,1,0:T(8,128)(2,1)}, u32[]{:S(2)}, u32[]{:S(2)}) collective-permute-start(bf16[3,32,128]{2,1,0:T(8,128)(2,1)S(1)} %get-tuple-element.148), channel_id=1, source_target_pairs={{8,16},{9,17},{10,18},{11,19},{12,20},{13,21},{14,22},{15,23},{16,... | collective-permute-start | bytes 73736 | tf_op jit(solution)/shard_map/cond/branch_4_fun/ppermute | solution.py:773
  4.8 1.3 %collective-permute-start.9 = (bf16[3,32,128]{2,1,0:T(8,128)(2,1)S(1)}, bf16[3,32,128]{2,1,0:T(8,128)(2,1)}, u32[]{:S(2)}, u32[]{:S(2)}) collective-permute-start(bf16[3,32,128]{2,1,0:T(8,128)(2,1)S(1)} %get-tuple-element.149), channel_id=1, source_target_pairs={{24,27},{25,26},{26,25},{27,24},{28,31},{29,30},{30,29},{31,28}} | collective-permute-start | bytes 73736 | tf_op jit(solution)/shard_map/cond/branch_4_fun/ppermute | solution.py:773
  6.0 1.3 %sides.12 = (bf16[3,128,128]{2,1,0:T(8,128)(2,1)S(1)}, bf16[3,128,128]{2,1,0:T(8,128)(2,1)S(1)}) custom-call(bf16[128,32,128]{2,1,0:T(8,128)(2,1)} %get-tuple-element.150.field), custom_call_target="tpu_custom_call" | custom-call | tf_op jit(solution)/shard_map/cond/branch_4_fun/sides/pallas_call | solution.py:690
  7.4 0.0 copy-start.1
  7.5 1.0 %join.2 = (bf16[3,32,128]{2,1,0:T(8,128)(2,1)S(1)}, bf16[3,32,128]{2,1,0:T(8,128)(2,1)S(1)}, bf16[3,134,128]{2,1,0:T(8,128)(2,1)S(1)}, bf16[3,134,128]{2,1,0:T(8,128)(2,1)S(1)}) custom-call(s32[2]{0:T(128)S(1)} %copy-done.5, bf16[3,32,128]{2,1,0:T(8,128)(2,1)S(1)} %collective-permute-done.32.near, bf16[3,32,128]{2,1,0:T(8,128)(2,1)} %get-tuple-element.258.far, ...), custom_call_target="tpu_custom_call" | custom-call | tf_op jit(solution)/shard_map/join/pallas_call | solution.py:750
  8.5 2.6 %collective-permute-start.33 = (bf16[3,134,128]{2,1,0:T(8,128)(2,1)S(1)}, bf16[3,134,128]{2,1,0:T(8,128)(2,1)S(1)}, u32[]{:S(2)}, u32[]{:S(2)}) collective-permute-start(bf16[3,134,128]{2,1,0:T(8,128)(2,1)S(1)} %get-tuple-element.264), channel_id=1, source_target_pairs={{0,1},{1,2},{2,3},{3,4},{4,5},{5,6},{6,7},{7,0},{8,9},{9,10},{10,1... | collective-permute-start | bytes 308744 | tf_op jit(solution)/shard_map/ppermute | solution.py:797
  11.1 3.3 %collective-permute-start.34 = (bf16[3,134,128]{2,1,0:T(8,128)(2,1)S(1)}, bf16[3,134,128]{2,1,0:T(8,128)(2,1)S(1)}, u32[]{:S(2)}, u32[]{:S(2)}) collective-permute-start(bf16[3,134,128]{2,1,0:T(8,128)(2,1)S(1)} %get-tuple-element.265), channel_id=1, source_target_pairs={{0,7},{1,0},{2,1},{3,2},{4,3},{5,4},{6,5},{7,6},{8,15},{9,8},{10,9... | collective-permute-start | bytes 308744 | tf_op jit(solution)/shard_map/ppermute | solution.py:796
  14.4 2.5 %collective-permute-done.33.left = bf16[3,134,128]{2,1,0:T(8,128)(2,1)S(1)} collective-permute-done((bf16[3,134,128]{2,1,0:T(8,128)(2,1)S(1)}, bf16[3,134,128]{2,1,0:T(8,128)(2,1)S(1)}, u32[]{:S(2)}, u32[]{:S(2)}) %collective-permute-start.33) | collective-permute-done | bytes 102944 | tf_op jit(solution)/shard_map/ppermute | solution.py:797
  16.9 0.1 collective-permute-done.34.right
  17.1 0.6 copy-done.6
  17.7 27.8 %block_pass.1 = (bf16[16,4,128]{2,1,0:T(4,128)(2,1)}, bf16[4096,128]{1,0:T(8,128)(2,1)S(1)}, bf16[4096,128]{1,0:T(8,128)(2,1)S(1)}, bf16[3,32,128]{2,1,0:T(8,128...) custom-call(bf16[128,32,128]{2,1,0:T(8,128)(2,1)} %field.3, ...), custom_call_target="tpu_custom_call" | custom-call | tf_op jit(solution)/shard_map/block_pass/pallas_call | solution.py:372
  45.4 2.0 %collective-permute-start.35 = (bf16[1440,128]{1,0:T(8,128)(2,1)S(1)}, bf16[1440,128]{1,0:T(8,128)(2,1)S(1)}, u32[]{:S(2)}, u32[]{:S(2)}) collective-permute-start(bf16[1440,128]{1,0:T(8,128)(2,1)S(1)} %get-tuple-element.269), channel_id=1, source_target_pairs={{0,8},{8,0},{16,24},{24,16},{1,9},{9,1},{17,25},{25,17},{2,10},{10... | collective-permute-start | bytes 1105928 | tf_op jit(solution)/shard_map/ppermute | solution.py:804
  47.4 1.3 %collective-permute-done.35.near = bf16[1440,128]{1,0:T(8,128)(2,1)S(1)} collective-permute-done((bf16[1440,128]{1,0:T(8,128)(2,1)S(1)}, bf16[1440,128]{1,0:T(8,128)(2,1)S(1)}, u32[]{:S(2)}, u32[]{:S(2)}) %collective-permute-start.35) | collective-permute-done | bytes 368672 | tf_op jit(solution)/shard_map/ppermute | solution.py:804
  48.7 0.1 add_convert_fusion
  48.8 0.0 copy-start.14
  48.8 0.0 copy-start.15
  48.9 3.6 %collective-permute-start.38 = (bf16[336,128]{1,0:T(8,128)(2,1)S(1)}, bf16[336,128]{1,0:T(8,128)(2,1)S(1)}, u32[]{:S(2)}, u32[]{:S(2)}) collective-permute-start(bf16[336,128]{1,0:T(8,128)(2,1)S(1)} %get-tuple-element.295), channel_id=1, source_target_pairs={{0,17},{1,16},{2,19},{3,18},{4,21},{5,20},{6,23},{7,22},{8,25},{9,... | collective-permute-start | bytes 258056 | tf_op jit(solution)/shard_map/ppermute | solution.py:607
  52.5 1.2 %collective-permute-start.37 = (bf16[336,128]{1,0:T(8,128)(2,1)S(1)}, bf16[336,128]{1,0:T(8,128)(2,1)S(1)}, u32[]{:S(2)}, u32[]{:S(2)}) collective-permute-start(bf16[336,128]{1,0:T(8,128)(2,1)S(1)} %get-tuple-element.296), channel_id=1, source_target_pairs={{0,16},{1,17},{2,18},{3,19},{4,20},{5,21},{6,22},{7,23},{8,24},{9,... | collective-permute-start | bytes 258056 | tf_op jit(solution)/shard_map/ppermute | solution.py:607
  53.7 1.4 %collective-permute-start.36 = (bf16[336,128]{1,0:T(8,128)(2,1)S(1)}, bf16[336,128]{1,0:T(8,128)(2,1)}, u32[]{:S(2)}, u32[]{:S(2)}) collective-permute-start(bf16[336,128]{1,0:T(8,128)(2,1)S(1)} %get-tuple-element.294), channel_id=1, source_target_pairs={{0,1},{1,0},{2,3},{3,2},{4,5},{5,4},{6,7},{7,6},{8,9},{9,8},{10,11... | collective-permute-start | bytes 258056 | tf_op jit(solution)/shard_map/ppermute | solution.py:607
  55.1 6.1 %conditional.3 = (bf16[3,32,128]{2,1,0:T(8,128)(2,1)}, bf16[3,32,128]{2,1,0:T(8,128)(2,1)}, bf16[4096,128]{1,0:T(8,128)(2,1)S(1)}) conditional(s32[]{:T(128)} %bitcast, (bf16[3,32,128]{2,1,0:T(8,128)(2,1)S(1)}, bf16[3,32,128]{2,1,0:T(8,128)(2,1)S(1)}, bf16[4096,128]{1,0:T(8,128)(2,1)S(1)}, ...), branch_computations={%region_8.9_spmd, %region_9.10_spmd, %region_10.11_spmd, %region_1... | conditional | flops 100000000 | bytes 31653992 | solution.py:777
  55.1 1.2 %collective-permute-start.24 = (bf16[3,32,128]{2,1,0:T(8,128)(2,1)S(1)}, bf16[3,32,128]{2,1,0:T(8,128)(2,1)}, u32[]{:S(2)}, u32[]{:S(2)}) collective-permute-start(bf16[3,32,128]{2,1,0:T(8,128)(2,1)S(1)} %get-tuple-element.188), channel_id=1, source_target_pairs={{8,16},{9,17},{10,18},{11,19},{12,20},{13,21},{14,22},{15,23},{16,... | collective-permute-start | bytes 73736 | tf_op jit(solution)/shard_map/cond/branch_4_fun/ppermute | solution.py:773
  56.3 1.3 %collective-permute-start.25 = (bf16[3,32,128]{2,1,0:T(8,128)(2,1)S(1)}, bf16[3,32,128]{2,1,0:T(8,128)(2,1)}, u32[]{:S(2)}, u32[]{:S(2)}) collective-permute-start(bf16[3,32,128]{2,1,0:T(8,128)(2,1)S(1)} %get-tuple-element.189), channel_id=1, source_target_pairs={{24,27},{25,26},{26,25},{27,24},{28,31},{29,30},{30,29},{31,28}} | collective-permute-start | bytes 73736 | tf_op jit(solution)/shard_map/cond/branch_4_fun/ppermute | solution.py:773
  57.6 3.5 %conv_back.12 = bf16[4096,128]{1,0:T(8,128)(2,1)S(1)} custom-call(bf16[4096,128]{1,0:T(8,128)(2,1)S(1)} %get-tuple-element.190.g, bf16[4096,128]{1,0:T(8,128)(2,1)S(1)} %get-tuple-element.191.dirin, bf16[49,128]{1,0:T(8,128)(2,1)S(1)} %get-tuple-element.192.dw), custom_call_target="tpu_custom_call" | custom-call | flops 100000000 | bytes 31457280 | tf_op jit(solution)/shard_map/cond/branch_4_fun/conv_back/pallas_call | solution.py:418
  61.2 1.1 %fusion.1 = bf16[336,128]{1,0:T(8,128)(2,1)S(1)} fusion(bf16[336,128]{1,0:T(8,128)(2,1)S(1)} %collective-permute-done.38, bf16[336,128]{1,0:T(8,128)(2,1)S(1)} %collective-permute-done.37, bf16[336,128]{1,0:T(8,128)(2,1)} %collective-permute-done.36, bf16[4,336,128]{2,1,0:T(8,128)(2,1)S(1)} %bitcast.20, s32[]{:T(128)S(6)} %select_n.26), kind=kLoop, calls=%fused_computation.4 | loop fusion | flops 344064 | bytes 430084 | tf_op jit(solution)/shard_map/convert_element_type | solution.py:582
  62.3 1.0 %join.3 = (bf16[3,32,128]{2,1,0:T(8,128)(2,1)S(1)}, bf16[3,32,128]{2,1,0:T(8,128)(2,1)S(1)}, bf16[416,128]{1,0:T(8,128)(2,1)S(1)}, bf16[416,128]{1,0:T(8,128)(2,1)S(1)}) custom-call(s32[2]{0:T(128)S(1)} %copy-done.5, bf16[1440,128]{1,0:T(8,128)(2,1)S(1)} %collective-permute-done.35.near, bf16[3,32,128]{2,1,0:T(8,128)(2,1)} %get-tuple-element.277.far, ...), custom_call_target="tpu_custom_call" | custom-call | tf_op jit(solution)/shard_map/join/pallas_call | solution.py:750
  63.3 3.7 %collective-permute-start.41 = (bf16[336,128]{1,0:T(8,128)(2,1)S(1)}, bf16[336,128]{1,0:T(8,128)(2,1)S(1)}, u32[]{:S(2)}, u32[]{:S(2)}) collective-permute-start(bf16[336,128]{1,0:T(8,128)(2,1)S(1)} %fusion.1), channel_id=1, source_target_pairs={{0,6},{1,7},{2,4},{3,5},{4,2},{5,3},{6,0},{7,1},{8,14},{9,15},{10,... | collective-permute-start | bytes 258056 | tf_op jit(solution)/shard_map/ppermute | solution.py:616
  67.0 0.8 collective-permute-start.39
  67.8 1.3 %collective-permute-start.43 = (bf16[416,128]{1,0:T(8,128)(2,1)S(1)}, bf16[416,128]{1,0:T(8,128)(2,1)S(1)}, u32[]{:S(2)}, u32[]{:S(2)}) collective-permute-start(bf16[416,128]{1,0:T(8,128)(2,1)S(1)} %get-tuple-element.286), channel_id=1, source_target_pairs={{0,1},{1,2},{2,3},{3,4},{4,5},{5,6},{6,7},{7,0},{8,9},{9,10},{10,1... | collective-permute-start | bytes 319496 | tf_op jit(solution)/shard_map/ppermute | solution.py:815
  69.1 3.5 %collective-permute-start.44 = (bf16[416,128]{1,0:T(8,128)(2,1)S(1)}, bf16[416,128]{1,0:T(8,128)(2,1)S(1)}, u32[]{:S(2)}, u32[]{:S(2)}) collective-permute-start(bf16[416,128]{1,0:T(8,128)(2,1)S(1)} %get-tuple-element.287), channel_id=1, source_target_pairs={{0,7},{1,0},{2,1},{3,2},{4,3},{5,4},{6,5},{7,6},{8,15},{9,8},{10,9... | collective-permute-start | bytes 319496 | tf_op jit(solution)/shard_map/ppermute | solution.py:814
  72.5 1.7 %collective-permute-done.40 = bf16[336,128]{1,0:T(8,128)(2,1)S(1)} collective-permute-done((bf16[336,128]{1,0:T(8,128)(2,1)S(1)}, bf16[336,128]{1,0:T(8,128)(2,1)S(1)}, u32[]{:S(2)}, u32[]{:S(2)}) %collective-permute-start.40) | collective-permute-done | bytes 86048 | tf_op jit(solution)/shard_map/ppermute | solution.py:616
  74.2 0.8 collective-permute-done.39
  75.1 0.1 add_convert_fusion.1
  75.1 2.0 %collective-permute-start.42 = (bf16[336,128]{1,0:T(8,128)(2,1)S(1)}, bf16[336,128]{1,0:T(8,128)(2,1)S(1)}, u32[]{:S(2)}, u32[]{:S(2)}) collective-permute-start(bf16[336,128]{1,0:T(8,128)(2,1)S(1)} %add_convert_fusion.1), channel_id=1, source_target_pairs={{0,1},{1,0},{2,3},{3,2},{4,5},{5,4},{6,7},{7,6},{8,9},{9,8},{10,11... | collective-permute-start | bytes 258056 | tf_op jit(solution)/shard_map/ppermute | solution.py:819
  77.1 1.7 %collective-permute-start.46 = (bf16[336,128]{1,0:T(8,128)(2,1)S(1)}, bf16[336,128]{1,0:T(8,128)(2,1)S(1)}, u32[]{:S(2)}, u32[]{:S(2)}) collective-permute-start(bf16[336,128]{1,0:T(8,128)(2,1)S(1)} %add_convert_fusion.1), channel_id=1, source_target_pairs={{0,17},{1,16},{2,19},{3,18},{4,21},{5,20},{6,23},{7,22},{8,25},{9,... | collective-permute-start | bytes 258056 | tf_op jit(solution)/shard_map/ppermute | solution.py:819
  78.8 3.7 %edges.1 = bf16[128,32,128]{2,1,0:T(8,128)(2,1)} custom-call(bf16[4096,128]{1,0:T(8,128)(2,1)S(1)} %copy-done.12, bf16[3,32,128]{2,1,0:T(8,128)(2,1)S(1)} %get-tuple-element.284.south, bf16[3,32,128]{2,1,0:T(8,128)(2,1)S(1)} %get-tuple-element.285.north, bf16[416,128]{1,0:T(8,128)(2,1)S(1)} %collective-permute-done.43.gl, ...), custom_call_target="tpu_custom_call" | custom-call | flops 100000000 | bytes 10485760 | tf_op jit(solution)/shard_map/edges/pallas_call | solution.py:524
  82.5 0.2 collective-permute-done.46
  82.8 1.3 %collective-permute-done.45 = bf16[336,128]{1,0:T(8,128)(2,1)S(1)} collective-permute-done((bf16[336,128]{1,0:T(8,128)(2,1)S(1)}, bf16[336,128]{1,0:T(8,128)(2,1)S(1)}, u32[]{:S(2)}, u32[]{:S(2)}) %collective-permute-start.45) | collective-permute-done | bytes 86048 | tf_op jit(solution)/shard_map/ppermute | solution.py:819
  84.1 0.3 collective-permute-start.47
  84.4 1.4 %collective-permute-done.47.other = bf16[4,336,128]{2,1,0:T(8,128)(2,1)S(1)} collective-permute-done((bf16[4,336,128]{2,1,0:T(8,128)(2,1)S(1)}, bf16[4,336,128]{2,1,0:T(8,128)(2,1)S(1)}, u32[]{:S(2)}, u32[]{:S(2)}) %collective-permute-start.47) | collective-permute-done | bytes 344096 | tf_op jit(solution)/shard_map/ppermute | solution.py:822
  85.8 1.4 %finish_sums.1 = (f32[49,128]{1,0:T(8,128)}, f32[128,512]{1,0:T(8,128)}, f32[512,128]{1,0:T(8,128)}, f32[3,512,128]{2,1,0:T(8,128)}) custom-call(bf16[4,336,128]{2,1,0:T(8,128)(2,1)S(1)} %pad_maximum_fusion.mine, bf16[4,336,128]{2,1,0:T(8,128)(2,1)S(1)} %collective-permute-done.47.other), custom_call_target="tpu_custom_call" | custom-call | tf_op jit(solution)/shard_map/finish_sums/pallas_call | solution.py:567
  (39 shorter events, 0.2 us)
Async XLA Ops:
  2.0 5.4 %collective-permute-start.32 = (bf16[3,32,128]{2,1,0:T(8,128)(2,1)}, bf16[3,32,128]{2,1,0:T(8,128)(2,1)S(1)}, u32[]{:S(2)}, u32[]{:S(2)}) collective-permute-start(bf16[3,32,128]{2,1,0:T(8,128)(2,1)} %get-tuple-element.255), channel_id=1, source_target_pairs={{0,8},{8,0},{16,24},{24,16},{1,9},{9,1},{17,25},{25,17},{2,10},{10... | collective-permute-start | bytes 73736 | tf_op jit(solution)/shard_map/ppermute | solution.py:793
  2.6 0.7 copy-start.5
  3.3 13.7 %copy-start = (bf16[3,512,128]{2,1,0:T(8,128)(2,1)S(1)}, bf16[3,512,128]{2,1,0:T(8,128)(2,1)}, u32[]{:S(2)}) copy-start(bf16[3,512,128]{2,1,0:T(8,128)(2,1)} %sw.1) | copy-start | bytes 1179652
  3.3 13.7 %copy-start.4 = (bf16[16,4,128]{2,1,0:T(4,128)(2,1)S(1)}, bf16[16,4,128]{2,1,0:T(4,128)(2,1)}, u32[]{:S(2)}) copy-start(bf16[16,4,128]{2,1,0:T(4,128)(2,1)} %cot.1) | copy-start | bytes 49156
  3.3 13.7 %copy-start.7 = (bf16[3,128]{1,0:T(4,128)(2,1)S(1)}, bf16[3,128]{1,0:T(4,128)(2,1)}, u32[]{:S(2)}) copy-start(bf16[3,128]{1,0:T(4,128)(2,1)} %sgain.1) | copy-start | bytes 2308
  3.3 13.7 %copy-start.8 = (bf16[3,128]{1,0:T(4,128)(2,1)S(1)}, bf16[3,128]{1,0:T(4,128)(2,1)}, u32[]{:S(2)}) copy-start(bf16[3,128]{1,0:T(4,128)(2,1)} %sbias.1) | copy-start | bytes 2308
  3.3 13.7 %copy-start.10 = (bf16[128]{0:T(256)(128)(2,1)S(1)}, bf16[128]{0:T(256)(128)(2,1)}, u32[]{:S(2)}) copy-start(bf16[128]{0:T(256)(128)(2,1)} %scale.1) | copy-start | bytes 772
  3.3 13.7 %copy-start.13 = (bf16[49,128]{1,0:T(8,128)(2,1)S(1)}, bf16[49,128]{1,0:T(8,128)(2,1)}, u32[]{:S(2)}) copy-start(bf16[49,128]{1,0:T(8,128)(2,1)} %dw.3) | copy-start | bytes 37636
  3.4 4.0 %collective-permute-start.8 = (bf16[3,32,128]{2,1,0:T(8,128)(2,1)S(1)}, bf16[3,32,128]{2,1,0:T(8,128)(2,1)}, u32[]{:S(2)}, u32[]{:S(2)}) collective-permute-start(bf16[3,32,128]{2,1,0:T(8,128)(2,1)S(1)} %get-tuple-element.148), channel_id=1, source_target_pairs={{8,16},{9,17},{10,18},{11,19},{12,20},{13,21},{14,22},{15,23},{16,... | collective-permute-start | bytes 73736 | tf_op jit(solution)/shard_map/cond/branch_4_fun/ppermute | solution.py:773
  4.8 2.6 %collective-permute-start.9 = (bf16[3,32,128]{2,1,0:T(8,128)(2,1)S(1)}, bf16[3,32,128]{2,1,0:T(8,128)(2,1)}, u32[]{:S(2)}, u32[]{:S(2)}) collective-permute-start(bf16[3,32,128]{2,1,0:T(8,128)(2,1)S(1)} %get-tuple-element.149), channel_id=1, source_target_pairs={{24,27},{25,26},{26,25},{27,24},{28,31},{29,30},{30,29},{31,28}} | collective-permute-start | bytes 73736 | tf_op jit(solution)/shard_map/cond/branch_4_fun/ppermute | solution.py:773
  7.4 9.6 %copy-start.1 = (bf16[128,512]{1,0:T(8,128)(2,1)S(1)}, bf16[128,512]{1,0:T(8,128)(2,1)}, u32[]{:S(2)}) copy-start(bf16[128,512]{1,0:T(8,128)(2,1)} %upw.1) | copy-start | bytes 393220
  7.4 9.6 %copy-start.2 = (bf16[512,128]{1,0:T(8,128)(2,1)S(1)}, bf16[512,128]{1,0:T(8,128)(2,1)}, u32[]{:S(2)}) copy-start(bf16[512,128]{1,0:T(8,128)(2,1)} %down.1) | copy-start | bytes 393220
  7.5 9.6 %copy-start.3 = (s32[128,32]{0,1:T(8,128)S(1)}, s32[128,32]{0,1:T(8,128)}, u32[]{:S(2)}) copy-start(s32[128,32]{0,1:T(8,128)} %param.30) | copy-start | bytes 49156
  8.5 8.4 %collective-permute-start.33 = (bf16[3,134,128]{2,1,0:T(8,128)(2,1)S(1)}, bf16[3,134,128]{2,1,0:T(8,128)(2,1)S(1)}, u32[]{:S(2)}, u32[]{:S(2)}) collective-permute-start(bf16[3,134,128]{2,1,0:T(8,128)(2,1)S(1)} %get-tuple-element.264), channel_id=1, source_target_pairs={{0,1},{1,2},{2,3},{3,4},{4,5},{5,6},{6,7},{7,0},{8,9},{9,10},{10,1... | collective-permute-start | bytes 308744 | tf_op jit(solution)/shard_map/ppermute | solution.py:797
  11.1 5.9 %collective-permute-start.34 = (bf16[3,134,128]{2,1,0:T(8,128)(2,1)S(1)}, bf16[3,134,128]{2,1,0:T(8,128)(2,1)S(1)}, u32[]{:S(2)}, u32[]{:S(2)}) collective-permute-start(bf16[3,134,128]{2,1,0:T(8,128)(2,1)S(1)} %get-tuple-element.265), channel_id=1, source_target_pairs={{0,7},{1,0},{2,1},{3,2},{4,3},{5,4},{6,5},{7,6},{8,15},{9,8},{10,9... | collective-permute-start | bytes 308744 | tf_op jit(solution)/shard_map/ppermute | solution.py:796
  17.0 0.7 copy-start.6
  17.0 0.7 copy-start.9
  45.4 3.3 %collective-permute-start.35 = (bf16[1440,128]{1,0:T(8,128)(2,1)S(1)}, bf16[1440,128]{1,0:T(8,128)(2,1)S(1)}, u32[]{:S(2)}, u32[]{:S(2)}) collective-permute-start(bf16[1440,128]{1,0:T(8,128)(2,1)S(1)} %get-tuple-element.269), channel_id=1, source_target_pairs={{0,8},{8,0},{16,24},{24,16},{1,9},{9,1},{17,25},{25,17},{2,10},{10... | collective-permute-start | bytes 1105928 | tf_op jit(solution)/shard_map/ppermute | solution.py:804
  48.8 6.3 %copy-start.14 = (bf16[3,32,128]{2,1,0:T(8,128)(2,1)S(1)}, bf16[3,32,128]{2,1,0:T(8,128)(2,1)}, u32[]{:S(2)}) copy-start(bf16[3,32,128]{2,1,0:T(8,128)(2,1)} %get-tuple-element.271) | copy-start | bytes 73732
  48.8 6.3 %copy-start.15 = (bf16[3,32,128]{2,1,0:T(8,128)(2,1)S(1)}, bf16[3,32,128]{2,1,0:T(8,128)(2,1)}, u32[]{:S(2)}) copy-start(bf16[3,32,128]{2,1,0:T(8,128)(2,1)} %get-tuple-element.272) | copy-start | bytes 73732
  48.9 12.3 %collective-permute-start.38 = (bf16[336,128]{1,0:T(8,128)(2,1)S(1)}, bf16[336,128]{1,0:T(8,128)(2,1)S(1)}, u32[]{:S(2)}, u32[]{:S(2)}) collective-permute-start(bf16[336,128]{1,0:T(8,128)(2,1)S(1)} %get-tuple-element.295), channel_id=1, source_target_pairs={{0,17},{1,16},{2,19},{3,18},{4,21},{5,20},{6,23},{7,22},{8,25},{9,... | collective-permute-start | bytes 258056 | tf_op jit(solution)/shard_map/ppermute | solution.py:607
  52.5 8.7 %collective-permute-start.37 = (bf16[336,128]{1,0:T(8,128)(2,1)S(1)}, bf16[336,128]{1,0:T(8,128)(2,1)S(1)}, u32[]{:S(2)}, u32[]{:S(2)}) collective-permute-start(bf16[336,128]{1,0:T(8,128)(2,1)S(1)} %get-tuple-element.296), channel_id=1, source_target_pairs={{0,16},{1,17},{2,18},{3,19},{4,20},{5,21},{6,22},{7,23},{8,24},{9,... | collective-permute-start | bytes 258056 | tf_op jit(solution)/shard_map/ppermute | solution.py:607
  53.7 7.5 %collective-permute-start.36 = (bf16[336,128]{1,0:T(8,128)(2,1)S(1)}, bf16[336,128]{1,0:T(8,128)(2,1)}, u32[]{:S(2)}, u32[]{:S(2)}) collective-permute-start(bf16[336,128]{1,0:T(8,128)(2,1)S(1)} %get-tuple-element.294), channel_id=1, source_target_pairs={{0,1},{1,0},{2,3},{3,2},{4,5},{5,4},{6,7},{7,6},{8,9},{9,8},{10,11... | collective-permute-start | bytes 258056 | tf_op jit(solution)/shard_map/ppermute | solution.py:607
  55.1 6.1 %collective-permute-start.24 = (bf16[3,32,128]{2,1,0:T(8,128)(2,1)S(1)}, bf16[3,32,128]{2,1,0:T(8,128)(2,1)}, u32[]{:S(2)}, u32[]{:S(2)}) collective-permute-start(bf16[3,32,128]{2,1,0:T(8,128)(2,1)S(1)} %get-tuple-element.188), channel_id=1, source_target_pairs={{8,16},{9,17},{10,18},{11,19},{12,20},{13,21},{14,22},{15,23},{16,... | collective-permute-start | bytes 73736 | tf_op jit(solution)/shard_map/cond/branch_4_fun/ppermute | solution.py:773
  56.3 4.8 %collective-permute-start.25 = (bf16[3,32,128]{2,1,0:T(8,128)(2,1)S(1)}, bf16[3,32,128]{2,1,0:T(8,128)(2,1)}, u32[]{:S(2)}, u32[]{:S(2)}) collective-permute-start(bf16[3,32,128]{2,1,0:T(8,128)(2,1)S(1)} %get-tuple-element.189), channel_id=1, source_target_pairs={{24,27},{25,26},{26,25},{27,24},{28,31},{29,30},{30,29},{31,28}} | collective-permute-start | bytes 73736 | tf_op jit(solution)/shard_map/cond/branch_4_fun/ppermute | solution.py:773
  61.2 1.1 %copy-start.11 = (bf16[4096,128]{1,0:T(8,128)(2,1)}, bf16[4096,128]{1,0:T(8,128)(2,1)S(1)}, u32[]{:S(2)}) copy-start(bf16[4096,128]{1,0:T(8,128)(2,1)S(1)} %get-tuple-element.283.base) | copy-start | bytes 3145732
  62.3 16.5 %copy-start.12 = (bf16[4096,128]{1,0:T(8,128)(2,1)S(1)}, bf16[4096,128]{1,0:T(8,128)(2,1)}, u32[]{:S(2)}) copy-start(bf16[4096,128]{1,0:T(8,128)(2,1)} %copy-done.11) | copy-start | bytes 3145732
  63.3 9.2 %collective-permute-start.41 = (bf16[336,128]{1,0:T(8,128)(2,1)S(1)}, bf16[336,128]{1,0:T(8,128)(2,1)S(1)}, u32[]{:S(2)}, u32[]{:S(2)}) collective-permute-start(bf16[336,128]{1,0:T(8,128)(2,1)S(1)} %fusion.1), channel_id=1, source_target_pairs={{0,6},{1,7},{2,4},{3,5},{4,2},{5,3},{6,0},{7,1},{8,14},{9,15},{10,... | collective-permute-start | bytes 258056 | tf_op jit(solution)/shard_map/ppermute | solution.py:616
  67.0 7.2 %collective-permute-start.40 = (bf16[336,128]{1,0:T(8,128)(2,1)S(1)}, bf16[336,128]{1,0:T(8,128)(2,1)S(1)}, u32[]{:S(2)}, u32[]{:S(2)}) collective-permute-start(bf16[336,128]{1,0:T(8,128)(2,1)S(1)} %fusion.1), channel_id=1, source_target_pairs={{0,4},{1,5},{2,6},{3,7},{4,0},{5,1},{6,2},{7,3},{8,12},{9,13},{10,... | collective-permute-start | bytes 258056 | tf_op jit(solution)/shard_map/ppermute | solution.py:616
  67.0 8.1 %collective-permute-start.39 = (bf16[336,128]{1,0:T(8,128)(2,1)S(1)}, bf16[336,128]{1,0:T(8,128)(2,1)S(1)}, u32[]{:S(2)}, u32[]{:S(2)}) collective-permute-start(bf16[336,128]{1,0:T(8,128)(2,1)S(1)} %fusion.1), channel_id=1, source_target_pairs={{0,2},{1,3},{2,0},{3,1},{4,6},{5,7},{6,4},{7,5},{8,10},{9,11},{10,... | collective-permute-start | bytes 258056 | tf_op jit(solution)/shard_map/ppermute | solution.py:616
  67.8 11.0 %collective-permute-start.43 = (bf16[416,128]{1,0:T(8,128)(2,1)S(1)}, bf16[416,128]{1,0:T(8,128)(2,1)S(1)}, u32[]{:S(2)}, u32[]{:S(2)}) collective-permute-start(bf16[416,128]{1,0:T(8,128)(2,1)S(1)} %get-tuple-element.286), channel_id=1, source_target_pairs={{0,1},{1,2},{2,3},{3,4},{4,5},{5,6},{6,7},{7,0},{8,9},{9,10},{10,1... | collective-permute-start | bytes 319496 | tf_op jit(solution)/shard_map/ppermute | solution.py:815
  69.1 9.7 %collective-permute-start.44 = (bf16[416,128]{1,0:T(8,128)(2,1)S(1)}, bf16[416,128]{1,0:T(8,128)(2,1)S(1)}, u32[]{:S(2)}, u32[]{:S(2)}) collective-permute-start(bf16[416,128]{1,0:T(8,128)(2,1)S(1)} %get-tuple-element.287), channel_id=1, source_target_pairs={{0,7},{1,0},{2,1},{3,2},{4,3},{5,4},{6,5},{7,6},{8,15},{9,8},{10,9... | collective-permute-start | bytes 319496 | tf_op jit(solution)/shard_map/ppermute | solution.py:814
  75.1 7.4 %collective-permute-start.42 = (bf16[336,128]{1,0:T(8,128)(2,1)S(1)}, bf16[336,128]{1,0:T(8,128)(2,1)S(1)}, u32[]{:S(2)}, u32[]{:S(2)}) collective-permute-start(bf16[336,128]{1,0:T(8,128)(2,1)S(1)} %add_convert_fusion.1), channel_id=1, source_target_pairs={{0,1},{1,0},{2,3},{3,2},{4,5},{5,4},{6,7},{7,6},{8,9},{9,8},{10,11... | collective-permute-start | bytes 258056 | tf_op jit(solution)/shard_map/ppermute | solution.py:819
  77.1 5.7 %collective-permute-start.46 = (bf16[336,128]{1,0:T(8,128)(2,1)S(1)}, bf16[336,128]{1,0:T(8,128)(2,1)S(1)}, u32[]{:S(2)}, u32[]{:S(2)}) collective-permute-start(bf16[336,128]{1,0:T(8,128)(2,1)S(1)} %add_convert_fusion.1), channel_id=1, source_target_pairs={{0,17},{1,16},{2,19},{3,18},{4,21},{5,20},{6,23},{7,22},{8,25},{9,... | collective-permute-start | bytes 258056 | tf_op jit(solution)/shard_map/ppermute | solution.py:819
  78.8 5.3 %collective-permute-start.45 = (bf16[336,128]{1,0:T(8,128)(2,1)S(1)}, bf16[336,128]{1,0:T(8,128)(2,1)S(1)}, u32[]{:S(2)}, u32[]{:S(2)}) collective-permute-start(bf16[336,128]{1,0:T(8,128)(2,1)S(1)} %add_convert_fusion.1), channel_id=1, source_target_pairs={{0,16},{1,17},{2,18},{3,19},{4,20},{5,21},{6,22},{7,23},{8,24},{9,... | collective-permute-start | bytes 258056 | tf_op jit(solution)/shard_map/ppermute | solution.py:819
  84.1 1.7 %collective-permute-start.47 = (bf16[4,336,128]{2,1,0:T(8,128)(2,1)S(1)}, bf16[4,336,128]{2,1,0:T(8,128)(2,1)S(1)}, u32[]{:S(2)}, u32[]{:S(2)}) collective-permute-start(bf16[4,336,128]{2,1,0:T(8,128)(2,1)S(1)} %pad_maximum_fusion.mine), channel_id=1, source_target_pairs={{0,8},{8,0},{16,24},{24,16},{1,9},{9,1},{17,25},{25,17},{2,10},{10... | collective-permute-start | bytes 1032200 | tf_op jit(solution)/shard_map/ppermute | solution.py:822

commit v6 on v5

--- a/solution.py
+++ b/solution.py
@@ -308,7 +308,7 @@
                 tacc[a * 7 + b] += s[:8] + s[8:]
         return 0
 
-    lax.fori_loop(0, I * (CW // 8), tap, 0)
+    lax.fori_loop(0, I * (CW // 8), tap, 0, unroll=2)
     ts = [jnp.sum(tacc[t], axis=0, keepdims=True) for t in range(49)]
     ts = jnp.concatenate(ts + [jnp.zeros((15, 128), f32)], axis=0)
     sums[2560:2624, :] = ts.astype(bf16)

time: 88.8 us -> 88.8 us (level); the launches traced: 87.2 us -> 88.4 us
  starting transfers between devices: 32.8 us -> 34.7 us
    ppermute x3, starting transfers between devices: 3.65 us -> 6.35 us  [on_device(): back = [lax.ppermute(chunk, axes, square_pairs(k)) for k in (1, 2, 3)]]
  transfers between devices with their start and end apart: 20 -> 20, of which waited for: 8 -> 6; matrix products, arithmetic and copies ran while one was open for 0% -> 0% of each run, Pallas kernels for 10% -> 10%
where the time goes in v6:
time: 88.8 us; the launch traced here: 88.4 us
  Pallas kernels  41 us (46%)
  starting transfers between devices  34.7 us (39%)
  waiting for transfers between devices  8.96 us (10%)
  local copies, waits for them, and re-layouts  1.37 us (2%)
  other arithmetic  1.25 us (1%)
  between operations  0.95 us (1%)
    pallas_call x1, Pallas kernels, block_pass(): pl.pallas_call(functools.partial(block_body, R, CW), out_shape=out_shape,...  27.6 us
    ppermute x3, starting transfers between devices, on_device(): back = [lax.ppermute(chunk, axes, square_pairs(k)) for k in (1, 2, 3)]  6.35 us
    ppermute x3, starting transfers between devices, square_sum(): came.append(lax.ppermute(part, ('lat', 'lon'), square_pairs(k)))  5.61 us
    ppermute x3, starting transfers between devices, line_sum(): lax.ppermute(total, 'lon', flip_pairs('lon', bit * k))  4.44 us
    pallas_call x1, Pallas kernels, edges(): pl.pallas_call(functools.partial(edges_body, R, CW), out_shape=jax.ShapeD...  3.74 us
    pallas_call x1, Pallas kernels, conv_back(): pl.pallas_call(functools.partial(conv_back_body, R, CW), out_shape=jax.Sh...  3.55 us
    ppermute x1, starting transfers between devices, on_device(): gr = lax.ppermute(lpay, 'lon', shift_pairs('lon', -1))  3.33 us
    ppermute x1, starting transfers between devices, on_device(): right_f = lax.ppermute(lpay, 'lon', shift_pairs('lon', -1))  3.28 us
  transfers between devices with their start and end apart: 20, of which 6 were waited for; matrix products, arithmetic and copies ran while one was open for 0% of the time, Pallas kernels for 10%

profile of v6, /device:TPU:0, one launch (start us, length us, event | category | flops | bytes accessed | tf_op | source)
XLA Modules:
  0.0 88.4 jit_solution(17220902040241671105)
XLA Ops:
  0.6 1.4 %rim.1 = (bf16[3,32,128]{2,1,0:T(8,128)(2,1)}, bf16[3,32,128]{2,1,0:T(8,128)(2,1)S(1)}, bf16[3,32,128]{2,1,0:T(8,128)(2,1)S(1)}, s32[2]{0:T(128)}) custom-call(bf16[128,32,128]{2,1,0:T(8,128)(2,1)} %field.3, s32[256]{0:T(256)} %mirror.1), custom_call_target="tpu_custom_call" | custom-call | tf_op jit(solution)/shard_map/rim/pallas_call | solution.py:655
  2.0 0.5 collective-permute-start.32
  2.6 0.7 copy-done.5
  3.3 0.0 copy-start
  3.3 0.0 copy-start.4
  3.3 0.0 copy-start.10
  3.3 0.0 copy-start.13
  3.3 4.1 %conditional.2 = (bf16[3,32,128]{2,1,0:T(8,128)(2,1)}, bf16[3,32,128]{2,1,0:T(8,128)(2,1)}, bf16[3,128,128]{2,1,0:T(8,128)(2,1)S(1)}, bf16[3,128,128]{2,1,0:T(8,128)(2,1)S(1)}) conditional(s32[]{:T(128)} %bitcast, (bf16[3,32,128]{2,1,0:T(8,128)(2,1)S(1)}, bf16[3,32,128]{2,1,0:T(8,128)(2,1)S(1)}, ...), branch_computations={%region_0.0_spmd, %region_1.0_spmd, %region_2.0_spmd, %region_3.0_... | conditional | bytes 196720 | solution.py:777
  3.4 1.4 %collective-permute-start.4 = (bf16[3,32,128]{2,1,0:T(8,128)(2,1)S(1)}, bf16[3,32,128]{2,1,0:T(8,128)(2,1)}, u32[]{:S(2)}, u32[]{:S(2)}) collective-permute-start(bf16[3,32,128]{2,1,0:T(8,128)(2,1)S(1)} %get-tuple-element.138), channel_id=1, source_target_pairs={{8,16},{9,17},{10,18},{11,19},{12,20},{13,21},{14,22},{15,23},{16,... | collective-permute-start | bytes 73736 | tf_op jit(solution)/shard_map/cond/branch_2_fun/ppermute | solution.py:773
  4.8 1.3 %collective-permute-start.5 = (bf16[3,32,128]{2,1,0:T(8,128)(2,1)S(1)}, bf16[3,32,128]{2,1,0:T(8,128)(2,1)}, u32[]{:S(2)}, u32[]{:S(2)}) collective-permute-start(bf16[3,32,128]{2,1,0:T(8,128)(2,1)S(1)} %get-tuple-element.139), channel_id=1, source_target_pairs={{24,25},{25,24},{26,31},{27,30},{28,29},{29,28},{30,27},{31,26}} | collective-permute-start | bytes 73736 | tf_op jit(solution)/shard_map/cond/branch_2_fun/ppermute | solution.py:773
  6.0 1.3 %sides.10 = (bf16[3,128,128]{2,1,0:T(8,128)(2,1)S(1)}, bf16[3,128,128]{2,1,0:T(8,128)(2,1)S(1)}) custom-call(bf16[128,32,128]{2,1,0:T(8,128)(2,1)} %get-tuple-element.140.field), custom_call_target="tpu_custom_call" | custom-call | tf_op jit(solution)/shard_map/cond/branch_2_fun/sides/pallas_call | solution.py:690
  7.4 0.0 copy-start.1
  7.5 1.0 %join.2 = (bf16[3,32,128]{2,1,0:T(8,128)(2,1)S(1)}, bf16[3,32,128]{2,1,0:T(8,128)(2,1)S(1)}, bf16[3,134,128]{2,1,0:T(8,128)(2,1)S(1)}, bf16[3,134,128]{2,1,0:T(8,128)(2,1)S(1)}) custom-call(s32[2]{0:T(128)S(1)} %copy-done.5, bf16[3,32,128]{2,1,0:T(8,128)(2,1)S(1)} %collective-permute-done.32.near, bf16[3,32,128]{2,1,0:T(8,128)(2,1)} %get-tuple-element.258.far, ...), custom_call_target="tpu_custom_call" | custom-call | tf_op jit(solution)/shard_map/join/pallas_call | solution.py:750
  8.5 2.6 %collective-permute-start.33 = (bf16[3,134,128]{2,1,0:T(8,128)(2,1)S(1)}, bf16[3,134,128]{2,1,0:T(8,128)(2,1)S(1)}, u32[]{:S(2)}, u32[]{:S(2)}) collective-permute-start(bf16[3,134,128]{2,1,0:T(8,128)(2,1)S(1)} %get-tuple-element.264), channel_id=1, source_target_pairs={{0,1},{1,2},{2,3},{3,4},{4,5},{5,6},{6,7},{7,0},{8,9},{9,10},{10,1... | collective-permute-start | bytes 308744 | tf_op jit(solution)/shard_map/ppermute | solution.py:797
  11.1 3.3 %collective-permute-start.34 = (bf16[3,134,128]{2,1,0:T(8,128)(2,1)S(1)}, bf16[3,134,128]{2,1,0:T(8,128)(2,1)S(1)}, u32[]{:S(2)}, u32[]{:S(2)}) collective-permute-start(bf16[3,134,128]{2,1,0:T(8,128)(2,1)S(1)} %get-tuple-element.265), channel_id=1, source_target_pairs={{0,7},{1,0},{2,1},{3,2},{4,3},{5,4},{6,5},{7,6},{8,15},{9,8},{10,9... | collective-permute-start | bytes 308744 | tf_op jit(solution)/shard_map/ppermute | solution.py:796
  14.4 2.5 %collective-permute-done.33.left = bf16[3,134,128]{2,1,0:T(8,128)(2,1)S(1)} collective-permute-done((bf16[3,134,128]{2,1,0:T(8,128)(2,1)S(1)}, bf16[3,134,128]{2,1,0:T(8,128)(2,1)S(1)}, u32[]{:S(2)}, u32[]{:S(2)}) %collective-permute-start.33) | collective-permute-done | bytes 102944 | tf_op jit(solution)/shard_map/ppermute | solution.py:797
  16.9 0.1 collective-permute-done.34.right
  17.1 0.6 copy-done.6
  17.7 27.6 %block_pass.1 = (bf16[16,4,128]{2,1,0:T(4,128)(2,1)}, bf16[4096,128]{1,0:T(8,128)(2,1)S(1)}, bf16[4096,128]{1,0:T(8,128)(2,1)S(1)}, bf16[3,32,128]{2,1,0:T(8,128...) custom-call(bf16[128,32,128]{2,1,0:T(8,128)(2,1)} %field.3, ...), custom_call_target="tpu_custom_call" | custom-call | tf_op jit(solution)/shard_map/block_pass/pallas_call | solution.py:372
  45.3 2.0 %collective-permute-start.35 = (bf16[1440,128]{1,0:T(8,128)(2,1)S(1)}, bf16[1440,128]{1,0:T(8,128)(2,1)S(1)}, u32[]{:S(2)}, u32[]{:S(2)}) collective-permute-start(bf16[1440,128]{1,0:T(8,128)(2,1)S(1)} %get-tuple-element.269), channel_id=1, source_target_pairs={{0,8},{8,0},{16,24},{24,16},{1,9},{9,1},{17,25},{25,17},{2,10},{10... | collective-permute-start | bytes 1105928 | tf_op jit(solution)/shard_map/ppermute | solution.py:804
  47.2 1.3 %collective-permute-done.35.near = bf16[1440,128]{1,0:T(8,128)(2,1)S(1)} collective-permute-done((bf16[1440,128]{1,0:T(8,128)(2,1)S(1)}, bf16[1440,128]{1,0:T(8,128)(2,1)S(1)}, u32[]{:S(2)}, u32[]{:S(2)}) %collective-permute-start.35) | collective-permute-done | bytes 368672 | tf_op jit(solution)/shard_map/ppermute | solution.py:804
  48.5 0.1 add_convert_fusion
  48.6 0.0 copy-start.14
  48.6 0.0 copy-start.15
  48.7 5.0 %collective-permute-start.38 = (bf16[336,128]{1,0:T(8,128)(2,1)S(1)}, bf16[336,128]{1,0:T(8,128)(2,1)S(1)}, u32[]{:S(2)}, u32[]{:S(2)}) collective-permute-start(bf16[336,128]{1,0:T(8,128)(2,1)S(1)} %get-tuple-element.295), channel_id=1, source_target_pairs={{0,17},{1,16},{2,19},{3,18},{4,21},{5,20},{6,23},{7,22},{8,25},{9,... | collective-permute-start | bytes 258056 | tf_op jit(solution)/shard_map/ppermute | solution.py:607
  53.7 0.6 collective-permute-start.36
  54.3 6.1 %conditional.3 = (bf16[3,32,128]{2,1,0:T(8,128)(2,1)}, bf16[3,32,128]{2,1,0:T(8,128)(2,1)}, bf16[4096,128]{1,0:T(8,128)(2,1)S(1)}) conditional(s32[]{:T(128)} %bitcast, (bf16[3,32,128]{2,1,0:T(8,128)(2,1)S(1)}, bf16[3,32,128]{2,1,0:T(8,128)(2,1)S(1)}, bf16[4096,128]{1,0:T(8,128)(2,1)S(1)}, ...), branch_computations={%region_8.9_spmd, %region_9.10_spmd, %region_10.11_spmd, %region_1... | conditional | flops 100000000 | bytes 31653992 | solution.py:777
  54.3 1.2 %collective-permute-start.20 = (bf16[3,32,128]{2,1,0:T(8,128)(2,1)S(1)}, bf16[3,32,128]{2,1,0:T(8,128)(2,1)}, u32[]{:S(2)}, u32[]{:S(2)}) collective-permute-start(bf16[3,32,128]{2,1,0:T(8,128)(2,1)S(1)} %get-tuple-element.178), channel_id=1, source_target_pairs={{8,16},{9,17},{10,18},{11,19},{12,20},{13,21},{14,22},{15,23},{16,... | collective-permute-start | bytes 73736 | tf_op jit(solution)/shard_map/cond/branch_2_fun/ppermute | solution.py:773
  55.6 1.3 %collective-permute-start.21 = (bf16[3,32,128]{2,1,0:T(8,128)(2,1)S(1)}, bf16[3,32,128]{2,1,0:T(8,128)(2,1)}, u32[]{:S(2)}, u32[]{:S(2)}) collective-permute-start(bf16[3,32,128]{2,1,0:T(8,128)(2,1)S(1)} %get-tuple-element.179), channel_id=1, source_target_pairs={{24,25},{25,24},{26,31},{27,30},{28,29},{29,28},{30,27},{31,26}} | collective-permute-start | bytes 73736 | tf_op jit(solution)/shard_map/cond/branch_2_fun/ppermute | solution.py:773
  56.8 3.5 %conv_back.10 = bf16[4096,128]{1,0:T(8,128)(2,1)S(1)} custom-call(bf16[4096,128]{1,0:T(8,128)(2,1)S(1)} %get-tuple-element.180.g, bf16[4096,128]{1,0:T(8,128)(2,1)S(1)} %get-tuple-element.181.dirin, bf16[49,128]{1,0:T(8,128)(2,1)S(1)} %get-tuple-element.182.dw), custom_call_target="tpu_custom_call" | custom-call | flops 100000000 | bytes 31457280 | tf_op jit(solution)/shard_map/cond/branch_2_fun/conv_back/pallas_call | solution.py:418
  60.4 0.0 copy-start.11
  60.4 1.1 %fusion.1 = bf16[336,128]{1,0:T(8,128)(2,1)S(1)} fusion(bf16[336,128]{1,0:T(8,128)(2,1)S(1)} %collective-permute-done.38, bf16[336,128]{1,0:T(8,128)(2,1)S(1)} %collective-permute-done.37, bf16[336,128]{1,0:T(8,128)(2,1)} %collective-permute-done.36, bf16[4,336,128]{2,1,0:T(8,128)(2,1)S(1)} %bitcast.20, s32[]{:T(128)S(6)} %select_n.26), kind=kLoop, calls=%fused_computation.4 | loop fusion | flops 344064 | bytes 430084 | tf_op jit(solution)/shard_map/convert_element_type | solution.py:582
  61.5 0.0 copy-start.12
  61.5 1.0 %join.3 = (bf16[3,32,128]{2,1,0:T(8,128)(2,1)S(1)}, bf16[3,32,128]{2,1,0:T(8,128)(2,1)S(1)}, bf16[416,128]{1,0:T(8,128)(2,1)S(1)}, bf16[416,128]{1,0:T(8,128)(2,1)S(1)}) custom-call(s32[2]{0:T(128)S(1)} %copy-done.5, bf16[1440,128]{1,0:T(8,128)(2,1)S(1)} %collective-permute-done.35.near, bf16[3,32,128]{2,1,0:T(8,128)(2,1)} %get-tuple-element.277.far, ...), custom_call_target="tpu_custom_call" | custom-call | tf_op jit(solution)/shard_map/join/pallas_call | solution.py:750
  62.5 3.3 %collective-permute-start.41 = (bf16[336,128]{1,0:T(8,128)(2,1)S(1)}, bf16[336,128]{1,0:T(8,128)(2,1)S(1)}, u32[]{:S(2)}, u32[]{:S(2)}) collective-permute-start(bf16[336,128]{1,0:T(8,128)(2,1)S(1)} %fusion.1), channel_id=1, source_target_pairs={{0,6},{1,7},{2,4},{3,5},{4,2},{5,3},{6,0},{7,1},{8,14},{9,15},{10,... | collective-permute-start | bytes 258056 | tf_op jit(solution)/shard_map/ppermute | solution.py:616
  65.8 1.1 %collective-permute-start.39 = (bf16[336,128]{1,0:T(8,128)(2,1)S(1)}, bf16[336,128]{1,0:T(8,128)(2,1)S(1)}, u32[]{:S(2)}, u32[]{:S(2)}) collective-permute-start(bf16[336,128]{1,0:T(8,128)(2,1)S(1)} %fusion.1), channel_id=1, source_target_pairs={{0,2},{1,3},{2,0},{3,1},{4,6},{5,7},{6,4},{7,5},{8,10},{9,11},{10,... | collective-permute-start | bytes 258056 | tf_op jit(solution)/shard_map/ppermute | solution.py:616
  67.0 1.4 %collective-permute-start.43 = (bf16[416,128]{1,0:T(8,128)(2,1)S(1)}, bf16[416,128]{1,0:T(8,128)(2,1)S(1)}, u32[]{:S(2)}, u32[]{:S(2)}) collective-permute-start(bf16[416,128]{1,0:T(8,128)(2,1)S(1)} %get-tuple-element.286), channel_id=1, source_target_pairs={{0,1},{1,2},{2,3},{3,4},{4,5},{5,6},{6,7},{7,0},{8,9},{9,10},{10,1... | collective-permute-start | bytes 319496 | tf_op jit(solution)/shard_map/ppermute | solution.py:815
  68.4 3.3 %collective-permute-start.44 = (bf16[416,128]{1,0:T(8,128)(2,1)S(1)}, bf16[416,128]{1,0:T(8,128)(2,1)S(1)}, u32[]{:S(2)}, u32[]{:S(2)}) collective-permute-start(bf16[416,128]{1,0:T(8,128)(2,1)S(1)} %get-tuple-element.287), channel_id=1, source_target_pairs={{0,7},{1,0},{2,1},{3,2},{4,3},{5,4},{6,5},{7,6},{8,15},{9,8},{10,9... | collective-permute-start | bytes 319496 | tf_op jit(solution)/shard_map/ppermute | solution.py:814
  71.7 2.2 %collective-permute-done.40 = bf16[336,128]{1,0:T(8,128)(2,1)S(1)} collective-permute-done((bf16[336,128]{1,0:T(8,128)(2,1)S(1)}, bf16[336,128]{1,0:T(8,128)(2,1)S(1)}, u32[]{:S(2)}, u32[]{:S(2)}) %collective-permute-start.40) | collective-permute-done | bytes 86048 | tf_op jit(solution)/shard_map/ppermute | solution.py:616
  74.0 0.1 add_convert_fusion.1
  74.0 3.6 %collective-permute-start.42 = (bf16[336,128]{1,0:T(8,128)(2,1)S(1)}, bf16[336,128]{1,0:T(8,128)(2,1)S(1)}, u32[]{:S(2)}, u32[]{:S(2)}) collective-permute-start(bf16[336,128]{1,0:T(8,128)(2,1)S(1)} %add_convert_fusion.1), channel_id=1, source_target_pairs={{0,1},{1,0},{2,3},{3,2},{4,5},{5,4},{6,7},{7,6},{8,9},{9,8},{10,11... | collective-permute-start | bytes 258056 | tf_op jit(solution)/shard_map/ppermute | solution.py:819
  77.6 2.2 %collective-permute-start.46 = (bf16[336,128]{1,0:T(8,128)(2,1)S(1)}, bf16[336,128]{1,0:T(8,128)(2,1)S(1)}, u32[]{:S(2)}, u32[]{:S(2)}) collective-permute-start(bf16[336,128]{1,0:T(8,128)(2,1)S(1)} %add_convert_fusion.1), channel_id=1, source_target_pairs={{0,17},{1,16},{2,19},{3,18},{4,21},{5,20},{6,23},{7,22},{8,25},{9,... | collective-permute-start | bytes 258056 | tf_op jit(solution)/shard_map/ppermute | solution.py:819
  79.9 0.5 collective-permute-start.45
  80.4 3.7 %edges.1 = bf16[128,32,128]{2,1,0:T(8,128)(2,1)} custom-call(bf16[4096,128]{1,0:T(8,128)(2,1)S(1)} %copy-done.12, bf16[3,32,128]{2,1,0:T(8,128)(2,1)S(1)} %get-tuple-element.284.south, bf16[3,32,128]{2,1,0:T(8,128)(2,1)S(1)} %get-tuple-element.285.north, bf16[416,128]{1,0:T(8,128)(2,1)S(1)} %collective-permute-done.43.gl, ...), custom_call_target="tpu_custom_call" | custom-call | flops 100000000 | bytes 10485760 | tf_op jit(solution)/shard_map/edges/pallas_call | solution.py:524
  84.1 1.1 %collective-permute-done.45 = bf16[336,128]{1,0:T(8,128)(2,1)S(1)} collective-permute-done((bf16[336,128]{1,0:T(8,128)(2,1)S(1)}, bf16[336,128]{1,0:T(8,128)(2,1)S(1)}, u32[]{:S(2)}, u32[]{:S(2)}) %collective-permute-start.45) | collective-permute-done | bytes 86048 | tf_op jit(solution)/shard_map/ppermute | solution.py:819
  85.3 0.1 collective-permute-start.47
  85.4 1.6 %collective-permute-done.47.other = bf16[4,336,128]{2,1,0:T(8,128)(2,1)S(1)} collective-permute-done((bf16[4,336,128]{2,1,0:T(8,128)(2,1)S(1)}, bf16[4,336,128]{2,1,0:T(8,128)(2,1)S(1)}, u32[]{:S(2)}, u32[]{:S(2)}) %collective-permute-start.47) | collective-permute-done | bytes 344096 | tf_op jit(solution)/shard_map/ppermute | solution.py:822
  87.0 1.4 %finish_sums.1 = (f32[49,128]{1,0:T(8,128)}, f32[128,512]{1,0:T(8,128)}, f32[512,128]{1,0:T(8,128)}, f32[3,512,128]{2,1,0:T(8,128)}) custom-call(bf16[4,336,128]{2,1,0:T(8,128)(2,1)S(1)} %pad_maximum_fusion.mine, bf16[4,336,128]{2,1,0:T(8,128)(2,1)S(1)} %collective-permute-done.47.other), custom_call_target="tpu_custom_call" | custom-call | tf_op jit(solution)/shard_map/finish_sums/pallas_call | solution.py:567
  (39 shorter events, 0.2 us)
Async XLA Ops:
  2.0 5.4 %collective-permute-start.32 = (bf16[3,32,128]{2,1,0:T(8,128)(2,1)}, bf16[3,32,128]{2,1,0:T(8,128)(2,1)S(1)}, u32[]{:S(2)}, u32[]{:S(2)}) collective-permute-start(bf16[3,32,128]{2,1,0:T(8,128)(2,1)} %get-tuple-element.255), channel_id=1, source_target_pairs={{0,8},{8,0},{16,24},{24,16},{1,9},{9,1},{17,25},{25,17},{2,10},{10... | collective-permute-start | bytes 73736 | tf_op jit(solution)/shard_map/ppermute | solution.py:793
  2.6 0.7 copy-start.5
  3.3 13.7 %copy-start = (bf16[3,512,128]{2,1,0:T(8,128)(2,1)S(1)}, bf16[3,512,128]{2,1,0:T(8,128)(2,1)}, u32[]{:S(2)}) copy-start(bf16[3,512,128]{2,1,0:T(8,128)(2,1)} %sw.1) | copy-start | bytes 1179652
  3.3 13.7 %copy-start.4 = (bf16[16,4,128]{2,1,0:T(4,128)(2,1)S(1)}, bf16[16,4,128]{2,1,0:T(4,128)(2,1)}, u32[]{:S(2)}) copy-start(bf16[16,4,128]{2,1,0:T(4,128)(2,1)} %cot.1) | copy-start | bytes 49156
  3.3 13.7 %copy-start.7 = (bf16[3,128]{1,0:T(4,128)(2,1)S(1)}, bf16[3,128]{1,0:T(4,128)(2,1)}, u32[]{:S(2)}) copy-start(bf16[3,128]{1,0:T(4,128)(2,1)} %sgain.1) | copy-start | bytes 2308
  3.3 13.7 %copy-start.8 = (bf16[3,128]{1,0:T(4,128)(2,1)S(1)}, bf16[3,128]{1,0:T(4,128)(2,1)}, u32[]{:S(2)}) copy-start(bf16[3,128]{1,0:T(4,128)(2,1)} %sbias.1) | copy-start | bytes 2308
  3.3 13.7 %copy-start.10 = (bf16[128]{0:T(256)(128)(2,1)S(1)}, bf16[128]{0:T(256)(128)(2,1)}, u32[]{:S(2)}) copy-start(bf16[128]{0:T(256)(128)(2,1)} %scale.1) | copy-start | bytes 772
  3.3 13.7 %copy-start.13 = (bf16[49,128]{1,0:T(8,128)(2,1)S(1)}, bf16[49,128]{1,0:T(8,128)(2,1)}, u32[]{:S(2)}) copy-start(bf16[49,128]{1,0:T(8,128)(2,1)} %dw.3) | copy-start | bytes 37636
  3.4 4.0 %collective-permute-start.4 = (bf16[3,32,128]{2,1,0:T(8,128)(2,1)S(1)}, bf16[3,32,128]{2,1,0:T(8,128)(2,1)}, u32[]{:S(2)}, u32[]{:S(2)}) collective-permute-start(bf16[3,32,128]{2,1,0:T(8,128)(2,1)S(1)} %get-tuple-element.138), channel_id=1, source_target_pairs={{8,16},{9,17},{10,18},{11,19},{12,20},{13,21},{14,22},{15,23},{16,... | collective-permute-start | bytes 73736 | tf_op jit(solution)/shard_map/cond/branch_2_fun/ppermute | solution.py:773
  4.8 2.6 %collective-permute-start.5 = (bf16[3,32,128]{2,1,0:T(8,128)(2,1)S(1)}, bf16[3,32,128]{2,1,0:T(8,128)(2,1)}, u32[]{:S(2)}, u32[]{:S(2)}) collective-permute-start(bf16[3,32,128]{2,1,0:T(8,128)(2,1)S(1)} %get-tuple-element.139), channel_id=1, source_target_pairs={{24,25},{25,24},{26,31},{27,30},{28,29},{29,28},{30,27},{31,26}} | collective-permute-start | bytes 73736 | tf_op jit(solution)/shard_map/cond/branch_2_fun/ppermute | solution.py:773
  7.4 9.6 %copy-start.1 = (bf16[128,512]{1,0:T(8,128)(2,1)S(1)}, bf16[128,512]{1,0:T(8,128)(2,1)}, u32[]{:S(2)}) copy-start(bf16[128,512]{1,0:T(8,128)(2,1)} %upw.1) | copy-start | bytes 393220
  7.4 9.6 %copy-start.2 = (bf16[512,128]{1,0:T(8,128)(2,1)S(1)}, bf16[512,128]{1,0:T(8,128)(2,1)}, u32[]{:S(2)}) copy-start(bf16[512,128]{1,0:T(8,128)(2,1)} %down.1) | copy-start | bytes 393220
  7.5 9.6 %copy-start.3 = (s32[128,32]{0,1:T(8,128)S(1)}, s32[128,32]{0,1:T(8,128)}, u32[]{:S(2)}) copy-start(s32[128,32]{0,1:T(8,128)} %param.30) | copy-start | bytes 49156
  8.5 8.4 %collective-permute-start.33 = (bf16[3,134,128]{2,1,0:T(8,128)(2,1)S(1)}, bf16[3,134,128]{2,1,0:T(8,128)(2,1)S(1)}, u32[]{:S(2)}, u32[]{:S(2)}) collective-permute-start(bf16[3,134,128]{2,1,0:T(8,128)(2,1)S(1)} %get-tuple-element.264), channel_id=1, source_target_pairs={{0,1},{1,2},{2,3},{3,4},{4,5},{5,6},{6,7},{7,0},{8,9},{9,10},{10,1... | collective-permute-start | bytes 308744 | tf_op jit(solution)/shard_map/ppermute | solution.py:797
  11.1 5.9 %collective-permute-start.34 = (bf16[3,134,128]{2,1,0:T(8,128)(2,1)S(1)}, bf16[3,134,128]{2,1,0:T(8,128)(2,1)S(1)}, u32[]{:S(2)}, u32[]{:S(2)}) collective-permute-start(bf16[3,134,128]{2,1,0:T(8,128)(2,1)S(1)} %get-tuple-element.265), channel_id=1, source_target_pairs={{0,7},{1,0},{2,1},{3,2},{4,3},{5,4},{6,5},{7,6},{8,15},{9,8},{10,9... | collective-permute-start | bytes 308744 | tf_op jit(solution)/shard_map/ppermute | solution.py:796
  17.0 0.7 copy-start.6
  17.0 0.7 copy-start.9
  45.3 3.3 %collective-permute-start.35 = (bf16[1440,128]{1,0:T(8,128)(2,1)S(1)}, bf16[1440,128]{1,0:T(8,128)(2,1)S(1)}, u32[]{:S(2)}, u32[]{:S(2)}) collective-permute-start(bf16[1440,128]{1,0:T(8,128)(2,1)S(1)} %get-tuple-element.269), channel_id=1, source_target_pairs={{0,8},{8,0},{16,24},{24,16},{1,9},{9,1},{17,25},{25,17},{2,10},{10... | collective-permute-start | bytes 1105928 | tf_op jit(solution)/shard_map/ppermute | solution.py:804
  48.6 5.7 %copy-start.14 = (bf16[3,32,128]{2,1,0:T(8,128)(2,1)S(1)}, bf16[3,32,128]{2,1,0:T(8,128)(2,1)}, u32[]{:S(2)}) copy-start(bf16[3,32,128]{2,1,0:T(8,128)(2,1)} %get-tuple-element.271) | copy-start | bytes 73732
  48.6 5.7 %copy-start.15 = (bf16[3,32,128]{2,1,0:T(8,128)(2,1)S(1)}, bf16[3,32,128]{2,1,0:T(8,128)(2,1)}, u32[]{:S(2)}) copy-start(bf16[3,32,128]{2,1,0:T(8,128)(2,1)} %get-tuple-element.272) | copy-start | bytes 73732
  48.7 11.7 %collective-permute-start.38 = (bf16[336,128]{1,0:T(8,128)(2,1)S(1)}, bf16[336,128]{1,0:T(8,128)(2,1)S(1)}, u32[]{:S(2)}, u32[]{:S(2)}) collective-permute-start(bf16[336,128]{1,0:T(8,128)(2,1)S(1)} %get-tuple-element.295), channel_id=1, source_target_pairs={{0,17},{1,16},{2,19},{3,18},{4,21},{5,20},{6,23},{7,22},{8,25},{9,... | collective-permute-start | bytes 258056 | tf_op jit(solution)/shard_map/ppermute | solution.py:607
  53.7 6.8 %collective-permute-start.37 = (bf16[336,128]{1,0:T(8,128)(2,1)S(1)}, bf16[336,128]{1,0:T(8,128)(2,1)S(1)}, u32[]{:S(2)}, u32[]{:S(2)}) collective-permute-start(bf16[336,128]{1,0:T(8,128)(2,1)S(1)} %get-tuple-element.296), channel_id=1, source_target_pairs={{0,16},{1,17},{2,18},{3,19},{4,20},{5,21},{6,22},{7,23},{8,24},{9,... | collective-permute-start | bytes 258056 | tf_op jit(solution)/shard_map/ppermute | solution.py:607
  53.7 6.8 %collective-permute-start.36 = (bf16[336,128]{1,0:T(8,128)(2,1)S(1)}, bf16[336,128]{1,0:T(8,128)(2,1)}, u32[]{:S(2)}, u32[]{:S(2)}) collective-permute-start(bf16[336,128]{1,0:T(8,128)(2,1)S(1)} %get-tuple-element.294), channel_id=1, source_target_pairs={{0,1},{1,0},{2,3},{3,2},{4,5},{5,4},{6,7},{7,6},{8,9},{9,8},{10,11... | collective-permute-start | bytes 258056 | tf_op jit(solution)/shard_map/ppermute | solution.py:607
  54.3 6.1 %collective-permute-start.20 = (bf16[3,32,128]{2,1,0:T(8,128)(2,1)S(1)}, bf16[3,32,128]{2,1,0:T(8,128)(2,1)}, u32[]{:S(2)}, u32[]{:S(2)}) collective-permute-start(bf16[3,32,128]{2,1,0:T(8,128)(2,1)S(1)} %get-tuple-element.178), channel_id=1, source_target_pairs={{8,16},{9,17},{10,18},{11,19},{12,20},{13,21},{14,22},{15,23},{16,... | collective-permute-start | bytes 73736 | tf_op jit(solution)/shard_map/cond/branch_2_fun/ppermute | solution.py:773
  55.6 4.8 %collective-permute-start.21 = (bf16[3,32,128]{2,1,0:T(8,128)(2,1)S(1)}, bf16[3,32,128]{2,1,0:T(8,128)(2,1)}, u32[]{:S(2)}, u32[]{:S(2)}) collective-permute-start(bf16[3,32,128]{2,1,0:T(8,128)(2,1)S(1)} %get-tuple-element.179), channel_id=1, source_target_pairs={{24,25},{25,24},{26,31},{27,30},{28,29},{29,28},{30,27},{31,26}} | collective-permute-start | bytes 73736 | tf_op jit(solution)/shard_map/cond/branch_2_fun/ppermute | solution.py:773
  60.4 1.1 %copy-start.11 = (bf16[4096,128]{1,0:T(8,128)(2,1)}, bf16[4096,128]{1,0:T(8,128)(2,1)S(1)}, u32[]{:S(2)}) copy-start(bf16[4096,128]{1,0:T(8,128)(2,1)S(1)} %get-tuple-element.283.base) | copy-start | bytes 3145732
  61.5 18.9 %copy-start.12 = (bf16[4096,128]{1,0:T(8,128)(2,1)S(1)}, bf16[4096,128]{1,0:T(8,128)(2,1)}, u32[]{:S(2)}) copy-start(bf16[4096,128]{1,0:T(8,128)(2,1)} %copy-done.11) | copy-start | bytes 3145732
  62.5 9.2 %collective-permute-start.41 = (bf16[336,128]{1,0:T(8,128)(2,1)S(1)}, bf16[336,128]{1,0:T(8,128)(2,1)S(1)}, u32[]{:S(2)}, u32[]{:S(2)}) collective-permute-start(bf16[336,128]{1,0:T(8,128)(2,1)S(1)} %fusion.1), channel_id=1, source_target_pairs={{0,6},{1,7},{2,4},{3,5},{4,2},{5,3},{6,0},{7,1},{8,14},{9,15},{10,... | collective-permute-start | bytes 258056 | tf_op jit(solution)/shard_map/ppermute | solution.py:616
  65.8 8.1 %collective-permute-start.40 = (bf16[336,128]{1,0:T(8,128)(2,1)S(1)}, bf16[336,128]{1,0:T(8,128)(2,1)S(1)}, u32[]{:S(2)}, u32[]{:S(2)}) collective-permute-start(bf16[336,128]{1,0:T(8,128)(2,1)S(1)} %fusion.1), channel_id=1, source_target_pairs={{0,4},{1,5},{2,6},{3,7},{4,0},{5,1},{6,2},{7,3},{8,12},{9,13},{10,... | collective-permute-start | bytes 258056 | tf_op jit(solution)/shard_map/ppermute | solution.py:616
  65.8 8.1 %collective-permute-start.39 = (bf16[336,128]{1,0:T(8,128)(2,1)S(1)}, bf16[336,128]{1,0:T(8,128)(2,1)S(1)}, u32[]{:S(2)}, u32[]{:S(2)}) collective-permute-start(bf16[336,128]{1,0:T(8,128)(2,1)S(1)} %fusion.1), channel_id=1, source_target_pairs={{0,2},{1,3},{2,0},{3,1},{4,6},{5,7},{6,4},{7,5},{8,10},{9,11},{10,... | collective-permute-start | bytes 258056 | tf_op jit(solution)/shard_map/ppermute | solution.py:616
  67.0 13.4 %collective-permute-start.43 = (bf16[416,128]{1,0:T(8,128)(2,1)S(1)}, bf16[416,128]{1,0:T(8,128)(2,1)S(1)}, u32[]{:S(2)}, u32[]{:S(2)}) collective-permute-start(bf16[416,128]{1,0:T(8,128)(2,1)S(1)} %get-tuple-element.286), channel_id=1, source_target_pairs={{0,1},{1,2},{2,3},{3,4},{4,5},{5,6},{6,7},{7,0},{8,9},{9,10},{10,1... | collective-permute-start | bytes 319496 | tf_op jit(solution)/shard_map/ppermute | solution.py:815
  68.4 12.0 %collective-permute-start.44 = (bf16[416,128]{1,0:T(8,128)(2,1)S(1)}, bf16[416,128]{1,0:T(8,128)(2,1)S(1)}, u32[]{:S(2)}, u32[]{:S(2)}) collective-permute-start(bf16[416,128]{1,0:T(8,128)(2,1)S(1)} %get-tuple-element.287), channel_id=1, source_target_pairs={{0,7},{1,0},{2,1},{3,2},{4,3},{5,4},{6,5},{7,6},{8,15},{9,8},{10,9... | collective-permute-start | bytes 319496 | tf_op jit(solution)/shard_map/ppermute | solution.py:814
  74.0 10.1 %collective-permute-start.42 = (bf16[336,128]{1,0:T(8,128)(2,1)S(1)}, bf16[336,128]{1,0:T(8,128)(2,1)S(1)}, u32[]{:S(2)}, u32[]{:S(2)}) collective-permute-start(bf16[336,128]{1,0:T(8,128)(2,1)S(1)} %add_convert_fusion.1), channel_id=1, source_target_pairs={{0,1},{1,0},{2,3},{3,2},{4,5},{5,4},{6,7},{7,6},{8,9},{9,8},{10,11... | collective-permute-start | bytes 258056 | tf_op jit(solution)/shard_map/ppermute | solution.py:819
  77.6 6.5 %collective-permute-start.46 = (bf16[336,128]{1,0:T(8,128)(2,1)S(1)}, bf16[336,128]{1,0:T(8,128)(2,1)S(1)}, u32[]{:S(2)}, u32[]{:S(2)}) collective-permute-start(bf16[336,128]{1,0:T(8,128)(2,1)S(1)} %add_convert_fusion.1), channel_id=1, source_target_pairs={{0,17},{1,16},{2,19},{3,18},{4,21},{5,20},{6,23},{7,22},{8,25},{9,... | collective-permute-start | bytes 258056 | tf_op jit(solution)/shard_map/ppermute | solution.py:819
  79.9 5.4 %collective-permute-start.45 = (bf16[336,128]{1,0:T(8,128)(2,1)S(1)}, bf16[336,128]{1,0:T(8,128)(2,1)S(1)}, u32[]{:S(2)}, u32[]{:S(2)}) collective-permute-start(bf16[336,128]{1,0:T(8,128)(2,1)S(1)} %add_convert_fusion.1), channel_id=1, source_target_pairs={{0,16},{1,17},{2,18},{3,19},{4,20},{5,21},{6,22},{7,23},{8,24},{9,... | collective-permute-start | bytes 258056 | tf_op jit(solution)/shard_map/ppermute | solution.py:819
  85.3 1.7 %collective-permute-start.47 = (bf16[4,336,128]{2,1,0:T(8,128)(2,1)S(1)}, bf16[4,336,128]{2,1,0:T(8,128)(2,1)S(1)}, u32[]{:S(2)}, u32[]{:S(2)}) collective-permute-start(bf16[4,336,128]{2,1,0:T(8,128)(2,1)S(1)} %pad_maximum_fusion.mine), channel_id=1, source_target_pairs={{0,8},{8,0},{16,24},{24,16},{1,9},{9,1},{17,25},{25,17},{2,10},{10... | collective-permute-start | bytes 1032200 | tf_op jit(solution)/shard_map/ppermute | solution.py:822
